TPU v7x, 256 devices: a whole 4x4x8 slice. The times are simulated.
256 devices in a mesh: group: 4 (over x), patch: 64 (over y, z, core).
Axes of the slice: x: 4, y: 4, z: 8, core: 2. Of those that a mesh axis runs over, the one named last changes fastest.
Arguments:
- node_tape: bfloat16 [4, 65536, 512], P('group', 'patch'), may hold values from -6 to 6
- edge_tape: bfloat16 [4, 65536, 512], P('group', 'patch'), may hold values from -16 to 16
- node_cot: bfloat16 [4, 65536, 512], P('group', 'patch'), may hold values from -6 to 6
- edge_cot: bfloat16 [4, 65536, 512], P('group', 'patch'), may hold values from -6 to 6
- w_edge_in: bfloat16 [1536, 512], replicated, may hold values from -0.15625 to 0.15625
- w_edge_out: bfloat16 [512, 512], replicated, may hold values from -0.25 to 0.25
- gain_edge: float32 [512], replicated, may hold values from 0.1 to 1.9
- w_node_in: bfloat16 [1024, 512], replicated, may hold values from -0.1875 to 0.1875
- w_node_out: bfloat16 [512, 512], replicated, may hold values from -0.25 to 0.25
- gain_node: float32 [512], replicated, may hold values from 0.1 to 1.9
- senders: int32 [512, 128], P('patch'), may hold values from 0 to 1279
- receivers: int32 [512, 128], P('patch'), may hold values from 0 to 1023
- tile_count: int32 [64], P('patch'), may hold values from 1 to 8, as said below
- send_rows: int32 [64, 256], P('patch'), may hold values from 0 to 1023
Outputs:
- edge_grad: bfloat16 [4, 65536, 512], P('group', 'patch')
- node_grad: bfloat16 [4, 65536, 512], P('group', 'patch')
- grad_edge_in: float32 [1536, 512], P('patch')
- grad_edge_out: float32 [512, 512], P('patch')
- grad_gain_edge: float32 [512], P('patch')
- grad_node_in: float32 [1024, 512], P('patch')
- grad_node_out: float32 [512, 512], P('patch')
- grad_gain_node: float32 [512], P('patch')
Inputs may be any that keep to these rules, and one draw needn't show every extreme that they name: Tiles 0 to tile_count - 1 of a patch's 8 slots hold edges, the rest are padding; some patch has all 8 live. `senders`: A value s below 1024 is a node of the edge's own patch; 1024 + k is the k-th halo row that patch receives, rows p * 4 to (p + 1) * 4 - 1 coming from patch p. `receivers`: A node of the edge's own patch. `send_rows`: entry p * 4 + j of patch q's list is the own node whose latent is the j-th halo row patch p receives from q; every patch sends exactly 4 rows to every patch.
All inputs are finite; a program needn't handle non-finite values.
Results may differ from a plain program's by a relative error of at most 0.014.
Values may be sent and summed in bfloat16 or wider, within the bound.
No kernel may reach another device: no remote copies, remote signals or barrier semaphores. Data moves between devices by JAX's collectives and lax.ppermute only.
A program may use at most 128 MiB of HBM per device.

v0:
```python
import functools

import jax
import jax.numpy as jnp
from jax import lax
from jax.experimental import pallas as pl
from jax.experimental.pallas import tpu as pltpu
from jax.sharding import PartitionSpec as P

epsilon = 1e-05
BF = jnp.bfloat16
F32 = jnp.float32
LANE = 128
ROWS = 256


def dot(a, b):
    return lax.dot_general(a, b, (((1,), (0,)), ((), ())), preferred_element_type=F32)


def dot_rt(a, b):
    return lax.dot_general(a, b, (((1,), (1,)), ((), ())), preferred_element_type=F32)


def dot_lt(a, b):
    return lax.dot_general(a, b, (((0,), (0,)), ((), ())), preferred_element_type=F32)


def iota(shape, dim):
    return lax.broadcasted_iota(jnp.int32, shape, dim)


def one_hot(mask):
    return jnp.where(mask, 1.0, 0.0).astype(BF)


def columns_of(index_ref, out_ref):
    tiles = index_ref.shape[0]
    full = jnp.concatenate(
        [index_ref[...], jnp.zeros((LANE - tiles, LANE), jnp.int32)], axis=0
    )
    turned = full.T
    for t in range(tiles):
        out_ref[t * LANE : (t + 1) * LANE, :] = jnp.broadcast_to(
            turned[:, t : t + 1], (LANE, LANE)
        )


def pick_rows(cols_ref, start, count, first, width):
    column = cols_ref[pl.ds(start, count), 0:1]
    return one_hot(column == iota((count, width), 1) + first)


def spread_rows(index_ref, start, count):
    tiles = index_ref.shape[0]
    base = iota((count, LANE), 0) + start
    return jnp.concatenate([one_hot(index_ref[t : t + 1, :] == base) for t in range(tiles)], axis=1)


def sigmoid(v):
    return 1.0 / (1.0 + jnp.exp(-v))


def live_rows(count_ref, start, count):
    return (iota((count, 1), 0) + start < count_ref[0] * LANE).astype(F32)


def normalize(values):
    centred = values - jnp.mean(values, axis=1, keepdims=True)
    inverse = lax.rsqrt(jnp.mean(centred * centred, axis=1, keepdims=True) + epsilon)
    return centred * inverse, inverse


def normalize_back(upstream, normed, inverse):
    return inverse * (
        upstream
        - jnp.mean(upstream, axis=1, keepdims=True)
        - normed * jnp.mean(upstream * normed, axis=1, keepdims=True)
    )


def loop(count, body):
    def step(i, carry):
        body(pl.multiple_of(i * ROWS, ROWS))
        return carry

    lax.fori_loop(0, count // ROWS, step, 0)


def outgoing_kernel(rows_ref, node_ref, out_ref):
    nodes, halo = node_ref.shape[0], rows_ref.shape[1]
    spread = one_hot(rows_ref[...] == iota((nodes, halo), 0))
    out_ref[...] = dot_lt(spread, node_ref[...]).astype(BF)


def own_kernel(node_ref, edge_ref, recv_ref, w_ref, out_ref, cols):
    nodes, width = node_ref.shape
    columns_of(recv_ref, cols)

    def body(start):
        here = pl.ds(start, ROWS)
        from_recv = dot(pick_rows(cols, start, ROWS, 0, nodes), node_ref[...]).astype(BF)
        out_ref[here, :] = dot(edge_ref[here, :], w_ref[0:width, :]) + dot(
            from_recv, w_ref[2 * width : 3 * width, :]
        )

    loop(edge_ref.shape[0], body)


def deal(place_ref, patches, pieces, send_ref, keep_ref):
    core, member = place_ref[0], place_ref[1]
    each = sum(rows for _, rows in pieces)
    batch = 1 if each % 16 == 0 else 2

    def step(i, carry):
        for which, out in ((core, keep_ref), (1 - core, send_ref)):
            for s in range(4):
                lanes = pl.ds(pl.multiple_of(((member + s) % 4) * LANE, LANE), LANE)
                found = []
                for b in range(batch):
                    patch = (i * batch + b) * 2 + which
                    for ref, rows in pieces:
                        found.append(ref[pl.ds(pl.multiple_of(patch * rows, 8), rows), lanes])
                where = pl.ds(pl.multiple_of(i * (batch * each), 16), batch * each)
                out[s, where, :] = jnp.concatenate(found, axis=0).astype(BF)
        return carry

    lax.fori_loop(0, patches // 2 // batch, step, 0)


def forward_kernel(
    patches,
    place_ref,
    count_ref,
    halo_ref,
    begun_ref,
    node_ref,
    cot_ref,
    send_ref,
    recv_ref,
    w_edge_ref,
    w_edge_out_ref,
    gain_edge_ref,
    w_node_ref,
    w_node_out_ref,
    gain_node_ref,
    hidden_ref,
    slope_ref,
    normed_ref,
    inverse_ref,
    node_acc_ref,
    back_ref,
    gain_ref,
    piece_send_ref,
    piece_keep_ref,
    cols,
    message,
    gathered,
    node_hidden,
    grad_second,
    grad_first,
    sum_in,
    sum_out,
):
    nodes, width = node_ref.shape
    halo = halo_ref.shape[0]
    columns_of(send_ref, cols)

    def edge_body(start):
        here = pl.ds(start, ROWS)
        latent = dot(pick_rows(cols, start, ROWS, 0, nodes), node_ref[...]) + dot(
            pick_rows(cols, start, ROWS, nodes, halo), halo_ref[...]
        )
        first = begun_ref[here, :] + dot(latent.astype(BF), w_edge_ref[width : 2 * width, :])
        squash = sigmoid(first)
        hidden = (first * squash).astype(BF)
        hidden_ref[here, :] = hidden
        slope_ref[here, :] = (squash * (1.0 + first * (1.0 - squash))).astype(BF)
        normed, inverse = normalize(dot(hidden, w_edge_out_ref[...]))
        normed_ref[here, :] = normed.astype(BF)
        inverse_ref[here, :] = jnp.broadcast_to(inverse, (ROWS, LANE))
        live = live_rows(count_ref, start, ROWS)
        message[here, :] = (live * (gain_edge_ref[...] * normed)).astype(BF)

    loop(begun_ref.shape[0], edge_body)
    gain_ref[...] = jnp.zeros_like(gain_ref)

    def node_body(start):
        here = pl.ds(start, ROWS)
        taken = dot(spread_rows(recv_ref, start, ROWS), message[...]).astype(BF)
        gathered[here, :] = taken
        first = dot(node_ref[here, :], w_node_ref[0:width, :]) + dot(
            taken, w_node_ref[width : 2 * width, :]
        )
        squash = sigmoid(first)
        hidden = (first * squash).astype(BF)
        node_hidden[here, :] = hidden
        slope = squash * (1.0 + first * (1.0 - squash))
        normed, inverse = normalize(dot(hidden, w_node_out_ref[...]))
        upstream = cot_ref[here, :].astype(F32)
        gain_ref[...] += jnp.sum(upstream * normed, axis=0, keepdims=True)
        second = normalize_back(upstream * gain_node_ref[...], normed, inverse).astype(BF)
        grad_second[here, :] = second
        grad = (dot_rt(second, w_node_out_ref[...]) * slope).astype(BF)
        grad_first[here, :] = grad
        node_acc_ref[here, :] = upstream + dot_rt(grad, w_node_ref[0:width, :])
        back_ref[here, :] = dot_rt(grad, w_node_ref[width : 2 * width, :]).astype(BF)

    loop(nodes, node_body)
    sum_out[...] = dot_lt(node_hidden[...], grad_second[...])
    sum_in[0:width, :] = dot_lt(node_ref[...], grad_first[...])
    sum_in[width : 2 * width, :] = dot_lt(gathered[...], grad_first[...])
    pieces = ((sum_in, 2 * width // patches), (sum_out, width // patches))
    deal(place_ref, patches, pieces, piece_send_ref, piece_keep_ref)


def backward_kernel(
    patches,
    count_ref,
    cot_ref,
    back_ref,
    send_ref,
    recv_ref,
    slope_ref,
    normed_ref,
    inverse_ref,
    node_acc_ref,
    gain_node_ref,
    w_edge_ref,
    w_edge_out_ref,
    gain_edge_ref,
    edge_grad_ref,
    node_out_ref,
    return_ref,
    second_ref,
    first_ref,
    from_send_ref,
    from_recv_ref,
    cols,
    gain,
):
    edges, width = cot_ref.shape
    nodes = back_ref.shape[0]
    halo = return_ref.shape[0]
    columns_of(recv_ref, cols)
    gain[...] = jnp.zeros_like(gain)

    def edge_body(start):
        here = pl.ds(start, ROWS)
        live = live_rows(count_ref, start, ROWS)
        upstream = live * cot_ref[here, :].astype(F32)
        taken = dot(pick_rows(cols, start, ROWS, 0, nodes), back_ref[...])
        message = upstream + live * taken
        normed = normed_ref[here, :].astype(F32)
        gain[...] += jnp.sum(message * normed, axis=0, keepdims=True)
        second = normalize_back(
            message * gain_edge_ref[...], normed, inverse_ref[here, 0:1]
        ).astype(BF)
        second_ref[here, :] = second
        grad = (dot_rt(second, w_edge_out_ref[...]) * slope_ref[here, :].astype(F32)).astype(BF)
        first_ref[here, :] = grad
        edge_grad_ref[here, :] = (upstream + dot_rt(grad, w_edge_ref[0:width, :])).astype(BF)

    loop(edges, edge_body)

    def halo_part(start):
        spread = spread_rows(send_ref, nodes + start, ROWS)
        total = dot(spread, first_ref[...]).astype(BF)
        from_send_ref[pl.ds(nodes + start, ROWS), :] = total
        return_ref[pl.ds(start, ROWS), 0:width] = dot_rt(
            total, w_edge_ref[width : 2 * width, :]
        ).astype(BF)

    loop(halo, halo_part)
    each, rows = width // patches, halo // patches
    row, lane = iota((halo, width), 0), iota((halo, width), 1)
    chosen = (row % rows == 0) & (lane // each == row // rows)
    deep, slot = iota((width, LANE), 0), iota((width, LANE), 1)
    for g, shift in ((gain, 0), (gain_node_ref, each)):
        part = dot(
            jnp.where(chosen, g[...], 0.0).astype(BF), one_hot(deep % each + shift == slot)
        )
        if shift == 0:
            both = part
        else:
            both = both + part
    return_ref[:, width : width + LANE] = both.astype(BF)

    def node_body(start):
        here = pl.ds(start, ROWS)
        sent = dot(spread_rows(send_ref, start, ROWS), first_ref[...]).astype(BF)
        received = dot(spread_rows(recv_ref, start, ROWS), first_ref[...]).astype(BF)
        from_send_ref[here, :] = sent
        from_recv_ref[here, :] = received
        node_out_ref[here, :] = (
            node_acc_ref[here, :]
            + dot_rt(sent, w_edge_ref[width : 2 * width, :])
            + dot_rt(received, w_edge_ref[2 * width : 3 * width, :])
        )

    loop(nodes, node_body)


def edge_weight_kernel(
    patches,
    place_ref,
    hidden_ref,
    second_ref,
    edge_ref,
    node_ref,
    halo_ref,
    first_ref,
    from_send_ref,
    from_recv_ref,
    piece_send_ref,
    piece_keep_ref,
    sum_in,
    sum_out,
):
    nodes, width = node_ref.shape
    halo = halo_ref.shape[0]
    sum_out[...] = dot_lt(hidden_ref[...], second_ref[...])
    sum_in[0:width, :] = dot_lt(edge_ref[...], first_ref[...])
    sum_in[width : 2 * width, :] = dot_lt(node_ref[...], from_send_ref[0:nodes, :]) + dot_lt(
        halo_ref[...], from_send_ref[nodes : nodes + halo, :]
    )
    sum_in[2 * width : 3 * width, :] = dot_lt(node_ref[...], from_recv_ref[...])
    pieces = ((sum_in, 3 * width // patches), (sum_out, width // patches))
    deal(place_ref, patches, pieces, piece_send_ref, piece_keep_ref)


def node_grad_kernel(rows_ref, returned_ref, acc_ref, out_ref, gain_ref):
    nodes, width = acc_ref.shape
    halo = returned_ref.shape[0]

    def body(start):
        here = pl.ds(start, ROWS)
        spread = one_hot(rows_ref[...] == iota((ROWS, halo), 0) + start)
        out_ref[here, :] = (acc_ref[here, :] + dot(spread, returned_ref[:, 0:width])).astype(BF)

    loop(nodes, body)
    total = jnp.sum(returned_ref[:, width : width + LANE].astype(F32), axis=0, keepdims=True)
    gain_ref[...] = jnp.broadcast_to(total, gain_ref.shape)


def pair_kernel(keep_ref, got_ref, *outs):
    for s in range(4):
        outs[s][...] = (keep_ref[s].astype(F32) + got_ref[s].astype(F32)).astype(BF)


def four_kernel(patches, *refs):
    out_ref = refs[-1]
    at = 0
    for part in range(2):
        a, b, c, d = refs[part * 4 : part * 4 + 4]
        total = a[...].astype(F32) + b[...].astype(F32) + c[...].astype(F32) + d[...].astype(F32)
        rows = total.shape[0] // patches
        out_ref[:, at : at + rows, :] = total.reshape(patches, rows, LANE).astype(BF)
        at += rows


def last_sum_kernel(got_ref, gain_ref, out_ref):
    rows = got_ref.shape[1]
    total = got_ref[0].astype(F32)
    for i in range(1, got_ref.shape[0]):
        total = total + got_ref[i].astype(F32)
    out_ref[...] = jnp.concatenate([total, gain_ref[...]], axis=0).astype(BF)


def finish_kernel(
    factor, place_ref, a, b, c, d, edge_in_ref, edge_out_ref, node_in_ref, node_out_ref, gain_ref
):
    member = place_ref[1]
    gain = jnp.zeros((8, LANE), F32)
    for s, ref in enumerate((a, b, c, d)):
        lanes = pl.ds(pl.multiple_of(((member - s + 4) % 4) * LANE, LANE), LANE)
        at = 0
        values = ref[...].astype(F32)
        for out in (node_in_ref, node_out_ref, edge_in_ref, edge_out_ref):
            rows = out.shape[0]
            out[:, lanes] = values[at : at + rows, :] * factor
            at += rows
        gain = gain + values[at : at + 8, :]
    gain_ref[...] = gain * factor


VM = pl.BlockSpec(memory_space=pltpu.VMEM)
SM = pl.BlockSpec(memory_space=pltpu.SMEM)


def call(kernel, outs, ins, scratch=(), scalars=0, flops=0, limit=40):
    shapes = [jax.ShapeDtypeStruct(s, d) for s, d in outs]
    single = len(shapes) == 1
    size = sum(int(a.size) * a.dtype.itemsize for a in list(ins) + shapes)
    return pl.pallas_call(
        kernel,
        out_shape=shapes[0] if single else shapes,
        in_specs=[SM] * scalars + [VM] * (len(ins) - scalars),
        out_specs=VM if single else [VM] * len(shapes),
        scratch_shapes=[pltpu.VMEM(s, d) for s, d in scratch],
        compiler_params=pltpu.CompilerParams(vmem_limit_bytes=limit * 2**20),
        cost_estimate=pl.CostEstimate(flops=flops, bytes_accessed=size, transcendentals=0),
    )(*ins)


def local(
    node_tape,
    edge_tape,
    node_cot,
    edge_cot,
    w_edge_in,
    w_edge_out,
    gain_edge,
    w_node_in,
    w_node_out,
    gain_node,
    senders,
    receivers,
    tile_count,
    send_rows,
):
    node, edge = node_tape[0], edge_tape[0]
    n_cot, e_cot = node_cot[0], edge_cot[0]
    nodes, width = node.shape
    edges = edge.shape[0]
    halo = send_rows.shape[1]
    patches = lax.axis_size("patch")
    members = lax.axis_size("group")
    half = patches // 2
    place = jnp.stack([lax.axis_index("patch") % 2, lax.axis_index("group")]).astype(jnp.int32)
    gain_edge = gain_edge.reshape(1, width)
    gain_node = gain_node.reshape(1, width)
    twins = [(i, i ^ 1) for i in range(patches)]
    same_core = [[2 * i + c for i in range(half)] for c in range(2)]
    unit = 2 * width * width

    def to_member(x, shift):
        return lax.ppermute(x, "group", [(g, (g + shift) % members) for g in range(members)])

    def node_rows_of(count):
        return count * unit

    outgoing = call(
        outgoing_kernel, [((halo, width), BF)], [send_rows, node], flops=2 * halo * nodes * width
    )
    incoming = lax.all_to_all(outgoing, "patch", split_axis=0, concat_axis=0, tiled=True)
    begun = call(
        own_kernel,
        [((edges, width), F32)],
        [node, edge, receivers, w_edge_in],
        [((edges, LANE), jnp.int32)],
        flops=4 * edges * unit,
    )
    per_node, per_edge = 3 * width // patches, 4 * width // patches
    (
        hidden,
        slope,
        normed,
        inverse,
        node_acc,
        back,
        sum_gain_node,
        node_send,
        node_keep,
    ) = call(
        functools.partial(forward_kernel, patches),
        [
            ((edges, width), BF),
            ((edges, width), BF),
            ((edges, width), BF),
            ((edges, LANE), F32),
            ((nodes, width), F32),
            ((nodes, width), BF),
            ((1, width), F32),
            ((4, half * per_node, LANE), BF),
            ((4, half * per_node, LANE), BF),
        ],
        [
            place,
            tile_count,
            incoming,
            begun,
            node,
            n_cot,
            senders,
            receivers,
            w_edge_in,
            w_edge_out,
            gain_edge,
            w_node_in,
            w_node_out,
            gain_node,
        ],
        [
            ((edges, LANE), jnp.int32),
            ((edges, width), BF),
            ((nodes, width), BF),
            ((nodes, width), BF),
            ((nodes, width), BF),
            ((nodes, width), BF),
            ((2 * width, width), F32),
            ((width, width), F32),
        ],
        scalars=2,
        flops=16 * nodes * unit,
    )
    node_got = lax.ppermute(node_send, "patch", twins)
    (edge_grad, node_part, outward, grad_second, grad_first, from_send, from_recv) = call(
        functools.partial(backward_kernel, patches),
        [
            ((edges, width), BF),
            ((nodes, width), F32),
            ((halo, width + LANE), BF),
            ((edges, width), BF),
            ((edges, width), BF),
            ((nodes + halo, width), BF),
            ((nodes, width), BF),
        ],
        [
            tile_count,
            e_cot,
            back,
            senders,
            receivers,
            slope,
            normed,
            inverse,
            node_acc,
            sum_gain_node,
            w_edge_in,
            w_edge_out,
            gain_edge,
        ],
        [((edges, LANE), jnp.int32), ((1, width), F32)],
        scalars=1,
        flops=12 * nodes * unit,
    )

    def after_pair(keep, got):
        shape = keep.shape[1:]
        parts = call(pair_kernel, [(shape, BF)] * 4, [keep, got])
        return [parts[0]] + [to_member(parts[s], s) for s in range(1, 4)]

    node_parts = after_pair(node_keep, node_got)
    edge_send, edge_keep = call(
        functools.partial(edge_weight_kernel, patches),
        [((4, half * per_edge, LANE), BF)] * 2,
        [place, hidden, grad_second, edge, node, incoming, grad_first, from_send, from_recv],
        [((3 * width, width), F32), ((width, width), F32)],
        scalars=1,
        flops=4 * nodes * unit,
    )
    edge_got = lax.ppermute(edge_send, "patch", twins)
    returned = lax.all_to_all(outward, "patch", split_axis=0, concat_axis=0, tiled=True)
    edge_parts = after_pair(edge_keep, edge_got)
    node_grad, gains = call(
        node_grad_kernel,
        [((nodes, width), BF), ((8, LANE), F32)],
        [send_rows, returned, node_part],
        flops=2 * nodes * halo * width,
    )
    rows = per_node + per_edge
    blocks = call(
        functools.partial(four_kernel, half),
        [((half, rows, LANE), BF)],
        node_parts + edge_parts,
    )
    got = lax.all_to_all(
        blocks, "patch", split_axis=0, concat_axis=0, axis_index_groups=same_core, tiled=True
    )
    mine = call(last_sum_kernel, [((rows + 8, LANE), BF)], [got, gains])
    shared = [mine] + [to_member(mine, s) for s in range(1, 4)]
    factor = float(members * patches * edges) ** (-0.5)
    each = width // patches
    out_edge_in, out_edge_out, out_node_in, out_node_out, out_gain = call(
        functools.partial(finish_kernel, factor),
        [
            ((3 * each, width), F32),
            ((each, width), F32),
            ((2 * each, width), F32),
            ((each, width), F32),
            ((8, LANE), F32),
        ],
        [place] + shared,
        scalars=1,
    )
    return (
        edge_grad[None],
        node_grad[None],
        out_edge_in,
        out_edge_out,
        out_gain[0, 0:each],
        out_node_in,
        out_node_out,
        out_gain[0, each : 2 * each],
    )


def solution(mesh):
    placed = (
        P("group", "patch", None),
        P("group", "patch", None),
        P("group", "patch", None),
        P("group", "patch", None),
        P(),
        P(),
        P(),
        P(),
        P(),
        P(),
        P("patch", None),
        P("patch", None),
        P("patch"),
        P("patch", None),
    )
    return jax.shard_map(
        local,
        mesh=mesh,
        in_specs=placed,
        out_specs=(
            P("group", "patch", None),
            P("group", "patch", None),
            P("patch", None),
            P("patch", None),
            P("patch"),
            P("patch", None),
            P("patch", None),
            P("patch"),
        ),
        check_vma=False,
    )
```

profile of v0, /device:TPU:8, one launch (start us, length us, event | category | flops | bytes accessed | tf_op | source)
XLA Modules:
  0.0 145.3 jit_solution(3277410749631074523)
XLA Ops:
  0.6 1.2 copy-done
  3.8 12.1 %all-to-all-start = ((bf16[64,4,512]{2,1,0:T(4,128)(2,1)}), bf16[64,4,512]{2,1,0:T(4,128)(2,1)S(1)}, u32[]{:S(2)}, u32[]{:S(2)}) async-start(bf16[64,4,512]{2,1,0:T(4,128)(2,1)} %all_to_all.17), calls=%async_computation | async-start | bytes 524288 | tf_op jit(solution)/shard_map/all_to_all | solution.py:446
  16.7 1.4 copy-done.10
  18.1 1.2 copy-done.16
  19.3 3.9 %shard_map.198.begun_ref = f32[1024,512]{1,0:T(8,128)S(1)} custom-call(bf16[1024,512]{1,0:T(8,128)(2,1)S(1)} %bitcast.15, bf16[1024,512]{1,0:T(8,128)(2,1)S(1)} %bitcast.20, s32[8,128]{1,0:T(8,128)S(1)} %copy-done.21, bf16[1536,512]{1,0:T(8,128)(2,1)S(1)} %copy-done.10), custom_call_target="tpu_custom_call" | custom-call | flops 2147483648 | bytes 5771264 | tf_op jit(solution)/shard_map/pallas_call | solution.py:395
  23.3 1.3 copy-done.25
  24.6 2.9 %all-to-all-done = bf16[64,4,512]{2,1,0:T(4,128)(2,1)S(1)} async-done(((bf16[64,4,512]{2,1,0:T(4,128)(2,1)}), bf16[64,4,512]{2,1,0:T(4,128)(2,1)S(1)}, u32[]{:S(2)}, u32[]{:S(2)}) %all-to-all-start) | async-done | bytes 262176 | tf_op jit(solution)/shard_map/all_to_all | solution.py:446
  27.6 1.3 copy-done.13
  28.9 1.2 copy-done.14
  31.1 1.0 copy-done.19
  32.2 19.2 %shard_map.199 = (bf16[1024,512]{1,0:T(8,128)(2,1)S(1)}, bf16[1024,512]{1,0:T(8,128)(2,1)S(1)}, bf16[1024,512]{1,0:T(8,128)(2,1)S(1)}, f32[1024,128]{1,0:T(8,128...) custom-call(s32[2]{0:T(128)S(1)} %pad_add_fusion.place_ref, ...), custom_call_target="tpu_custom_call" | custom-call | flops 8589934592 | bytes 16529420 | tf_op jit(solution)/shard_map/pallas_call | solution.py:395
  52.3 1.3 copy-done.26
  53.7 11.3 %shard_map.200 = (bf16[1024,512]{1,0:T(8,128)(2,1)}, f32[1024,512]{1,0:T(8,128)S(1)}, bf16[256,640]{1,0:T(8,128)(2,1)S(1)}, bf16[1024,512]{1,0:T(8,128)(2,1)S(1)...) custom-call(s32[1]{0:T(128)S(6)} %copy.22.count_ref, ...), custom_call_target="tpu_custom_call" | custom-call | flops 6442450944 | bytes 16855044 | tf_op jit(solution)/shard_map/pallas_call | solution.py:395
  65.0 5.2 %shard_map.203 = (bf16[4,1024,128]{2,1,0:T(8,128)(2,1)}, bf16[4,1024,128]{2,1,0:T(8,128)(2,1)S(1)}) custom-call(s32[2]{0:T(128)S(1)} %pad_add_fusion.place_ref, bf16[1024,512]{1,0:T(8,128)(2,1)S(1)} %get-tuple-element.57.hidden_ref, bf16[1024,512]{1,0:T(8,128)(2,1)S(1)} %get-tuple-element.58.second_ref, bf16[1024,512]{1,0:T(8,128)(2,1)S(1)} %bitcast.21, ...), custom_call_target="tpu_custom_call" | custom-call | flops 2147483648 | bytes 9961480 | tf_op jit(solution)/shard_map/pallas_call | solution.py:395
  72.4 7.6 %all-to-all-start.1 = ((bf16[64,4,640]{2,1,0:T(4,128)(2,1)}), bf16[64,4,640]{2,1,0:T(4,128)(2,1)}, u32[]{:S(2)}, u32[]{:S(2)}) async-start(bf16[64,4,640]{2,1,0:T(4,128)(2,1)} %all_to_all.20), calls=%async_computation.1 | async-start | bytes 655360 | tf_op jit(solution)/shard_map/all_to_all | solution.py:554
  80.1 1.1 copy-done.5
  81.2 1.3 shard_map.202
  82.5 1.5 %collective-permute-start.1 = (bf16[768,128]{1,0:T(8,128)(2,1)S(1)}, bf16[768,128]{1,0:T(8,128)(2,1)S(1)}, u32[]{:S(2)}, u32[]{:S(2)}) collective-permute-start(bf16[768,128]{1,0:T(8,128)(2,1)S(1)} %get-tuple-element.54), channel_id=1, source_target_pairs={{0,64},{64,128},{128,192},{192,0},{1,65},{65,129},{129,193},{193,1... | collective-permute-start | bytes 589832 | tf_op jit(solution)/shard_map/ppermute | solution.py:438
  84.0 1.5 %shard_map.204 = (bf16[1024,128]{1,0:T(8,128)(2,1)S(1)}, bf16[1024,128]{1,0:T(8,128)(2,1)S(1)}, bf16[1024,128]{1,0:T(8,128)(2,1)S(1)}, bf16[1024,128]{1,0:T(8,128)(2,1)S(1)}) custom-call(bf16[4,1024,128]{2,1,0:T(8,128)(2,1)S(1)} %copy-done.3, bf16[4,1024,128]{2,1,0:T(8,128)(2,1)} %collective-permute-done.4.got_ref), custom_call_target="tpu_custom_call" | custom-call | bytes 3145728 | tf_op jit(solution)/shard_map/pallas_call | solution.py:395
  85.5 1.7 %collective-permute-start.5 = (bf16[1024,128]{1,0:T(8,128)(2,1)S(1)}, bf16[1024,128]{1,0:T(8,128)(2,1)S(1)}, u32[]{:S(2)}, u32[]{:S(2)}) collective-permute-start(bf16[1024,128]{1,0:T(8,128)(2,1)S(1)} %get-tuple-element.65), channel_id=1, source_target_pairs={{0,64},{64,128},{128,192},{192,0},{1,65},{65,129},{129,193},{193,1... | collective-permute-start | bytes 786440 | tf_op jit(solution)/shard_map/ppermute | solution.py:438
  87.2 1.7 %collective-permute-start.6 = (bf16[1024,128]{1,0:T(8,128)(2,1)S(1)}, bf16[1024,128]{1,0:T(8,128)(2,1)S(1)}, u32[]{:S(2)}, u32[]{:S(2)}) collective-permute-start(bf16[1024,128]{1,0:T(8,128)(2,1)S(1)} %get-tuple-element.66), channel_id=1, source_target_pairs={{0,128},{64,192},{128,0},{192,64},{1,129},{65,193},{129,1},{193,65... | collective-permute-start | bytes 786440 | tf_op jit(solution)/shard_map/ppermute | solution.py:438
  88.9 2.1 %collective-permute-start.7 = (bf16[1024,128]{1,0:T(8,128)(2,1)S(1)}, bf16[1024,128]{1,0:T(8,128)(2,1)S(1)}, u32[]{:S(2)}, u32[]{:S(2)}) collective-permute-start(bf16[1024,128]{1,0:T(8,128)(2,1)S(1)} %get-tuple-element.67), channel_id=1, source_target_pairs={{0,192},{64,0},{128,64},{192,128},{1,193},{65,1},{129,65},{193,129... | collective-permute-start | bytes 786440 | tf_op jit(solution)/shard_map/ppermute | solution.py:438
  91.7 1.8 %collective-permute-start.3 = (bf16[768,128]{1,0:T(8,128)(2,1)S(1)}, bf16[768,128]{1,0:T(8,128)(2,1)S(1)}, u32[]{:S(2)}, u32[]{:S(2)}) collective-permute-start(bf16[768,128]{1,0:T(8,128)(2,1)S(1)} %get-tuple-element.56), channel_id=1, source_target_pairs={{0,192},{64,0},{128,64},{192,128},{1,193},{65,1},{129,65},{193,129... | collective-permute-start | bytes 589832 | tf_op jit(solution)/shard_map/ppermute | solution.py:438
  93.6 13.6 %collective-permute-done.2.refs_2_ = bf16[768,128]{1,0:T(8,128)(2,1)S(1)} collective-permute-done((bf16[768,128]{1,0:T(8,128)(2,1)S(1)}, bf16[768,128]{1,0:T(8,128)(2,1)S(1)}, u32[]{:S(2)}, u32[]{:S(2)}) %collective-permute-start.2) | collective-permute-done | bytes 196640 | tf_op jit(solution)/shard_map/ppermute | solution.py:438
  107.2 2.4 %collective-permute-done.3.refs_3_ = bf16[768,128]{1,0:T(8,128)(2,1)S(1)} collective-permute-done((bf16[768,128]{1,0:T(8,128)(2,1)S(1)}, bf16[768,128]{1,0:T(8,128)(2,1)S(1)}, u32[]{:S(2)}, u32[]{:S(2)}) %collective-permute-start.3) | collective-permute-done | bytes 196640 | tf_op jit(solution)/shard_map/ppermute | solution.py:438
  110.6 9.9 %all-to-all-start.2 = ((bf16[32,56,128]{2,1,0:T(8,128)(2,1)}), bf16[32,56,128]{2,1,0:T(8,128)(2,1)S(1)}, u32[]{:S(2)}, u32[]{:S(2)}) async-start(bf16[32,56,128]{2,1,0:T(8,128)(2,1)} %shard_map.205), calls=%async_computation.2 | async-start | bytes 917504 | tf_op jit(solution)/shard_map/all_to_all | solution.py:568
  120.5 1.1 all_to_all.22.returned_ref
  121.6 1.9 %shard_map.201 = (bf16[1024,512]{1,0:T(8,128)(2,1)}, f32[8,128]{1,0:T(8,128)S(1)}) custom-call(s32[1,256]{1,0:T(1,128)S(1)} %copy-done.9, bf16[256,640]{1,0:T(8,128)(2,1)S(1)} %all_to_all.22.returned_ref, f32[1024,512]{1,0:T(8,128)S(1)} %get-tuple-element.49.acc_ref), custom_call_target="tpu_custom_call" | custom-call | flops 268435456 | bytes 3478528 | tf_op jit(solution)/shard_map/pallas_call | solution.py:395
  123.5 10.5 %all-to-all-done.2.got_ref = bf16[32,56,128]{2,1,0:T(8,128)(2,1)S(1)} async-done(((bf16[32,56,128]{2,1,0:T(8,128)(2,1)}), bf16[32,56,128]{2,1,0:T(8,128)(2,1)S(1)}, u32[]{:S(2)}, u32[]{:S(2)}) %all-to-all-start.2) | async-done | bytes 458784 | tf_op jit(solution)/shard_map/all_to_all | solution.py:568
  134.0 3.7 %collective-permute-start.10 = (bf16[64,128]{1,0:T(8,128)(2,1)S(1)}, bf16[64,128]{1,0:T(8,128)(2,1)S(1)}, u32[]{:S(2)}, u32[]{:S(2)}) collective-permute-start(bf16[64,128]{1,0:T(8,128)(2,1)S(1)} %shard_map.206.a), channel_id=1, source_target_pairs={{0,192},{64,0},{128,64},{192,128},{1,193},{65,1},{129,65},{193,129... | collective-permute-start | bytes 49160 | tf_op jit(solution)/shard_map/ppermute | solution.py:438
  139.2 3.8 %collective-permute-done.9.c = bf16[64,128]{1,0:T(8,128)(2,1)S(1)} collective-permute-done((bf16[64,128]{1,0:T(8,128)(2,1)S(1)}, bf16[64,128]{1,0:T(8,128)(2,1)S(1)}, u32[]{:S(2)}, u32[]{:S(2)}) %collective-permute-start.9) | collective-permute-done | bytes 16416 | tf_op jit(solution)/shard_map/ppermute | solution.py:438
  143.5 1.2 shard_map.207
  (67 shorter events, 10.7 us)
Async XLA Ops:
  2.5 14.1 %copy-start.1 = (bf16[1,1024,512]{2,1,0:T(8,128)(2,1)S(1)}, bf16[1,1024,512]{2,1,0:T(8,128)(2,1)}, u32[]{:S(2)}) copy-start(bf16[1,1024,512]{2,1,0:T(8,128)(2,1)} %param.14) | copy-start | bytes 3145732
  2.5 14.1 %copy-start.21 = (s32[8,128]{1,0:T(8,128)S(1)}, s32[8,128]{1,0:T(8,128)}, u32[]{:S(2)}) copy-start(s32[8,128]{1,0:T(8,128)} %recv_ref.5) | copy-start | bytes 12292
  3.8 23.7 %all-to-all-start = ((bf16[64,4,512]{2,1,0:T(4,128)(2,1)}), bf16[64,4,512]{2,1,0:T(4,128)(2,1)S(1)}, u32[]{:S(2)}, u32[]{:S(2)}) async-start(bf16[64,4,512]{2,1,0:T(4,128)(2,1)} %all_to_all.17), calls=%async_computation | async-start | bytes 524288 | tf_op jit(solution)/shard_map/all_to_all | solution.py:446
  16.7 1.4 copy-start.10
  19.3 8.2 %copy-start.11 = (bf16[1536,512]{1,0:T(8,128)(2,1)S(1)}, bf16[1536,512]{1,0:T(8,128)(2,1)}, u32[]{:S(2)}) copy-start(bf16[1536,512]{1,0:T(8,128)(2,1)} %w_edge_ref.3) | copy-start | bytes 4718596
  19.3 8.3 %copy-start.22 = (s32[8,128]{1,0:T(8,128)S(1)}, s32[8,128]{1,0:T(8,128)}, u32[]{:S(2)}) copy-start(s32[8,128]{1,0:T(8,128)} %send_ref.3) | copy-start | bytes 12292
  19.3 8.3 %copy-start.23 = (f32[512]{0:T(512)S(1)}, f32[512]{0:T(512)}, u32[]{:S(2)}) copy-start(f32[512]{0:T(512)} %param.23) | copy-start | bytes 6148
  19.3 8.3 %copy-start.24 = (f32[512]{0:T(512)S(1)}, f32[512]{0:T(512)}, u32[]{:S(2)}) copy-start(f32[512]{0:T(512)} %param.20) | copy-start | bytes 6148
  23.2 1.3 copy-start.25
  27.5 23.9 %copy-start.6 = (bf16[256,512]{1,0:T(8,128)(2,1)}, bf16[256,512]{1,0:T(8,128)(2,1)S(1)}, u32[]{:S(2)}) copy-start(bf16[256,512]{1,0:T(8,128)(2,1)S(1)} %all_to_all.19.halo_ref) | copy-start | bytes 786436
  27.6 1.3 copy-start.13
  32.2 21.5 %copy-start.12 = (bf16[1536,512]{1,0:T(8,128)(2,1)S(1)}, bf16[1536,512]{1,0:T(8,128)(2,1)}, u32[]{:S(2)}) copy-start(bf16[1536,512]{1,0:T(8,128)(2,1)} %w_edge_ref.3) | copy-start | bytes 4718596
  32.2 21.5 %copy-start.15 = (bf16[1,1024,512]{2,1,0:T(8,128)(2,1)S(1)}, bf16[1,1024,512]{2,1,0:T(8,128)(2,1)}, u32[]{:S(2)}) copy-start(bf16[1,1024,512]{2,1,0:T(8,128)(2,1)} %param.17) | copy-start | bytes 3145732
  32.2 21.5 %copy-start.20 = (bf16[512,512]{1,0:T(8,128)(2,1)S(1)}, bf16[512,512]{1,0:T(8,128)(2,1)}, u32[]{:S(2)}) copy-start(bf16[512,512]{1,0:T(8,128)(2,1)} %w_edge_out_ref.3) | copy-start | bytes 1572868
  52.3 1.3 copy-start.26
  53.7 11.3 %copy-start.7 = (bf16[256,512]{1,0:T(8,128)(2,1)S(1)}, bf16[256,512]{1,0:T(8,128)(2,1)}, u32[]{:S(2)}) copy-start(bf16[256,512]{1,0:T(8,128)(2,1)} %copy-done.6) | copy-start | bytes 786436
  53.7 11.3 %copy-start.17 = (bf16[1,1024,512]{2,1,0:T(8,128)(2,1)S(1)}, bf16[1,1024,512]{2,1,0:T(8,128)(2,1)}, u32[]{:S(2)}) copy-start(bf16[1,1024,512]{2,1,0:T(8,128)(2,1)} %param.15) | copy-start | bytes 3145732
  71.1 12.9 %copy-start.3 = (bf16[4,1024,128]{2,1,0:T(8,128)(2,1)S(1)}, bf16[4,1024,128]{2,1,0:T(8,128)(2,1)}, u32[]{:S(2)}) copy-start(bf16[4,1024,128]{2,1,0:T(8,128)(2,1)} %copy-done.2) | copy-start | bytes 3145732
  71.1 12.9 %collective-permute-start.4 = (bf16[4,1024,128]{2,1,0:T(8,128)(2,1)}, bf16[4,1024,128]{2,1,0:T(8,128)(2,1)}, u32[]{:S(2)}, u32[]{:S(2)}) collective-permute-start(bf16[4,1024,128]{2,1,0:T(8,128)(2,1)} %get-tuple-element.63), channel_id=1, source_target_pairs={{0,1},{1,0},{2,3},{3,2},{4,5},{5,4},{6,7},{7,6},{8,9},{9,8},{10,11... | collective-permute-start | bytes 3145736 | tf_op jit(solution)/shard_map/ppermute | solution.py:553
  71.3 8.8 %collective-permute-start = (bf16[4,768,128]{2,1,0:T(8,128)(2,1)}, bf16[4,768,128]{2,1,0:T(8,128)(2,1)}, u32[]{:S(2)}, u32[]{:S(2)}) collective-permute-start(bf16[4,768,128]{2,1,0:T(8,128)(2,1)} %get-tuple-element.52), channel_id=1, source_target_pairs={{0,1},{1,0},{2,3},{3,2},{4,5},{5,4},{6,7},{7,6},{8,9},{9,8},{10,11... | collective-permute-start | bytes 2359304 | tf_op jit(solution)/shard_map/ppermute | solution.py:507
  72.4 38.2 %all-to-all-start.1 = ((bf16[64,4,640]{2,1,0:T(4,128)(2,1)}), bf16[64,4,640]{2,1,0:T(4,128)(2,1)}, u32[]{:S(2)}, u32[]{:S(2)}) async-start(bf16[64,4,640]{2,1,0:T(4,128)(2,1)} %all_to_all.20), calls=%async_computation.1 | async-start | bytes 655360 | tf_op jit(solution)/shard_map/all_to_all | solution.py:554
  82.5 9.2 %collective-permute-start.1 = (bf16[768,128]{1,0:T(8,128)(2,1)S(1)}, bf16[768,128]{1,0:T(8,128)(2,1)S(1)}, u32[]{:S(2)}, u32[]{:S(2)}) collective-permute-start(bf16[768,128]{1,0:T(8,128)(2,1)S(1)} %get-tuple-element.54), channel_id=1, source_target_pairs={{0,64},{64,128},{128,192},{192,0},{1,65},{65,129},{129,193},{193,1... | collective-permute-start | bytes 589832 | tf_op jit(solution)/shard_map/ppermute | solution.py:438
  85.5 36.1 %copy-start.9 = (s32[1,256]{1,0:T(1,128)S(1)}, s32[1,256]{1,0:T(1,128)}, u32[]{:S(2)}) copy-start(s32[1,256]{1,0:T(1,128)} %rows_ref.3) | copy-start | bytes 3076
  85.5 24.1 %collective-permute-start.5 = (bf16[1024,128]{1,0:T(8,128)(2,1)S(1)}, bf16[1024,128]{1,0:T(8,128)(2,1)S(1)}, u32[]{:S(2)}, u32[]{:S(2)}) collective-permute-start(bf16[1024,128]{1,0:T(8,128)(2,1)S(1)} %get-tuple-element.65), channel_id=1, source_target_pairs={{0,64},{64,128},{128,192},{192,0},{1,65},{65,129},{129,193},{193,1... | collective-permute-start | bytes 786440 | tf_op jit(solution)/shard_map/ppermute | solution.py:438
  87.2 22.4 %collective-permute-start.6 = (bf16[1024,128]{1,0:T(8,128)(2,1)S(1)}, bf16[1024,128]{1,0:T(8,128)(2,1)S(1)}, u32[]{:S(2)}, u32[]{:S(2)}) collective-permute-start(bf16[1024,128]{1,0:T(8,128)(2,1)S(1)} %get-tuple-element.66), channel_id=1, source_target_pairs={{0,128},{64,192},{128,0},{192,64},{1,129},{65,193},{129,1},{193,65... | collective-permute-start | bytes 786440 | tf_op jit(solution)/shard_map/ppermute | solution.py:438
  88.9 20.7 %collective-permute-start.7 = (bf16[1024,128]{1,0:T(8,128)(2,1)S(1)}, bf16[1024,128]{1,0:T(8,128)(2,1)S(1)}, u32[]{:S(2)}, u32[]{:S(2)}) collective-permute-start(bf16[1024,128]{1,0:T(8,128)(2,1)S(1)} %get-tuple-element.67), channel_id=1, source_target_pairs={{0,192},{64,0},{128,64},{192,128},{1,193},{65,1},{129,65},{193,129... | collective-permute-start | bytes 786440 | tf_op jit(solution)/shard_map/ppermute | solution.py:438
  91.0 16.2 %collective-permute-start.2 = (bf16[768,128]{1,0:T(8,128)(2,1)S(1)}, bf16[768,128]{1,0:T(8,128)(2,1)S(1)}, u32[]{:S(2)}, u32[]{:S(2)}) collective-permute-start(bf16[768,128]{1,0:T(8,128)(2,1)S(1)} %get-tuple-element.55), channel_id=1, source_target_pairs={{0,128},{64,192},{128,0},{192,64},{1,129},{65,193},{129,1},{193,65... | collective-permute-start | bytes 589832 | tf_op jit(solution)/shard_map/ppermute | solution.py:438
  91.7 17.8 %collective-permute-start.3 = (bf16[768,128]{1,0:T(8,128)(2,1)S(1)}, bf16[768,128]{1,0:T(8,128)(2,1)S(1)}, u32[]{:S(2)}, u32[]{:S(2)}) collective-permute-start(bf16[768,128]{1,0:T(8,128)(2,1)S(1)} %get-tuple-element.56), channel_id=1, source_target_pairs={{0,192},{64,0},{128,64},{192,128},{1,193},{65,1},{129,65},{193,129... | collective-permute-start | bytes 589832 | tf_op jit(solution)/shard_map/ppermute | solution.py:438
  110.6 23.4 %all-to-all-start.2 = ((bf16[32,56,128]{2,1,0:T(8,128)(2,1)}), bf16[32,56,128]{2,1,0:T(8,128)(2,1)S(1)}, u32[]{:S(2)}, u32[]{:S(2)}) async-start(bf16[32,56,128]{2,1,0:T(8,128)(2,1)} %shard_map.205), calls=%async_computation.2 | async-start | bytes 917504 | tf_op jit(solution)/shard_map/all_to_all | solution.py:568
  134.0 5.1 %collective-permute-start.10 = (bf16[64,128]{1,0:T(8,128)(2,1)S(1)}, bf16[64,128]{1,0:T(8,128)(2,1)S(1)}, u32[]{:S(2)}, u32[]{:S(2)}) collective-permute-start(bf16[64,128]{1,0:T(8,128)(2,1)S(1)} %shard_map.206.a), channel_id=1, source_target_pairs={{0,192},{64,0},{128,64},{192,128},{1,193},{65,1},{129,65},{193,129... | collective-permute-start | bytes 49160 | tf_op jit(solution)/shard_map/ppermute | solution.py:438
  137.7 5.2 %collective-permute-start.9 = (bf16[64,128]{1,0:T(8,128)(2,1)S(1)}, bf16[64,128]{1,0:T(8,128)(2,1)S(1)}, u32[]{:S(2)}, u32[]{:S(2)}) collective-permute-start(bf16[64,128]{1,0:T(8,128)(2,1)S(1)} %shard_map.206.a), channel_id=1, source_target_pairs={{0,128},{64,192},{128,0},{192,64},{1,129},{65,193},{129,1},{193,65... | collective-permute-start | bytes 49160 | tf_op jit(solution)/shard_map/ppermute | solution.py:438
  138.6 4.9 %collective-permute-start.8 = (bf16[64,128]{1,0:T(8,128)(2,1)S(1)}, bf16[64,128]{1,0:T(8,128)(2,1)S(1)}, u32[]{:S(2)}, u32[]{:S(2)}) collective-permute-start(bf16[64,128]{1,0:T(8,128)(2,1)S(1)} %shard_map.206.a), channel_id=1, source_target_pairs={{0,64},{64,128},{128,192},{192,0},{1,65},{65,129},{129,193},{193,1... | collective-permute-start | bytes 49160 | tf_op jit(solution)/shard_map/ppermute | solution.py:438
  (9 other events, 9.4 us)
where the time goes:
time: 148 us; the launch traced here: 145 us
  Pallas kernels  47.1 us (32%)
  starting transfers between devices  44.4 us (30%)
  waiting for transfers between devices  34.2 us (23%)
  local copies, waits for them, and re-layouts  18.1 us (12%)
  between operations  1.51 us (1%)
    pallas_call x11, Pallas kernels, call(): pl.pallas_call(kernel, out_shape=shapes[0] if single else shapes, in_spec...  47.1 us
    ppermute x9, waiting for transfers between devices, to_member(): lax.ppermute(x, 'group', [(g, (g + shift) % members) for g in range(membe...  20.8 us
    unnamed x54, local copies, waits for them, and re-layouts  14.8 us
    ppermute x9, starting transfers between devices, to_member(): lax.ppermute(x, 'group', [(g, (g + shift) % members) for g in range(membe...  14.2 us
    all_to_all x1, starting transfers between devices, local(): lax.all_to_all(outgoing, 'patch', split_axis=0, concat_axis=0, tiled=True)  12.1 us
    all_to_all x1, waiting for transfers between devices, local(): lax.all_to_all(blocks, 'patch', split_axis=0, concat_axis=0, axis_index_g...  10.5 us
    all_to_all x1, starting transfers between devices, local(): lax.all_to_all(blocks, 'patch', split_axis=0, concat_axis=0, axis_index_g...  9.92 us
    all_to_all x1, starting transfers between devices, local(): lax.all_to_all(outward, 'patch', split_axis=0, concat_axis=0, tiled=True)  7.62 us
  transfers between devices with their start and end apart: 14, of which 7 were waited for; matrix products, arithmetic and copies ran while one was open for 0% of the time, Pallas kernels for 7%

commit v1 on v0

v1 whole, which is shorter than its diff:
```python
import functools

import jax
import jax.numpy as jnp
from jax import lax
from jax.experimental import pallas as pl
from jax.experimental.pallas import tpu as pltpu
from jax.sharding import PartitionSpec as P

epsilon = 1e-05
BF = jnp.bfloat16
F32 = jnp.float32
LANE = 128
ROWS = 256
FULL = 60 * 2**20


def dot(a, b):
    return lax.dot_general(a, b, (((1,), (0,)), ((), ())), preferred_element_type=F32)


def dot_rt(a, b):
    return lax.dot_general(a, b, (((1,), (1,)), ((), ())), preferred_element_type=F32)


def dot_lt(a, b):
    return lax.dot_general(a, b, (((0,), (0,)), ((), ())), preferred_element_type=F32)


def iota(shape, dim):
    return lax.broadcasted_iota(jnp.int32, shape, dim)


def one_hot(mask):
    return jnp.where(mask, 1.0, 0.0).astype(BF)


def columns_of(index_ref, out_ref):
    tiles = index_ref.shape[0]
    full = jnp.concatenate(
        [index_ref[...], jnp.zeros((LANE - tiles, LANE), jnp.int32)], axis=0
    )
    turned = full.T
    for t in range(tiles):
        out_ref[t * LANE : (t + 1) * LANE, :] = jnp.broadcast_to(
            turned[:, t : t + 1], (LANE, LANE)
        )


def pick_rows(cols_ref, start, count, first, width):
    column = cols_ref[pl.ds(start, count), 0:1]
    return one_hot(column == iota((count, width), 1) + first)


def spread_rows(index_ref, start, count):
    tiles = index_ref.shape[0]
    base = iota((count, LANE), 0) + start
    return jnp.concatenate([one_hot(index_ref[t : t + 1, :] == base) for t in range(tiles)], axis=1)


def sigmoid(v):
    return 1.0 / (1.0 + jnp.exp(-v))


def live_rows(count_ref, start, count):
    return (iota((count, 1), 0) + start < count_ref[0] * LANE).astype(F32)


def normalize(values):
    centred = values - jnp.mean(values, axis=1, keepdims=True)
    inverse = lax.rsqrt(jnp.mean(centred * centred, axis=1, keepdims=True) + epsilon)
    return centred * inverse, inverse


def normalize_back(upstream, normed, inverse):
    return inverse * (
        upstream
        - jnp.mean(upstream, axis=1, keepdims=True)
        - normed * jnp.mean(upstream * normed, axis=1, keepdims=True)
    )


def loop(count, body):
    def step(i, carry):
        body(pl.multiple_of(i * ROWS, ROWS), i)
        return carry

    lax.fori_loop(0, count // ROWS, step, 0)


def outgoing_kernel(rows_ref, node, out_ref):
    nodes, halo = node.shape[0], rows_ref.shape[1]
    spread = one_hot(rows_ref[...] == iota((nodes, halo), 0))
    out_ref[...] = dot_lt(spread, node.ready()[...]).astype(BF)


def own_kernel(
    send_ref,
    recv_ref,
    node,
    edge,
    w_edge,
    spread_recv,
    spread_send,
    node_turned,
    edge_turned,
    pick,
    begun,
    send_cols,
    recv_cols,
):
    nodes, width = node.shape
    columns_of(send_ref, send_cols)
    columns_of(recv_ref, recv_cols)
    for index_ref, out in ((recv_ref, spread_recv), (send_ref, spread_send)):

        def spread(start, i):
            out.buffer[pl.ds(start, ROWS), :] = spread_rows(index_ref, start, ROWS)
            out.send(i)

        loop(out.shape[0], spread)
    node_ref, edge_ref, w_ref = node.ready(), edge.ready(), w_edge.ready()
    for source, out in ((node_ref, node_turned), (edge_ref, edge_turned)):
        for i in range(0, source.shape[0], ROWS):
            out.buffer[:, i : i + ROWS] = source[i : i + ROWS, :].T
        out.send(0)

    def body(start, i):
        here = pl.ds(start, ROWS)
        picked = pick_rows(recv_cols, start, ROWS, 0, nodes)
        pick.buffer[here, :] = picked
        from_send = dot(pick_rows(send_cols, start, ROWS, 0, nodes), node_ref[...]).astype(BF)
        from_recv = dot(picked, node_ref[...]).astype(BF)
        begun.buffer[here, :] = (
            dot(edge_ref[here, :], w_ref[0:width, :])
            + dot(from_send, w_ref[width : 2 * width, :])
            + dot(from_recv, w_ref[2 * width : 3 * width, :])
        )
        pick.send(i)
        begun.send(i)

    loop(edge_ref.shape[0], body)


def deal(place_ref, depth, pieces, send, keep):
    core, column = place_ref[0], place_ref[1]
    each = sum(rows for _, rows in pieces)
    batch = 1 if each % 16 == 0 else 2
    for which, out in ((1 - core, send), (core, keep)):

        def step(s, carry):
            for i in range(0, depth, batch):
                found = []
                for b in range(batch):
                    patch = (((column + s) % 4) * depth + i + b) * 2 + which
                    for ref, rows in pieces:
                        found.append(ref[pl.ds(pl.multiple_of(patch * rows, 8), rows), :])
                out.buffer[s, i * each : (i + batch) * each, :] = jnp.concatenate(
                    found, axis=0
                ).astype(BF)
            out.send(s)
            return carry

        lax.fori_loop(0, 4, step, 0)


def forward_kernel(
    patches,
    place_ref,
    count_ref,
    send_ref,
    gain_edge_ref,
    gain_node_ref,
    incoming,
    begun,
    w_send,
    w_edge_out,
    spread_recv,
    node,
    w_node,
    w_node_out,
    cot,
    node_turned,
    gain_ref,
    slope,
    normed_out,
    inverse_out,
    hidden_out,
    node_acc,
    back,
    piece_send,
    piece_keep,
    cols,
    message,
    gathered,
    node_hidden,
    grad_second,
    grad_first,
    sum_in,
    sum_out,
):
    nodes, width = node.shape
    halo = incoming.shape[0]
    columns_of(send_ref, cols)
    halo_ref, w_send_ref, w_edge_out_ref = incoming.ready(), w_send.ready(), w_edge_out.ready()

    def edge_body(start, i):
        here = pl.ds(start, ROWS)
        latent = dot(pick_rows(cols, start, ROWS, nodes, halo), halo_ref[...])
        begun_ref = begun.part(i)
        first = begun_ref[here, :] + dot(latent.astype(BF), w_send_ref[...])
        squash = sigmoid(first)
        hidden = (first * squash).astype(BF)
        hidden_out.buffer[here, :] = hidden
        slope.buffer[here, :] = (squash * (1.0 + first * (1.0 - squash))).astype(BF)
        normed, inverse = normalize(dot(hidden, w_edge_out_ref[...]))
        normed_out.buffer[here, :] = normed.astype(BF)
        inverse_out.buffer[here, :] = jnp.broadcast_to(inverse, (ROWS, LANE))
        live = live_rows(count_ref, start, ROWS)
        message[here, :] = (live * (gain_edge_ref[...] * normed)).astype(BF)

        for out in (hidden_out, slope, normed_out, inverse_out):
            out.send(i)

    loop(begun.shape[0], edge_body)
    gain_ref[...] = jnp.zeros_like(gain_ref)
    node_ref, w_node_ref, w_node_out_ref = node.ready(), w_node.ready(), w_node_out.ready()
    cot_ref = cot.ready()

    def node_body(start, i):
        here = pl.ds(start, ROWS)
        spread_recv_ref = spread_recv.part(i)
        taken = dot(spread_recv_ref[here, :], message[...]).astype(BF)
        gathered[here, :] = taken
        first = dot(node_ref[here, :], w_node_ref[0:width, :]) + dot(
            taken, w_node_ref[width : 2 * width, :]
        )
        squash = sigmoid(first)
        hidden = (first * squash).astype(BF)
        node_hidden[here, :] = hidden
        node_slope = squash * (1.0 + first * (1.0 - squash))
        normed, inverse = normalize(dot(hidden, w_node_out_ref[...]))
        upstream = cot_ref[here, :].astype(F32)
        gain_ref[...] += jnp.sum(upstream * normed, axis=0, keepdims=True)
        second = normalize_back(upstream * gain_node_ref[...], normed, inverse).astype(BF)
        grad_second[here, :] = second
        grad = (dot_rt(second, w_node_out_ref[...]) * node_slope).astype(BF)
        grad_first[here, :] = grad
        node_acc.buffer[here, :] = upstream + dot_rt(grad, w_node_ref[0:width, :])
        back.buffer[here, :] = dot_rt(grad, w_node_ref[width : 2 * width, :]).astype(BF)
        node_acc.send(i)
        back.send(i)

    loop(nodes, node_body)
    sum_out[...] = dot_lt(node_hidden[...], grad_second[...])
    node_turned_ref = node_turned.ready()
    sum_in[0:width, :] = dot(node_turned_ref[...], grad_first[...])
    sum_in[width : 2 * width, :] = dot_lt(gathered[...], grad_first[...])
    pieces = ((sum_in, 2 * width // patches), (sum_out, width // patches))
    deal(place_ref, patches // 8, pieces, piece_send, piece_keep)


def backward_kernel(
    count_ref,
    gain_edge_ref,
    w_edge_out,
    back,
    pick,
    cot,
    normed_in,
    inverse,
    slope,
    gain_ref,
    token_ref,
    second_out,
    first_out,
):
    edges = cot.shape[0]
    gain_ref[...] = jnp.zeros_like(gain_ref)
    token_ref[...] = jnp.zeros_like(token_ref)
    w_edge_out_ref, back_ref = w_edge_out.ready(), back.ready()

    def edge_body(start, i):
        here = pl.ds(start, ROWS)
        live = live_rows(count_ref, start, ROWS)
        for part in (pick, cot, normed_in, inverse, slope):
            part.part(i)
        taken = dot(pick.buffer[here, :], back_ref[...])
        message = live * (cot.buffer[here, :].astype(F32) + taken)
        normed = normed_in.buffer[here, :].astype(F32)
        gain_ref[...] += jnp.sum(message * normed, axis=0, keepdims=True)
        second = normalize_back(
            message * gain_edge_ref[...], normed, inverse.buffer[here, 0:1]
        ).astype(BF)
        second_out.buffer[here, :] = second
        first_out.buffer[here, :] = (
            dot_rt(second, w_edge_out_ref[...]) * slope.buffer[here, :].astype(F32)
        ).astype(BF)
        second_out.send(i)
        first_out.send(i)

    loop(edges, edge_body)


def edge_weight_kernel(
    patches,
    place_ref,
    gain_edge_ref,
    gain_node_ref,
    after_ref,
    first,
    spread_send,
    spread_recv,
    hidden,
    second,
    edge_turned,
    node_turned,
    incoming,
    token_ref,
    from_send,
    from_recv,
    piece_send,
    piece_keep,
    sum_in,
    sum_out,
):
    width, nodes = node_turned.shape
    halo = incoming.shape[0]
    token_ref[...] = jnp.zeros_like(token_ref)
    first_ref = first.ready()
    for out, spread in ((from_send, spread_send), (from_recv, spread_recv)):

        def body(start, i):
            here = pl.ds(start, ROWS)
            out.buffer[here, :] = dot(spread.part(i)[here, :], first_ref[...]).astype(BF)
            out.send(i)

        loop(out.shape[0], body)
    sent, received = from_send.buffer, from_recv.buffer
    node_turned_ref = node_turned.ready()
    sum_in[0:width, :] = dot(edge_turned.ready()[...], first_ref[...])
    sum_in[width : 2 * width, :] = dot(node_turned_ref[...], sent[0:nodes, :]) + dot_lt(
        incoming.ready()[...], sent[nodes : nodes + halo, :]
    )
    sum_in[2 * width : 3 * width, :] = dot(node_turned_ref[...], received[...])
    sum_out[...] = dot_lt(hidden.ready()[...], second.ready()[...])
    extra = jnp.concatenate(
        [gain_edge_ref[...], gain_node_ref[...], jnp.zeros((14, width), F32)], axis=0
    ).astype(BF)
    rows = piece_keep.shape[1]
    for out in (piece_send, piece_keep):
        for s in range(4):
            out.buffer[s, rows - 16 : rows, :] = extra
    pieces = ((sum_in, 3 * width // patches), (sum_out, width // patches))
    deal(place_ref, patches // 8, pieces, piece_send, piece_keep)


def gate_kernel(after_ref, x_ref, out_ref):
    pass


def return_kernel(after_ref, halo_part, w_send, return_ref):
    return_ref[...] = dot_rt(halo_part.ready()[...], w_send.ready()[...]).astype(BF)


def input_kernel(
    count_ref,
    after_ref,
    w_edge,
    node_acc,
    from_send,
    from_recv,
    first,
    cot,
    token_ref,
    node_out,
    edge_grad,
):
    nodes, width = node_acc.shape
    token_ref[...] = jnp.zeros_like(token_ref)
    w_edge_ref = w_edge.ready()

    def node_body(start, i):
        here = pl.ds(start, ROWS)
        node_out.buffer[here, :] = (
            node_acc.part(i)[here, :]
            + dot_rt(from_send.part(i)[here, :], w_edge_ref[width : 2 * width, :])
            + dot_rt(from_recv.part(i)[here, :], w_edge_ref[2 * width : 3 * width, :])
        )
        node_out.send(i)

    loop(nodes, node_body)

    def edge_body(start, i):
        here = pl.ds(start, ROWS)
        live = live_rows(count_ref, start, ROWS)
        edge_grad.buffer[here, :] = (
            live * cot.part(i)[here, :].astype(F32)
            + dot_rt(first.part(i)[here, :], w_edge_ref[0:width, :])
        ).astype(BF)
        edge_grad.send(i)

    loop(cot.shape[0], edge_body)


def node_grad_kernel(rows_ref, after_ref, returned, acc, out):
    nodes = acc.shape[0]
    halo = returned.shape[0]
    returned_ref = returned.ready()

    def body(start, i):
        here = pl.ds(start, ROWS)
        spread = one_hot(rows_ref[...] == iota((ROWS, halo), 0) + start)
        out.buffer[here, :] = (acc.part(i)[here, :] + dot(spread, returned_ref[...])).astype(BF)
        out.send(i)

    loop(nodes, body)


def pair_kernel(after_ref, got, keep, token_ref, *outs):
    token_ref[...] = jnp.zeros_like(token_ref)
    for s in (1, 2, 3, 0):
        got.part(s)
        keep.part(s)
        outs[s].buffer[...] = (keep.buffer[s].astype(F32) + got.buffer[s].astype(F32)).astype(BF)
        outs[s].send(0)


def four_kernel(a, b, c, d, after_ref, out_ref, token_ref):
    total = a[...].astype(F32) + b[...].astype(F32) + c[...].astype(F32) + d[...].astype(F32)
    token_ref[...] = jnp.zeros_like(token_ref)
    depth, rows = out_ref.shape[0:2]
    if total.shape[0] == depth * rows:
        out_ref[...] = total.reshape(depth, rows, total.shape[1]).astype(BF)
    else:
        for z in range(depth):
            out_ref[z] = jnp.concatenate(
                [total[z * (rows - 8) : (z + 1) * (rows - 8)], total[depth * (rows - 8) :][0:8]],
                axis=0,
            ).astype(BF)


def depth_kernel(node_ref, edge_ref, out_ref):
    found = []
    for ref in (node_ref, edge_ref):
        total = ref[0].astype(F32)
        for i in range(1, ref.shape[0]):
            total = total + ref[i].astype(F32)
        found.append(total)
    out_ref[...] = jnp.concatenate(found, axis=0).astype(BF)


def finish_kernel(
    factor,
    place_ref,
    a,
    b,
    c,
    d,
    edge_in_ref,
    edge_out_ref,
    node_in_ref,
    node_out_ref,
    gain_ref,
    rows,
):
    member = place_ref[2]
    for s, ref in enumerate((a, b, c, d)):
        rows[(member - s + 4) % 4] = ref[...].astype(F32)
    total = ((rows[0] + rows[1]) + (rows[2] + rows[3])) * factor
    at = 0
    for out in (node_in_ref, node_out_ref, edge_in_ref, edge_out_ref, gain_ref):
        out[...] = total[at : at + out.shape[0], :]
        at += out.shape[0]


VM = pl.BlockSpec(memory_space=pltpu.VMEM)
SM = pl.BlockSpec(memory_space=pltpu.SMEM)
TOKEN = ((8, LANE), F32)


class Moved:
    def __init__(self, far, buffer, semaphores, parts, first, outward):
        self.far, self.buffer, self.semaphores = far, buffer, semaphores
        self.parts, self.first, self.outward = parts, first, outward
        self.shape = buffer.shape
        self.step = buffer.shape[0] // parts

    def copy(self, i):
        near = self.buffer.at[pl.ds(i * self.step, self.step)]
        far = self.far.at[pl.ds(self.first + i * self.step, self.step)]
        ends = (near, far) if self.outward else (far, near)
        return pltpu.make_async_copy(*ends, self.semaphores.at[i])

    def send(self, i):
        self.copy(i).start()

    def part(self, i):
        self.copy(i).wait()
        return self.buffer

    def ready(self):
        for i in range(self.parts):
            self.copy(i).wait()
        return self.buffer


class Part:
    def __init__(self, array, parts=1, first=0, rows=None):
        self.array, self.parts, self.first = array, parts, first
        self.rows = array.shape[0] if rows is None else rows


def call(kernel, outs, ins, scratch=(), scalars=0, flops=0, fetch=(), store=(), limit=None):
    ins = list(ins)
    fetch = [f if isinstance(f, Part) else Part(f) for f in fetch]
    shapes = [jax.ShapeDtypeStruct(s, d) for s, d in list(outs) + [o[:2] for o in store]]
    single = len(shapes) == 1
    buffers = [((f.rows, *f.array.shape[1:]), f.array.dtype) for f in fetch]
    size = sum(int(a.size) * a.dtype.itemsize for a in ins + shapes)
    held = list(scratch) + buffers + [o[:2] for o in store]
    bytes_here = sum(
        functools.reduce(lambda x, y: x * y, s) * jnp.dtype(d).itemsize for s, d in held
    )
    many, kept, given = len(fetch), len(store), len(outs)

    def take(refs, count):
        return refs[:count], refs[count:]

    def body(*refs):
        args, refs = take(refs, len(ins))
        sources, refs = take(refs, many)
        results, refs = take(refs, given)
        targets, refs = take(refs, kept)
        own, refs = take(refs, len(scratch))
        slots, refs = take(refs, many)
        rooms, refs = take(refs, kept)
        marks, ends = take(refs, many)
        arriving = [
            Moved(src, slot, mark, f.parts, f.first, False)
            for src, f, slot, mark in zip(sources, fetch, slots, marks)
        ]
        for one in arriving:
            for i in range(one.parts):
                one.send(i)
        leaving = [
            Moved(t, room, end, o[2], 0, True)
            for t, room, end, o in zip(targets, rooms, ends, store)
        ]
        kernel(*args, *arriving, *results, *leaving, *own)
        for one in leaving:
            one.ready()

    far = pl.BlockSpec(memory_space=pltpu.HBM)
    out_specs = [VM] * given + [far] * kept
    return pl.pallas_call(
        body,
        out_shape=shapes[0] if single else shapes,
        in_specs=[SM] * scalars + [VM] * (len(ins) - scalars) + [far] * many,
        out_specs=out_specs[0] if single else out_specs,
        scratch_shapes=[pltpu.VMEM(s, d) for s, d in held]
        + [pltpu.SemaphoreType.DMA((f.parts,)) for f in fetch]
        + [pltpu.SemaphoreType.DMA((o[2],)) for o in store],
        compiler_params=pltpu.CompilerParams(
            vmem_limit_bytes=bytes_here + 4 * 2**20 if limit is None else limit
        ),
        cost_estimate=pl.CostEstimate(flops=flops, bytes_accessed=size, transcendentals=0),
    )(*ins, *[f.array for f in fetch])


def gate(x, token):
    return pl.pallas_call(
        gate_kernel,
        out_shape=jax.ShapeDtypeStruct(x.shape, x.dtype),
        in_specs=[VM, pl.BlockSpec(memory_space=pltpu.HBM)],
        out_specs=pl.BlockSpec(memory_space=pltpu.HBM),
        input_output_aliases={1: 0},
        compiler_params=pltpu.CompilerParams(vmem_limit_bytes=FULL),
    )(token, x)


def local(
    node_tape,
    edge_tape,
    node_cot,
    edge_cot,
    w_edge_in,
    w_edge_out,
    gain_edge,
    w_node_in,
    w_node_out,
    gain_node,
    senders,
    receivers,
    tile_count,
    send_rows,
):
    node, edge = node_tape[0], edge_tape[0]
    n_cot, e_cot = node_cot[0], edge_cot[0]
    nodes, width = node.shape
    edges = edge.shape[0]
    halo = send_rows.shape[1]
    patches = lax.axis_size("patch")
    members = lax.axis_size("group")
    depth = patches // 8
    here = lax.axis_index("patch")
    place = jnp.stack([here % 2, here // (2 * depth), lax.axis_index("group")]).astype(jnp.int32)
    gain_edge = gain_edge.reshape(1, width)
    gain_node = gain_node.reshape(1, width)
    twins = [(i, i ^ 1) for i in range(patches)]
    column = 2 * depth
    lines = [[y * column + 2 * z + c for z in range(depth)] for y in range(4) for c in range(2)]
    unit = 2 * width * width

    def to_member(x, shift):
        return lax.ppermute(x, "group", [(g, (g + shift) % members) for g in range(members)])

    def to_column(x, shift):
        return lax.ppermute(x, "patch", [(i, (i + shift * column) % patches) for i in range(patches)])

    def along_depth(x, rows):
        return lax.all_to_all(
            x.reshape(depth, rows, width), "patch", 0, 0, axis_index_groups=lines, tiled=True
        )

    parts = edges // ROWS

    def wide(rows, kind=BF):
        return ((rows, width), kind, rows // ROWS)

    outgoing = call(
        outgoing_kernel,
        [((halo, width), BF)],
        [send_rows],
        flops=2 * halo * nodes * width,
        fetch=[node],
        limit=FULL,
    )
    incoming = lax.all_to_all(outgoing, "patch", split_axis=0, concat_axis=0, tiled=True)
    spread_recv, spread_send, node_turned, edge_turned, pick_recv, begun = call(
        own_kernel,
        [],
        [senders, receivers],
        [((edges, LANE), jnp.int32)] * 2,
        flops=7 * edges * unit,
        fetch=[node, edge, w_edge_in],
        store=[
            ((nodes, edges), BF, nodes // ROWS),
            ((nodes + halo, edges), BF, (nodes + halo) // ROWS),
            ((width, nodes), BF, 1),
            ((width, edges), BF, 1),
            ((edges, nodes), BF, parts),
            wide(edges, F32),
        ],
        limit=FULL,
    )
    per_node, per_edge = 3 * width // patches, 4 * width // patches
    node_piece = ((4, depth * per_node, width), BF, 4)
    edge_piece = ((4, depth * per_edge + 16, width), BF, 4)
    w_send = Part(w_edge_in, 1, width, width)
    (
        sum_gain_node,
        slope,
        normed,
        inverse,
        hidden,
        node_acc,
        back,
        node_send,
        node_keep,
    ) = call(
        functools.partial(forward_kernel, patches),
        [((1, width), F32)],
        [place, tile_count, senders, gain_edge, gain_node],
        [
            ((edges, LANE), jnp.int32),
            ((edges, width), BF),
            ((nodes, width), BF),
            ((nodes, width), BF),
            ((nodes, width), BF),
            ((nodes, width), BF),
            ((2 * width, width), F32),
            ((width, width), F32),
        ],
        scalars=2,
        flops=14 * nodes * unit,
        fetch=[
            incoming,
            Part(begun, parts),
            w_send,
            w_edge_out,
            Part(spread_recv, nodes // ROWS),
            node,
            w_node_in,
            w_node_out,
            n_cot,
            node_turned,
        ],
        store=[
            wide(edges),
            wide(edges),
            ((edges, LANE), F32, parts),
            wide(edges),
            wide(nodes, F32),
            wide(nodes),
            node_piece,
            node_piece,
        ],
        limit=FULL,
    )
    node_got = lax.ppermute(node_send, "patch", twins)
    sum_gain_edge, token, grad_second, grad_first = call(
        backward_kernel,
        [((1, width), F32), TOKEN],
        [tile_count, gain_edge],
        scalars=1,
        flops=3 * nodes * unit,
        fetch=[
            w_edge_out,
            back,
            Part(pick_recv, parts),
            Part(e_cot, parts),
            Part(normed, parts),
            Part(inverse, parts),
            Part(slope, parts),
        ],
        store=[wide(edges), wide(edges)],
        limit=FULL,
    )

    def after_pair(keep, got, after):
        shape = keep.shape[1:]
        token, *found = call(
            pair_kernel,
            [TOKEN],
            [after],
            fetch=[Part(got, 4), Part(keep, 4)],
            store=[(shape, BF, 1)] * 4,
        )
        return token, [found[0]] + [to_column(found[s], s) for s in range(1, 4)]

    token, node_parts = after_pair(node_keep, node_got, token)
    token, from_send, from_recv, edge_send, edge_keep = call(
        functools.partial(edge_weight_kernel, patches),
        [TOKEN],
        [place, sum_gain_edge, sum_gain_node, token],
        [((3 * width, width), F32), ((width, width), F32)],
        scalars=1,
        flops=9 * nodes * unit,
        fetch=[
            grad_first,
            Part(spread_send, (nodes + halo) // ROWS),
            Part(spread_recv, nodes // ROWS),
            hidden,
            grad_second,
            edge_turned,
            node_turned,
            incoming,
        ],
        store=[wide(nodes + halo), wide(nodes), edge_piece, edge_piece],
        limit=FULL,
    )
    node_blocks, token = call(
        four_kernel, [((depth, per_node, width), BF), TOKEN], node_parts + [token]
    )
    node_lines = along_depth(node_blocks, per_node)
    edge_got = lax.ppermute(gate(edge_send, token), "patch", twins)
    token, edge_parts = after_pair(edge_keep, edge_got, token)
    outward = call(
        return_kernel,
        [((halo, width), BF)],
        [token],
        flops=unit * halo,
        fetch=[Part(from_send, 1, nodes, halo), w_send],
    )
    returned = lax.all_to_all(outward, "patch", split_axis=0, concat_axis=0, tiled=True)
    token, node_part, edge_grad = call(
        input_kernel,
        [TOKEN],
        [tile_count, token],
        scalars=1,
        flops=3 * nodes * unit,
        fetch=[
            w_edge_in,
            Part(node_acc, nodes // ROWS),
            Part(from_send, nodes // ROWS, 0, nodes),
            Part(from_recv, nodes // ROWS),
            Part(grad_first, parts),
            Part(e_cot, parts),
        ],
        store=[wide(nodes, F32), wide(edges)],
        limit=FULL,
    )
    edge_blocks, token = call(
        four_kernel, [((depth, per_edge + 8, width), BF), TOKEN], edge_parts + [token]
    )
    edge_lines = along_depth(edge_blocks, per_edge + 8)
    node_grad = call(
        node_grad_kernel,
        [],
        [send_rows, token],
        flops=2 * nodes * halo * width,
        fetch=[returned, Part(node_part, nodes // ROWS)],
        store=[wide(nodes)],
        limit=FULL,
    )
    rows = per_node + per_edge + 8
    mine = call(depth_kernel, [((rows, width), BF)], [node_lines, edge_lines])
    shared = [mine] + [to_member(mine, s) for s in range(1, 4)]
    factor = float(members * patches * edges) ** (-0.5)
    each = width // patches
    out_edge_in, out_edge_out, out_node_in, out_node_out, out_gain = call(
        functools.partial(finish_kernel, factor),
        [
            ((3 * each, width), F32),
            ((each, width), F32),
            ((2 * each, width), F32),
            ((each, width), F32),
            ((8, width), F32),
        ],
        [place] + shared,
        [((4, rows, width), F32)],
        scalars=1,
    )
    out_gain = lax.dynamic_slice(out_gain, (0, here * each), (2, each))
    return (
        edge_grad[None],
        node_grad[None],
        out_edge_in,
        out_edge_out,
        out_gain[0],
        out_node_in,
        out_node_out,
        out_gain[1],
    )


def solution(mesh):
    placed = (
        P("group", "patch", None),
        P("group", "patch", None),
        P("group", "patch", None),
        P("group", "patch", None),
        P(),
        P(),
        P(),
        P(),
        P(),
        P(),
        P("patch", None),
        P("patch", None),
        P("patch"),
        P("patch", None),
    )
    return jax.shard_map(
        local,
        mesh=mesh,
        in_specs=placed,
        out_specs=(
            P("group", "patch", None),
            P("group", "patch", None),
            P("patch", None),
            P("patch", None),
            P("patch"),
            P("patch", None),
            P("patch", None),
            P("patch"),
        ),
        check_vma=False,
    )
```

time: 148 us -> 160 us (1.081)
  Pallas kernels: 47.1 us -> 77.9 us
  waiting for transfers between devices: 34.2 us -> 22.2 us
  local copies, waits for them, and re-layouts: 18.1 us -> 10.2 us
    pallas_call x11 -> x15, Pallas kernels: 47.1 us -> 77.9 us  [the longest x14 77.1 us: call(): pl.pallas_call(body, out_shape=shapes[0] if single else shapes, in_specs=...]
    ppermute x9 -> x3, waiting for transfers between devices: 20.8 us -> 0.01 us  [to_member(): lax.ppermute(x, 'group', [(g, (g + shift) % members) for g in range(membe...]
    ppermute x9 -> x3, starting transfers between devices: 14.2 us -> 4.52 us  [to_member(): lax.ppermute(x, 'group', [(g, (g + shift) % members) for g in range(membe...]
    unnamed x54 -> x32, local copies, waits for them, and re-layouts: 14.8 us -> 5.56 us
    ppermute x1 -> x7, starting transfers between devices: 0.15 us -> 8.43 us  [the longest x6 8.42 us: to_column(): lax.ppermute(x, 'patch', [(i, (i + shift * column) % patches) for i in ra...]
    all_to_all x1, waiting for transfers between devices: 0.01 us -> 6.01 us  [local(): lax.all_to_all(outward, 'patch', split_axis=0, concat_axis=0, tiled=True)]
    ppermute x1 -> x7, waiting for transfers between devices: 0.01 us -> 3.93 us  [the longest x6 3.93 us: to_column(): lax.ppermute(x, 'patch', [(i, (i + shift * column) % patches) for i in ra...]
    all_to_all x1 -> x2, starting transfers between devices: 9.92 us -> 13.6 us  [along_depth(): lax.all_to_all(x.reshape(depth, rows, width), 'patch', 0, 0, axis_index_g...]
  transfers between devices with their start and end apart: 14 -> 15, of which waited for: 7 -> 3; matrix products, arithmetic and copies ran while one was open for 0% -> 0% of each run, Pallas kernels for 7% -> 31%
where the time goes in v1:
time: 160 us; the launch traced here: 157 us
  Pallas kernels  77.9 us (49%)
  starting transfers between devices  44.7 us (28%)
  waiting for transfers between devices  22.2 us (14%)
  local copies, waits for them, and re-layouts  10.2 us (6%)
  between operations  1.62 us (1%)
    pallas_call x14, Pallas kernels, call(): pl.pallas_call(body, out_shape=shapes[0] if single else shapes, in_specs=...  77.1 us
    all_to_all x2, starting transfers between devices, along_depth(): lax.all_to_all(x.reshape(depth, rows, width), 'patch', 0, 0, axis_index_g...  13.6 us
    all_to_all x2, waiting for transfers between devices, along_depth(): lax.all_to_all(x.reshape(depth, rows, width), 'patch', 0, 0, axis_index_g...  12.2 us
    all_to_all x1, starting transfers between devices, local(): lax.all_to_all(outgoing, 'patch', split_axis=0, concat_axis=0, tiled=True)  12.1 us
    ppermute x6, starting transfers between devices, to_column(): lax.ppermute(x, 'patch', [(i, (i + shift * column) % patches) for i in ra...  8.42 us
    all_to_all x1, waiting for transfers between devices, local(): lax.all_to_all(outward, 'patch', split_axis=0, concat_axis=0, tiled=True)  6.01 us
    all_to_all x1, starting transfers between devices, local(): lax.all_to_all(outward, 'patch', split_axis=0, concat_axis=0, tiled=True)  5.78 us
    unnamed x32, local copies, waits for them, and re-layouts  5.56 us
  transfers between devices with their start and end apart: 15, of which 3 were waited for; matrix products, arithmetic and copies ran while one was open for 0% of the time, Pallas kernels for 31%

profile of v1, /device:TPU:8, one launch (start us, length us, event | category | flops | bytes accessed | tf_op | source)
XLA Modules:
  0.0 157.3 jit_solution(1610243841286799102)
XLA Ops:
  0.6 3.1 %shard_map.197 = bf16[256,512]{1,0:T(8,128)(2,1)} custom-call(s32[1,256]{1,0:T(1,128)} %refs_0_.7, bf16[1024,512]{1,0:T(8,128)(2,1)} %bitcast.18), custom_call_target="tpu_custom_call" | custom-call | flops 268435456 | bytes 263168 | tf_op jit(solution)/shard_map/pallas_call | solution.py:556
  3.7 1.7 %all_to_all.20 = bf16[64,4,512]{2,1,0:T(4,128)(2,1)} reshape(bf16[256,512]{1,0:T(8,128)(2,1)} %shard_map.197) | data formatting | bytes 524288 | tf_op jit(solution)/shard_map/all_to_all | solution.py:639
  5.5 12.1 %all-to-all-start = ((bf16[64,4,512]{2,1,0:T(4,128)(2,1)}), bf16[64,4,512]{2,1,0:T(4,128)(2,1)S(1)}, u32[]{:S(2)}, u32[]{:S(2)}) async-start(bf16[64,4,512]{2,1,0:T(4,128)(2,1)} %all_to_all.20), calls=%async_computation | async-start | bytes 524288 | tf_op jit(solution)/shard_map/all_to_all | solution.py:639
  18.9 11.2 %shard_map.198 = (bf16[1024,1024]{1,0:T(8,128)(2,1)}, bf16[1280,1024]{1,0:T(8,128)(2,1)}, bf16[512,1024]{1,0:T(8,128)(2,1)}, bf16[512,1024]{1,0:T(8,128)(2,1)}, ...) custom-call(s32[8,128]{1,0:T(8,128)} %refs_2_.4, s32[8,128]{1,0:T(8,128)} %refs_1_.2, bf16[1024,512]{1,0:T(8,128)(2,1)} %bitcast.19, ...), custom_call_target="tpu_custom_call" | custom-call | flops 3758096384 | bytes 11018240 | tf_op jit(solution)/shard_map/pallas_call | solution.py:556
  30.1 0.8 all_to_all.22.refs_5_.refs_11_
  30.9 19.9 %shard_map.199 = (f32[1,512]{1,0:T(1,128)}, bf16[1024,512]{1,0:T(8,128)(2,1)}, bf16[1024,512]{1,0:T(8,128)(2,1)}, f32[1024,128]{1,0:T(8,128)}, bf16[1024,512]{1,...) custom-call(s32[3]{0:T(128)} %pad_add_fusion.refs_0_, ...), custom_call_target="tpu_custom_call" | custom-call | flops 7516192768 | bytes 8398864 | tf_op jit(solution)/shard_map/pallas_call | solution.py:556
  51.0 8.5 %shard_map.200 = (f32[1,512]{1,0:T(1,128)}, f32[8,128]{1,0:T(8,128)}, bf16[1024,512]{1,0:T(8,128)(2,1)}, bf16[1024,512]{1,0:T(8,128)(2,1)}) custom-call(s32[1]{0:T(128)S(6)} %copy.24.refs_1_.refs_0_, f32[1,512]{1,0:T(1,128)} %bitcast.22, bf16[512,512]{1,0:T(8,128)(2,1)} %refs_2_.5, bf16[1024,512]{1,0:T(8,128)(2,1)} %get-tuple-element.57.refs_3_, ...), custom_call_target="tpu_custom_call" | custom-call | flops 1610612736 | bytes 2105348 | tf_op jit(solution)/shard_map/pallas_call | solution.py:556
  60.2 3.3 %shard_map.201 = (f32[8,128]{1,0:T(8,128)S(1)}, bf16[192,512]{1,0:T(8,128)(2,1)S(1)}, bf16[192,512]{1,0:T(8,128)(2,1)S(1)}, bf16[192,512]{1,0:T(8,128)(2,1)S(1)}, bf16[192,512]{1,0:T(8,128)(2,1)S(1)}) custom-call(f32[8,128]{1,0:T(8,128)S(1)} %copy-done.13, bf16[4,192,512]{2,1,0:T(8,128)(2,1)S(1)} %collective-permute-done.refs_1_, ...), custom_call_target="tpu_custom_call" | custom-call | bytes 794624 | tf_op jit(solution)/shard_map/pallas_call | solution.py:556
  63.5 1.7 %collective-permute-start.1 = (bf16[192,512]{1,0:T(8,128)(2,1)S(1)}, bf16[192,512]{1,0:T(8,128)(2,1)S(1)}, u32[]{:S(2)}, u32[]{:S(2)}) collective-permute-start(bf16[192,512]{1,0:T(8,128)(2,1)S(1)} %get-tuple-element.66), channel_id=1, source_target_pairs={{0,16},{1,17},{2,18},{3,19},{4,20},{5,21},{6,22},{7,23},{8,24},{9,... | collective-permute-start | bytes 589832 | tf_op jit(solution)/shard_map/ppermute | solution.py:619
  65.2 0.8 collective-permute-start.2
  66.0 2.5 %collective-permute-start.3 = (bf16[192,512]{1,0:T(8,128)(2,1)S(1)}, bf16[192,512]{1,0:T(8,128)(2,1)S(1)}, u32[]{:S(2)}, u32[]{:S(2)}) collective-permute-start(bf16[192,512]{1,0:T(8,128)(2,1)S(1)} %get-tuple-element.68), channel_id=1, source_target_pairs={{0,48},{1,49},{2,50},{3,51},{4,52},{5,53},{6,54},{7,55},{8,56},{9,... | collective-permute-start | bytes 589832 | tf_op jit(solution)/shard_map/ppermute | solution.py:619
  68.5 12.4 %shard_map.202 = (f32[8,128]{1,0:T(8,128)}, bf16[1280,512]{1,0:T(8,128)(2,1)}, bf16[1024,512]{1,0:T(8,128)(2,1)}, bf16[4,272,512]{2,1,0:T(8,128)(2,1)}, bf16[4,272,512]{2,1,0:T(8,128)(2,1)}) custom-call(s32[3]{0:T(128)} %pad_add_fusion.refs_0_, f32[1,512]{1,0:T(1,128)} %get-tuple-element.69.refs_1_, f32[1,512]{1,0:T(1,128)} %get-tuple-element.70.refs_2_, ...), custom_call_target="tpu_custom_call" | custom-call | flops 4831838208 | bytes 4599820 | tf_op jit(solution)/shard_map/pallas_call | solution.py:556
  81.0 0.8 copy-done.11
  81.7 0.8 shard_map.203
  83.9 6.7 %all-to-all-start.2 = ((bf16[8,24,512]{2,1,0:T(8,128)(2,1)}), bf16[8,24,512]{2,1,0:T(8,128)(2,1)S(1)}, u32[]{:S(2)}, u32[]{:S(2)}) async-start(bf16[8,24,512]{2,1,0:T(8,128)(2,1)} %get-tuple-element.93), calls=%async_computation.2 | async-start | bytes 393216 | tf_op jit(solution)/shard_map/all_to_all | solution.py:622
  90.6 1.4 shard_map.205
  92.6 3.4 %collective-permute-start.6 = (bf16[272,512]{1,0:T(8,128)(2,1)}, bf16[272,512]{1,0:T(8,128)(2,1)S(1)}, u32[]{:S(2)}, u32[]{:S(2)}) collective-permute-start(bf16[272,512]{1,0:T(8,128)(2,1)} %get-tuple-element.88), channel_id=1, source_target_pairs={{0,32},{1,33},{2,34},{3,35},{4,36},{5,37},{6,38},{7,39},{8,40},{9,... | collective-permute-start | bytes 835592 | tf_op jit(solution)/shard_map/ppermute | solution.py:619
  96.0 9.2 %shard_map.206 = (f32[8,128]{1,0:T(8,128)}, f32[1024,512]{1,0:T(8,128)}, bf16[1024,512]{1,0:T(8,128)(2,1)}) custom-call(s32[1]{0:T(128)S(6)} %copy.24.refs_1_.refs_0_, f32[8,128]{1,0:T(8,128)} %copy-done.6, bf16[1536,512]{1,0:T(8,128)(2,1)} %refs_2_.7, f32[1024,512]{1,0:T(8,128)} %get-tuple-element.82.refs_3_, ...), custom_call_target="tpu_custom_call" | custom-call | flops 1610612736 | bytes 3153924 | tf_op jit(solution)/shard_map/pallas_call | solution.py:556
  105.3 3.9 %collective-permute-done.7.refs_3_ = bf16[272,512]{1,0:T(8,128)(2,1)} collective-permute-done((bf16[272,512]{1,0:T(8,128)(2,1)}, bf16[272,512]{1,0:T(8,128)(2,1)}, u32[]{:S(2)}, u32[]{:S(2)}) %collective-permute-start.7) | collective-permute-done | bytes 278560 | tf_op jit(solution)/shard_map/ppermute | solution.py:619
  109.9 1.8 %shard_map.207 = (bf16[8,40,512]{2,1,0:T(8,128)(2,1)}, f32[8,128]{1,0:T(8,128)S(1)}) custom-call(bf16[272,512]{1,0:T(8,128)(2,1)S(1)} %get-tuple-element.86.refs_0_, bf16[272,512]{1,0:T(8,128)(2,1)S(1)} %collective-permute-done.5.refs_1_, bf16[272,512]{1,0:T(8,128)(2,1)S(1)} %collective-permute-done.6.refs_2_, ...), custom_call_target="tpu_custom_call" | custom-call | bytes 1449984 | tf_op jit(solution)/shard_map/pallas_call | solution.py:556
  113.0 6.9 %all-to-all-start.3 = ((bf16[8,40,512]{2,1,0:T(8,128)(2,1)}), bf16[8,40,512]{2,1,0:T(8,128)(2,1)S(1)}, u32[]{:S(2)}, u32[]{:S(2)}) async-start(bf16[8,40,512]{2,1,0:T(8,128)(2,1)} %get-tuple-element.94), calls=%async_computation.3 | async-start | bytes 655360 | tf_op jit(solution)/shard_map/all_to_all | solution.py:622
  120.4 0.8 all_to_all.23
  121.2 12.2 %all-to-all-done.3.refs_1_ = bf16[8,40,512]{2,1,0:T(8,128)(2,1)S(1)} async-done(((bf16[8,40,512]{2,1,0:T(8,128)(2,1)}), bf16[8,40,512]{2,1,0:T(8,128)(2,1)S(1)}, u32[]{:S(2)}, u32[]{:S(2)}) %all-to-all-start.3) | async-done | bytes 327712 | tf_op jit(solution)/shard_map/all_to_all | solution.py:622
  133.4 5.8 %all-to-all-start.1 = ((bf16[64,4,512]{2,1,0:T(4,128)(2,1)}), bf16[64,4,512]{2,1,0:T(4,128)(2,1)S(1)}, u32[]{:S(2)}, u32[]{:S(2)}) async-start(bf16[64,4,512]{2,1,0:T(4,128)(2,1)} %all_to_all.23), calls=%async_computation.1 | async-start | bytes 524288 | tf_op jit(solution)/shard_map/all_to_all | solution.py:776
  139.2 0.9 copy-done.5
  140.2 2.9 %collective-permute-start.10 = (bf16[64,512]{1,0:T(8,128)(2,1)S(1)}, bf16[64,512]{1,0:T(8,128)(2,1)S(1)}, u32[]{:S(2)}, u32[]{:S(2)}) collective-permute-start(bf16[64,512]{1,0:T(8,128)(2,1)S(1)} %shard_map.210.refs_1_), channel_id=1, source_target_pairs={{0,192},{64,0},{128,64},{192,128},{1,193},{65,1},{129,65},{193,129... | collective-permute-start | bytes 196616 | tf_op jit(solution)/shard_map/ppermute | solution.py:616
  143.0 0.8 collective-permute-start.9
  143.8 0.9 collective-permute-start.8
  144.7 6.0 %all-to-all-done.1 = bf16[64,4,512]{2,1,0:T(4,128)(2,1)S(1)} async-done(((bf16[64,4,512]{2,1,0:T(4,128)(2,1)}), bf16[64,4,512]{2,1,0:T(4,128)(2,1)S(1)}, u32[]{:S(2)}, u32[]{:S(2)}) %all-to-all-start.1) | async-done | bytes 262176 | tf_op jit(solution)/shard_map/all_to_all | solution.py:776
  150.7 0.8 all_to_all.25.refs_2_
  151.5 3.9 %shard_map.209 = bf16[1024,512]{1,0:T(8,128)(2,1)} custom-call(s32[1,256]{1,0:T(1,128)} %refs_0_.7, f32[8,128]{1,0:T(8,128)} %copy-done.10, bf16[256,512]{1,0:T(8,128)(2,1)} %all_to_all.25.refs_2_, f32[1024,512]{1,0:T(8,128)} %get-tuple-element.92.refs_3_), custom_call_target="tpu_custom_call" | custom-call | flops 268435456 | bytes 1053696 | tf_op jit(solution)/shard_map/pallas_call | solution.py:556
  155.4 1.3 shard_map.211
  (52 shorter events, 6.7 us)
Async XLA Ops:
  5.5 24.6 %all-to-all-start = ((bf16[64,4,512]{2,1,0:T(4,128)(2,1)}), bf16[64,4,512]{2,1,0:T(4,128)(2,1)S(1)}, u32[]{:S(2)}, u32[]{:S(2)}) async-start(bf16[64,4,512]{2,1,0:T(4,128)(2,1)} %all_to_all.20), calls=%async_computation | async-start | bytes 524288 | tf_op jit(solution)/shard_map/all_to_all | solution.py:639
  50.7 8.8 %collective-permute-start = (bf16[4,192,512]{2,1,0:T(8,128)(2,1)}, bf16[4,192,512]{2,1,0:T(8,128)(2,1)S(1)}, u32[]{:S(2)}, u32[]{:S(2)}) collective-permute-start(bf16[4,192,512]{2,1,0:T(8,128)(2,1)} %get-tuple-element.63), channel_id=1, source_target_pairs={{0,1},{1,0},{2,3},{3,2},{4,5},{5,4},{6,7},{7,6},{8,9},{9,8},{10,11... | collective-permute-start | bytes 2359304 | tf_op jit(solution)/shard_map/ppermute | solution.py:711
  51.0 8.5 %copy-start.3 = (bf16[4,192,512]{2,1,0:T(8,128)(2,1)S(1)}, bf16[4,192,512]{2,1,0:T(8,128)(2,1)}, u32[]{:S(2)}) copy-start(bf16[4,192,512]{2,1,0:T(8,128)(2,1)} %get-tuple-element.64.refs_2_) | copy-start | bytes 2359300
  59.5 0.7 copy-start.13
  63.5 5.0 %copy-start.15 = (f32[8,128]{1,0:T(8,128)}, f32[8,128]{1,0:T(8,128)S(1)}, u32[]{:S(2)}) copy-start(f32[8,128]{1,0:T(8,128)S(1)} %get-tuple-element.71.refs_3_) | copy-start | bytes 12292
  63.5 17.4 %collective-permute-start.1 = (bf16[192,512]{1,0:T(8,128)(2,1)S(1)}, bf16[192,512]{1,0:T(8,128)(2,1)S(1)}, u32[]{:S(2)}, u32[]{:S(2)}) collective-permute-start(bf16[192,512]{1,0:T(8,128)(2,1)S(1)} %get-tuple-element.66), channel_id=1, source_target_pairs={{0,16},{1,17},{2,18},{3,19},{4,20},{5,21},{6,22},{7,23},{8,24},{9,... | collective-permute-start | bytes 589832 | tf_op jit(solution)/shard_map/ppermute | solution.py:619
  65.2 15.8 %collective-permute-start.2 = (bf16[192,512]{1,0:T(8,128)(2,1)S(1)}, bf16[192,512]{1,0:T(8,128)(2,1)S(1)}, u32[]{:S(2)}, u32[]{:S(2)}) collective-permute-start(bf16[192,512]{1,0:T(8,128)(2,1)S(1)} %get-tuple-element.67), channel_id=1, source_target_pairs={{0,32},{1,33},{2,34},{3,35},{4,36},{5,37},{6,38},{7,39},{8,40},{9,... | collective-permute-start | bytes 589832 | tf_op jit(solution)/shard_map/ppermute | solution.py:619
  66.0 14.9 %collective-permute-start.3 = (bf16[192,512]{1,0:T(8,128)(2,1)S(1)}, bf16[192,512]{1,0:T(8,128)(2,1)S(1)}, u32[]{:S(2)}, u32[]{:S(2)}) collective-permute-start(bf16[192,512]{1,0:T(8,128)(2,1)S(1)} %get-tuple-element.68), channel_id=1, source_target_pairs={{0,48},{1,49},{2,50},{3,51},{4,52},{5,53},{6,54},{7,55},{8,56},{9,... | collective-permute-start | bytes 589832 | tf_op jit(solution)/shard_map/ppermute | solution.py:619
  80.9 9.7 %copy-start.2 = (bf16[4,272,512]{2,1,0:T(8,128)(2,1)S(1)}, bf16[4,272,512]{2,1,0:T(8,128)(2,1)}, u32[]{:S(2)}) copy-start(bf16[4,272,512]{2,1,0:T(8,128)(2,1)} %get-tuple-element.80.refs_2_) | copy-start | bytes 3342340
  81.0 0.8 copy-start.11
  82.5 0.6 copy-start.8
  83.1 7.5 %copy-start.9 = (f32[8,128]{1,0:T(8,128)S(1)}, f32[8,128]{1,0:T(8,128)}, u32[]{:S(2)}) copy-start(f32[8,128]{1,0:T(8,128)} %copy-done.8) | copy-start | bytes 12292
  83.9 6.7 %collective-permute-start.4 = (bf16[4,272,512]{2,1,0:T(8,128)(2,1)}, bf16[4,272,512]{2,1,0:T(8,128)(2,1)S(1)}, u32[]{:S(2)}, u32[]{:S(2)}) collective-permute-start(bf16[4,272,512]{2,1,0:T(8,128)(2,1)} %shard_map.204), channel_id=1, source_target_pairs={{0,1},{1,0},{2,3},{3,2},{4,5},{5,4},{6,7},{7,6},{8,9},{9,8},{10,11... | collective-permute-start | bytes 3342344 | tf_op jit(solution)/shard_map/ppermute | solution.py:767
  83.9 28.4 %all-to-all-start.2 = ((bf16[8,24,512]{2,1,0:T(8,128)(2,1)}), bf16[8,24,512]{2,1,0:T(8,128)(2,1)S(1)}, u32[]{:S(2)}, u32[]{:S(2)}) async-start(bf16[8,24,512]{2,1,0:T(8,128)(2,1)} %get-tuple-element.93), calls=%async_computation.2 | async-start | bytes 393216 | tf_op jit(solution)/shard_map/all_to_all | solution.py:622
  92.0 0.6 copy-start.6
  92.6 12.7 %collective-permute-start.5 = (bf16[272,512]{1,0:T(8,128)(2,1)}, bf16[272,512]{1,0:T(8,128)(2,1)S(1)}, u32[]{:S(2)}, u32[]{:S(2)}) collective-permute-start(bf16[272,512]{1,0:T(8,128)(2,1)} %get-tuple-element.87), channel_id=1, source_target_pairs={{0,16},{1,17},{2,18},{3,19},{4,20},{5,21},{6,22},{7,23},{8,24},{9,... | collective-permute-start | bytes 835592 | tf_op jit(solution)/shard_map/ppermute | solution.py:619
  92.6 12.7 %collective-permute-start.6 = (bf16[272,512]{1,0:T(8,128)(2,1)}, bf16[272,512]{1,0:T(8,128)(2,1)S(1)}, u32[]{:S(2)}, u32[]{:S(2)}) collective-permute-start(bf16[272,512]{1,0:T(8,128)(2,1)} %get-tuple-element.88), channel_id=1, source_target_pairs={{0,32},{1,33},{2,34},{3,35},{4,36},{5,37},{6,38},{7,39},{8,40},{9,... | collective-permute-start | bytes 835592 | tf_op jit(solution)/shard_map/ppermute | solution.py:619
  96.0 13.2 %collective-permute-start.7 = (bf16[272,512]{1,0:T(8,128)(2,1)}, bf16[272,512]{1,0:T(8,128)(2,1)}, u32[]{:S(2)}, u32[]{:S(2)}) collective-permute-start(bf16[272,512]{1,0:T(8,128)(2,1)} %get-tuple-element.89), channel_id=1, source_target_pairs={{0,48},{1,49},{2,50},{3,51},{4,52},{5,53},{6,54},{7,55},{8,56},{9,... | collective-permute-start | bytes 835592 | tf_op jit(solution)/shard_map/ppermute | solution.py:619
  96.0 23.9 %copy-start.1 = (bf16[1280,512]{1,0:T(8,128)(2,1)S(1)}, bf16[1280,512]{1,0:T(8,128)(2,1)}, u32[]{:S(2)}) copy-start(bf16[1280,512]{1,0:T(8,128)(2,1)} %get-tuple-element.83.refs_4_.refs_1_) | copy-start | bytes 3932164
  96.0 23.9 %copy-start.7 = (f32[8,128]{1,0:T(8,128)S(1)}, f32[8,128]{1,0:T(8,128)}, u32[]{:S(2)}) copy-start(f32[8,128]{1,0:T(8,128)} %copy-done.6) | copy-start | bytes 12292
  105.3 14.7 %copy-start = (bf16[1536,512]{1,0:T(8,128)(2,1)S(1)}, bf16[1536,512]{1,0:T(8,128)(2,1)}, u32[]{:S(2)}) copy-start(bf16[1536,512]{1,0:T(8,128)(2,1)} %refs_2_.7) | copy-start | bytes 4718596
  109.2 0.7 copy-start.12
  111.7 0.6 copy-start.10
  112.3 0.7 copy-start.4
  113.0 20.4 %all-to-all-start.3 = ((bf16[8,40,512]{2,1,0:T(8,128)(2,1)}), bf16[8,40,512]{2,1,0:T(8,128)(2,1)S(1)}, u32[]{:S(2)}, u32[]{:S(2)}) async-start(bf16[8,40,512]{2,1,0:T(8,128)(2,1)} %get-tuple-element.94), calls=%async_computation.3 | async-start | bytes 655360 | tf_op jit(solution)/shard_map/all_to_all | solution.py:622
  133.4 17.3 %all-to-all-start.1 = ((bf16[64,4,512]{2,1,0:T(4,128)(2,1)}), bf16[64,4,512]{2,1,0:T(4,128)(2,1)S(1)}, u32[]{:S(2)}, u32[]{:S(2)}) async-start(bf16[64,4,512]{2,1,0:T(4,128)(2,1)} %all_to_all.23), calls=%async_computation.1 | async-start | bytes 524288 | tf_op jit(solution)/shard_map/all_to_all | solution.py:776
  139.2 0.9 copy-start.5
  140.2 15.2 %copy-start.14 = (s32[3]{0:T(128)S(1)}, s32[3]{0:T(128)}, u32[]{:S(2)}) copy-start(s32[3]{0:T(128)} %pad_add_fusion.refs_0_) | copy-start | bytes 40
  140.2 15.2 %collective-permute-start.10 = (bf16[64,512]{1,0:T(8,128)(2,1)S(1)}, bf16[64,512]{1,0:T(8,128)(2,1)S(1)}, u32[]{:S(2)}, u32[]{:S(2)}) collective-permute-start(bf16[64,512]{1,0:T(8,128)(2,1)S(1)} %shard_map.210.refs_1_), channel_id=1, source_target_pairs={{0,192},{64,0},{128,64},{192,128},{1,193},{65,1},{129,65},{193,129... | collective-permute-start | bytes 196616 | tf_op jit(solution)/shard_map/ppermute | solution.py:616
  143.0 12.4 %collective-permute-start.9 = (bf16[64,512]{1,0:T(8,128)(2,1)S(1)}, bf16[64,512]{1,0:T(8,128)(2,1)S(1)}, u32[]{:S(2)}, u32[]{:S(2)}) collective-permute-start(bf16[64,512]{1,0:T(8,128)(2,1)S(1)} %shard_map.210.refs_1_), channel_id=1, source_target_pairs={{0,128},{64,192},{128,0},{192,64},{1,129},{65,193},{129,1},{193,65... | collective-permute-start | bytes 196616 | tf_op jit(solution)/shard_map/ppermute | solution.py:616
  143.8 11.6 %collective-permute-start.8 = (bf16[64,512]{1,0:T(8,128)(2,1)S(1)}, bf16[64,512]{1,0:T(8,128)(2,1)S(1)}, u32[]{:S(2)}, u32[]{:S(2)}) collective-permute-start(bf16[64,512]{1,0:T(8,128)(2,1)S(1)} %shard_map.210.refs_1_), channel_id=1, source_target_pairs={{0,64},{64,128},{128,192},{192,0},{1,65},{65,129},{129,193},{193,1... | collective-permute-start | bytes 196616 | tf_op jit(solution)/shard_map/ppermute | solution.py:616

commit v2 on v1

v2 whole, which is shorter than its diff:
```python
import functools

import jax
import jax.numpy as jnp
from jax import lax
from jax.experimental import pallas as pl
from jax.experimental.pallas import tpu as pltpu
from jax.sharding import PartitionSpec as P

epsilon = 1e-05
BF = jnp.bfloat16
F32 = jnp.float32
LANE = 128
ROWS = 256
FULL = 60 * 2**20


def dot(a, b):
    return lax.dot_general(a, b, (((1,), (0,)), ((), ())), preferred_element_type=F32)


def dot_rt(a, b):
    return lax.dot_general(a, b, (((1,), (1,)), ((), ())), preferred_element_type=F32)


def dot_lt(a, b):
    return lax.dot_general(a, b, (((0,), (0,)), ((), ())), preferred_element_type=F32)


def iota(shape, dim):
    return lax.broadcasted_iota(jnp.int32, shape, dim)


def one_hot(mask):
    return jnp.where(mask, 1.0, 0.0).astype(BF)


def columns_of(index_ref, out_ref):
    tiles = index_ref.shape[0]
    full = jnp.concatenate(
        [index_ref[...], jnp.zeros((LANE - tiles, LANE), jnp.int32)], axis=0
    )
    turned = full.T
    for t in range(tiles):
        out_ref[t * LANE : (t + 1) * LANE, :] = jnp.broadcast_to(
            turned[:, t : t + 1], (LANE, LANE)
        )


def pick_rows(cols_ref, start, count, first, width):
    column = cols_ref[pl.ds(start, count), 0:1]
    return one_hot(column == iota((count, width), 1) + first)


def spread_rows(index_ref, start, count):
    tiles = index_ref.shape[0]
    base = iota((count, LANE), 0) + start
    return jnp.concatenate([one_hot(index_ref[t : t + 1, :] == base) for t in range(tiles)], axis=1)


def sigmoid(v):
    return 0.5 * jnp.tanh(0.5 * v) + 0.5


def live_rows(count_ref, start, count):
    return (iota((count, 1), 0) + start < count_ref[0] * LANE).astype(F32)


def normalize(values):
    centred = values - jnp.mean(values, axis=1, keepdims=True)
    inverse = lax.rsqrt(jnp.mean(centred * centred, axis=1, keepdims=True) + epsilon)
    return centred * inverse, inverse


def normalize_back(upstream, normed, inverse):
    return inverse * (
        upstream
        - jnp.mean(upstream, axis=1, keepdims=True)
        - normed * jnp.mean(upstream * normed, axis=1, keepdims=True)
    )


def loop(count, body):
    def step(i, carry):
        body(pl.multiple_of(i * ROWS, ROWS), i)
        return carry

    lax.fori_loop(0, count // ROWS, step, 0)


def outgoing_kernel(rows_ref, node_ref, out_ref):
    nodes, halo = node_ref.shape[0], rows_ref.shape[1]
    spread = one_hot(rows_ref[...] == iota((nodes, halo), 0))
    out_ref[...] = dot_lt(spread, node_ref[...]).astype(BF)


def own_kernel(
    send_ref,
    recv_ref,
    node,
    edge,
    w_edge,
    node_turned,
    edge_turned,
    begun,
    send_cols,
    recv_cols,
):
    nodes, width = node.shape
    columns_of(send_ref, send_cols)
    columns_of(recv_ref, recv_cols)
    node_ref, edge_ref, w_ref = node.ready(), edge.ready(), w_edge.ready()

    def body(start, i):
        here = pl.ds(start, ROWS)
        from_send = dot(pick_rows(send_cols, start, ROWS, 0, nodes), node_ref[...]).astype(BF)
        from_recv = dot(pick_rows(recv_cols, start, ROWS, 0, nodes), node_ref[...]).astype(BF)
        begun.buffer[here, :] = (
            dot(edge_ref[here, :], w_ref[0:width, :])
            + dot(from_send, w_ref[width : 2 * width, :])
            + dot(from_recv, w_ref[2 * width : 3 * width, :])
        )
        begun.send(i)

    loop(edge_ref.shape[0], body)
    for source, out in ((node_ref, node_turned), (edge_ref, edge_turned)):
        for i in range(0, source.shape[0], ROWS):
            out.buffer[:, i : i + ROWS] = source[i : i + ROWS, :].T
        out.send(0)


def deal(place_ref, depth, pieces, first, send, keep):
    core, column = place_ref[0], place_ref[1]
    each = sum(rows for _, rows in pieces)
    batch = 1 if each % 16 == 0 else 2
    for which, out in ((1 - core, send), (core, keep)):

        def step(s, carry):
            for i in range(0, depth, batch):
                found = []
                for b in range(batch):
                    patch = (((column + s) % 4) * depth + i + b) * 2 + which
                    for ref, rows in pieces:
                        found.append(ref[pl.ds(pl.multiple_of(patch * rows, 8), rows), :])
                at = first + i * each
                out.buffer[s, at : at + batch * each, :] = jnp.concatenate(found, axis=0).astype(BF)
            return carry

        lax.fori_loop(0, 4, step, 0)


def main_kernel(
    patches,
    place_ref,
    count_ref,
    send_ref,
    recv_ref,
    gain_edge_ref,
    gain_node_ref,
    incoming,
    w_edge_send,
    begun,
    w_edge_out,
    node,
    w_node,
    w_node_out,
    node_cot,
    node_turned,
    edge_cot,
    edge_turned,
    node_acc,
    first_out,
    from_send,
    from_recv,
    outward,
    piece_send,
    piece_keep,
    send_cols,
    recv_cols,
    hidden_ref,
    slope_ref,
    normed_ref,
    inverse_ref,
    message,
    gathered,
    node_hidden,
    grad_second,
    grad_first,
    back_ref,
    gains,
    sum_in,
    sum_out,
    edge_sum_in,
    edge_sum_out,
):
    nodes, width = node.shape
    edges = begun.shape[0]
    halo = incoming.shape[0]
    columns_of(send_ref, send_cols)
    columns_of(recv_ref, recv_cols)
    halo_ref, w_send_ref, w_edge_out_ref = incoming.ready(), w_edge_send.ready(), None
    w_edge_out_ref = w_edge_out.ready()

    def edge_body(start, i):
        here = pl.ds(start, ROWS)
        latent = dot(pick_rows(send_cols, start, ROWS, nodes, halo), halo_ref[...])
        first = begun.part(i)[here, :] + dot(latent.astype(BF), w_send_ref[...])
        squash = sigmoid(first)
        hidden = (first * squash).astype(BF)
        hidden_ref[here, :] = hidden
        slope_ref[here, :] = (squash * (1.0 + first * (1.0 - squash))).astype(BF)
        normed, inverse = normalize(dot(hidden, w_edge_out_ref[...]))
        normed_ref[here, :] = normed.astype(BF)
        inverse_ref[here, :] = jnp.broadcast_to(inverse, (ROWS, LANE))
        live = live_rows(count_ref, start, ROWS)
        message[here, :] = (live * (gain_edge_ref[...] * normed)).astype(BF)

    loop(edges, edge_body)
    gains[...] = jnp.zeros_like(gains)
    node_ref, w_node_ref, w_node_out_ref = node.ready(), w_node.ready(), w_node_out.ready()

    def node_body(start, i):
        here = pl.ds(start, ROWS)
        taken = dot(spread_rows(recv_ref, start, ROWS), message[...]).astype(BF)
        gathered[here, :] = taken
        first = dot(node_ref[here, :], w_node_ref[0:width, :]) + dot(
            taken, w_node_ref[width : 2 * width, :]
        )
        squash = sigmoid(first)
        hidden = (first * squash).astype(BF)
        node_hidden[here, :] = hidden
        slope = squash * (1.0 + first * (1.0 - squash))
        normed, inverse = normalize(dot(hidden, w_node_out_ref[...]))
        upstream = node_cot.part(i)[here, :].astype(F32)
        gains[1:2, :] += jnp.sum(upstream * normed, axis=0, keepdims=True)
        second = normalize_back(upstream * gain_node_ref[...], normed, inverse).astype(BF)
        grad_second[here, :] = second
        grad = (dot_rt(second, w_node_out_ref[...]) * slope).astype(BF)
        grad_first[here, :] = grad
        node_acc.buffer[here, :] = (upstream + dot_rt(grad, w_node_ref[0:width, :])).astype(BF)
        back_ref[here, :] = dot_rt(grad, w_node_ref[width : 2 * width, :]).astype(BF)
        node_acc.send(i)

    loop(nodes, node_body)
    node_turned_ref = node_turned.ready()
    sum_out[...] = dot_lt(node_hidden[...], grad_second[...])
    sum_in[0:width, :] = dot(node_turned_ref[...], grad_first[...])
    sum_in[width : 2 * width, :] = dot_lt(gathered[...], grad_first[...])

    def back_body(start, i):
        here = pl.ds(start, ROWS)
        live = live_rows(count_ref, start, ROWS)
        taken = dot(pick_rows(recv_cols, start, ROWS, 0, nodes), back_ref[...])
        arrived = live * (edge_cot.part(i)[here, :].astype(F32) + taken)
        normed = normed_ref[here, :].astype(F32)
        gains[0:1, :] += jnp.sum(arrived * normed, axis=0, keepdims=True)
        second = normalize_back(
            arrived * gain_edge_ref[...], normed, inverse_ref[here, 0:1]
        ).astype(BF)
        grad_second[here, :] = second
        first_out.buffer[here, :] = (
            dot_rt(second, w_edge_out_ref[...]) * slope_ref[here, :].astype(F32)
        ).astype(BF)
        first_out.send(i)

    loop(edges, back_body)
    first_ref = first_out.buffer
    for out, index_ref in ((from_send, send_ref), (from_recv, recv_ref)):

        def body(start, i):
            out.buffer[pl.ds(start, ROWS), :] = dot(
                spread_rows(index_ref, start, ROWS), first_ref[...]
            ).astype(BF)
            out.send(i)

        loop(out.shape[0], body)
    sent, received = from_send.buffer, from_recv.buffer
    outward.buffer[...] = dot_rt(sent[nodes : nodes + halo, :], w_send_ref[...]).astype(BF)
    outward.send(0)
    edge_sum_out[...] = dot_lt(hidden_ref[...], grad_second[...])
    edge_sum_in[0:width, :] = dot(edge_turned.ready()[...], first_ref[...])
    edge_sum_in[width : 2 * width, :] = dot(node_turned_ref[...], sent[0:nodes, :]) + dot_lt(
        halo_ref[...], sent[nodes : nodes + halo, :]
    )
    edge_sum_in[2 * width : 3 * width, :] = dot(node_turned_ref[...], received[...])
    extra = jnp.concatenate([gains[...], jnp.zeros((8, width), F32)], axis=0).astype(BF)
    rows = piece_keep.shape[1]
    for out in (piece_send, piece_keep):
        for s in range(4):
            out.buffer[s, rows - 16 : rows, :] = extra
    depth = patches // 8
    each = width // patches
    pieces = ((sum_in, 2 * each), (sum_out, each))
    deal(place_ref, depth, pieces, 0, piece_send, piece_keep)
    pieces = ((edge_sum_in, 3 * each), (edge_sum_out, each))
    deal(place_ref, depth, pieces, depth * 3 * each, piece_send, piece_keep)
    for s in range(4):
        piece_send.send(s)
        piece_keep.send(s)


def edge_grad_kernel(count_ref, w_own, first, cot, edge_grad, token):
    token.buffer[...] = jnp.zeros(token.shape, F32)
    token.send(0)
    w_ref = w_own.ready()

    def edge_body(start, i):
        here = pl.ds(start, ROWS)
        live = live_rows(count_ref, start, ROWS)
        edge_grad.buffer[here, :] = (
            live * cot.part(i)[here, :].astype(F32) + dot_rt(first.part(i)[here, :], w_ref[...])
        ).astype(BF)
        edge_grad.send(i)

    loop(cot.shape[0], edge_body)


def node_grad_kernel(rows_ref, w_both, returned, acc, from_send, from_recv, out, token):
    token.buffer[...] = jnp.zeros(token.shape, F32)
    token.send(0)
    nodes, width = acc.shape
    halo = returned.shape[0]
    w_ref, returned_ref = w_both.ready(), returned.ready()

    def body(start, i):
        here = pl.ds(start, ROWS)
        spread = one_hot(rows_ref[...] == iota((ROWS, halo), 0) + start)
        out.buffer[here, :] = (
            acc.part(i)[here, :].astype(F32)
            + dot(spread, returned_ref[...])
            + dot_rt(from_send.part(i)[here, :], w_ref[0:width, :])
            + dot_rt(from_recv.part(i)[here, :], w_ref[width : 2 * width, :])
        ).astype(BF)
        out.send(i)

    loop(nodes, body)


def pair_kernel(keep_ref, got_ref, *outs):
    for s in range(4):
        outs[s][...] = (keep_ref[s].astype(F32) + got_ref[s].astype(F32)).astype(BF)


def four_kernel(counts, a, b, c, d, out_ref):
    total = a[...].astype(F32) + b[...].astype(F32) + c[...].astype(F32) + d[...].astype(F32)
    depth = out_ref.shape[0]
    last = total[depth * sum(counts) :][0:8]
    for z in range(depth):
        found, base = [], 0
        for rows in counts:
            found.append(total[base + z * rows : base + (z + 1) * rows])
            base += depth * rows
        out_ref[z] = jnp.concatenate(found + [last], axis=0).astype(BF)


def depth_kernel(got_ref, out_ref):
    total = got_ref[0].astype(F32)
    for i in range(1, got_ref.shape[0]):
        total = total + got_ref[i].astype(F32)
    out_ref[...] = total.astype(BF)


def finish_kernel(
    factor,
    place_ref,
    a,
    b,
    c,
    d,
    edge_in_ref,
    edge_out_ref,
    node_in_ref,
    node_out_ref,
    gain_ref,
    rows,
):
    member = place_ref[2]
    for s, ref in enumerate((a, b, c, d)):
        rows[(member - s + 4) % 4] = ref[...].astype(F32)
    total = ((rows[0] + rows[1]) + (rows[2] + rows[3])) * factor
    at = 0
    for out in (node_in_ref, node_out_ref, edge_in_ref, edge_out_ref, gain_ref):
        out[...] = total[at : at + out.shape[0], :]
        at += out.shape[0]


VM = pl.BlockSpec(memory_space=pltpu.VMEM)
SM = pl.BlockSpec(memory_space=pltpu.SMEM)

TOKEN = ((8, LANE), F32, 1)


class Moved:
    def __init__(self, far, buffer, semaphores, parts, first, outward):
        self.far, self.buffer, self.semaphores = far, buffer, semaphores
        self.parts, self.first, self.outward = parts, first, outward
        self.shape = buffer.shape
        self.step = buffer.shape[0] // parts

    def copy(self, i):
        near = self.buffer.at[pl.ds(i * self.step, self.step)]
        far = self.far.at[pl.ds(self.first + i * self.step, self.step)]
        ends = (near, far) if self.outward else (far, near)
        return pltpu.make_async_copy(*ends, self.semaphores.at[i])

    def send(self, i):
        self.copy(i).start()

    def part(self, i):
        self.copy(i).wait()
        return self.buffer

    def ready(self):
        for i in range(self.parts):
            self.copy(i).wait()
        return self.buffer


class Part:
    def __init__(self, array, parts=1, first=0, rows=None):
        self.array, self.parts, self.first = array, parts, first
        self.rows = array.shape[0] if rows is None else rows


def call(kernel, outs, ins, scratch=(), scalars=0, flops=0, fetch=(), store=(), limit=None, after=()):
    ins = list(ins)
    fetch = [f if isinstance(f, Part) else Part(f) for f in fetch]
    shapes = [jax.ShapeDtypeStruct(s, d) for s, d in list(outs) + [o[:2] for o in store]]
    single = len(shapes) == 1
    buffers = [((f.rows, *f.array.shape[1:]), f.array.dtype) for f in fetch]
    size = sum(int(a.size) * a.dtype.itemsize for a in ins + shapes)
    held = list(scratch) + buffers + [o[:2] for o in store]
    bytes_here = sum(
        functools.reduce(lambda x, y: x * y, s) * jnp.dtype(d).itemsize for s, d in held
    )
    many, kept, given = len(fetch), len(store), len(outs)

    def take(refs, count):
        return refs[:count], refs[count:]

    def body(*refs):
        args, refs = take(refs, len(ins))
        _, refs = take(refs, len(after))
        sources, refs = take(refs, many)
        results, refs = take(refs, given)
        targets, refs = take(refs, kept)
        own, refs = take(refs, len(scratch))
        slots, refs = take(refs, many)
        rooms, refs = take(refs, kept)
        marks, ends = take(refs, many)
        arriving = [
            Moved(src, slot, mark, f.parts, f.first, False)
            for src, f, slot, mark in zip(sources, fetch, slots, marks)
        ]
        for one in arriving:
            for i in range(one.parts):
                one.send(i)
        leaving = [
            Moved(t, room, end, o[2], 0, True)
            for t, room, end, o in zip(targets, rooms, ends, store)
        ]
        kernel(*args, *arriving, *results, *leaving, *own)
        for one in leaving:
            one.ready()

    far = pl.BlockSpec(memory_space=pltpu.HBM)
    out_specs = [VM] * given + [far] * kept
    return pl.pallas_call(
        body,
        out_shape=shapes[0] if single else shapes,
        in_specs=[SM] * scalars
        + [VM] * (len(ins) - scalars)
        + [pl.BlockSpec(memory_space=pl.ANY)] * len(after)
        + [far] * many,
        out_specs=out_specs[0] if single else out_specs,
        scratch_shapes=[pltpu.VMEM(s, d) for s, d in held]
        + [pltpu.SemaphoreType.DMA((f.parts,)) for f in fetch]
        + [pltpu.SemaphoreType.DMA((o[2],)) for o in store],
        compiler_params=pltpu.CompilerParams(
            vmem_limit_bytes=bytes_here + 4 * 2**20 if limit is None else limit
        ),
        cost_estimate=pl.CostEstimate(flops=flops, bytes_accessed=size, transcendentals=0),
    )(*ins, *after, *[f.array for f in fetch])


def local(
    node_tape,
    edge_tape,
    node_cot,
    edge_cot,
    w_edge_in,
    w_edge_out,
    gain_edge,
    w_node_in,
    w_node_out,
    gain_node,
    senders,
    receivers,
    tile_count,
    send_rows,
):
    node, edge = node_tape[0], edge_tape[0]
    n_cot, e_cot = node_cot[0], edge_cot[0]
    nodes, width = node.shape
    edges = edge.shape[0]
    halo = send_rows.shape[1]
    patches = lax.axis_size("patch")
    members = lax.axis_size("group")
    depth = patches // 8
    here = lax.axis_index("patch")
    place = jnp.stack([here % 2, here // (2 * depth), lax.axis_index("group")]).astype(jnp.int32)
    gain_edge = gain_edge.reshape(1, width)
    gain_node = gain_node.reshape(1, width)
    twins = [(i, i ^ 1) for i in range(patches)]
    column = 2 * depth
    lines = [[y * column + 2 * z + c for z in range(depth)] for y in range(4) for c in range(2)]
    unit = 2 * width * width

    def to_member(x, shift):
        return lax.ppermute(x, "group", [(g, (g + shift) % members) for g in range(members)])

    def to_column(x, shift):
        return lax.ppermute(x, "patch", [(i, (i + shift * column) % patches) for i in range(patches)])

    def along_depth(x, rows):
        return lax.all_to_all(
            x.reshape(depth, rows, width), "patch", 0, 0, axis_index_groups=lines, tiled=True
        )

    parts = edges // ROWS

    def wide(rows, kind=BF):
        return ((rows, width), kind, rows // ROWS)

    parts = edges // ROWS

    def wide(rows, kind=BF):
        return ((rows, width), kind, rows // ROWS)

    outgoing = call(
        outgoing_kernel,
        [((halo, width), BF)],
        [send_rows, node],
        flops=2 * halo * nodes * width,
        limit=16 * 2**20,
    )
    incoming = lax.all_to_all(outgoing, "patch", split_axis=0, concat_axis=0, tiled=True)
    node_turned, edge_turned, begun = call(
        own_kernel,
        [],
        [senders, receivers],
        [((edges, LANE), jnp.int32)] * 2,
        flops=7 * edges * unit,
        fetch=[node, edge, w_edge_in],
        store=[((width, nodes), BF, 1), ((width, edges), BF, 1), wide(edges, F32)],
        limit=FULL,
    )
    each = width // patches
    per_node, per_edge = 3 * each, 4 * each
    piece = ((4, depth * (per_node + per_edge) + 16, width), BF, 4)
    w_send = Part(w_edge_in, 1, width, width)
    node_acc, grad_first, from_send, from_recv, outward, send, keep = call(
        functools.partial(main_kernel, patches),
        [],
        [place, tile_count, senders, receivers, gain_edge, gain_node],
        [((edges, LANE), jnp.int32)] * 2
        + [((edges, width), BF)] * 3
        + [((edges, LANE), F32)]
        + [((edges, width), BF)]
        + [((nodes, width), BF)] * 5
        + [
            ((8, width), F32),
            ((2 * width, width), F32),
            ((width, width), F32),
            ((3 * width, width), F32),
            ((width, width), F32),
        ],
        scalars=2,
        flops=26 * nodes * unit,
        fetch=[
            incoming,
            w_send,
            Part(begun, parts),
            w_edge_out,
            node,
            w_node_in,
            w_node_out,
            Part(n_cot, nodes // ROWS),
            node_turned,
            Part(e_cot, parts),
            edge_turned,
        ],
        store=[
            wide(nodes),
            wide(edges),
            wide(nodes + halo),
            wide(nodes),
            ((halo, width), BF, 1),
            piece,
            piece,
        ],
        limit=FULL,
    )
    got = lax.ppermute(send, "patch", twins)
    sums = call(pair_kernel, [(keep.shape[1:], BF)] * 4, [keep, got])
    columns = [sums[0]] + [to_column(sums[s], s) for s in range(1, 4)]
    returned = lax.all_to_all(outward, "patch", split_axis=0, concat_axis=0, tiled=True)
    edge_grad, edge_token = call(
        edge_grad_kernel,
        [],
        [tile_count],
        scalars=1,
        flops=nodes * unit,
        fetch=[Part(w_edge_in, 1, 0, width), Part(grad_first, parts), Part(e_cot, parts)],
        store=[wide(edges), TOKEN],
        limit=FULL,
    )
    rows = per_node + per_edge + 8
    node_grad, node_token = call(
        node_grad_kernel,
        [],
        [send_rows],
        flops=3 * nodes * unit,
        fetch=[
            Part(w_edge_in, 1, width, 2 * width),
            returned,
            Part(node_acc, nodes // ROWS),
            Part(from_send, nodes // ROWS, 0, nodes),
            Part(from_recv, nodes // ROWS),
        ],
        store=[wide(nodes), TOKEN],
        limit=FULL,
    )
    blocks = call(
        functools.partial(four_kernel, (per_node, per_edge)),
        [((depth, rows, width), BF)],
        columns,
        after=[edge_token, node_token],
    )
    lines_got = along_depth(blocks, rows)
    mine = call(depth_kernel, [((rows, width), BF)], [lines_got])
    shared = [mine] + [to_member(mine, s) for s in range(1, 4)]
    factor = float(members * patches * edges) ** (-0.5)
    out_edge_in, out_edge_out, out_node_in, out_node_out, out_gain = call(
        functools.partial(finish_kernel, factor),
        [
            ((3 * each, width), F32),
            ((each, width), F32),
            ((2 * each, width), F32),
            ((each, width), F32),
            ((8, width), F32),
        ],
        [place] + shared,
        [((4, rows, width), F32)],
        scalars=1,
    )
    out_gain = lax.dynamic_slice(out_gain, (0, here * each), (2, each))
    return (
        edge_grad[None],
        node_grad[None],
        out_edge_in,
        out_edge_out,
        out_gain[0],
        out_node_in,
        out_node_out,
        out_gain[1],
    )


def solution(mesh):
    placed = (
        P("group", "patch", None),
        P("group", "patch", None),
        P("group", "patch", None),
        P("group", "patch", None),
        P(),
        P(),
        P(),
        P(),
        P(),
        P(),
        P("patch", None),
        P("patch", None),
        P("patch"),
        P("patch", None),
    )
    return jax.shard_map(
        local,
        mesh=mesh,
        in_specs=placed,
        out_specs=(
            P("group", "patch", None),
            P("group", "patch", None),
            P("patch", None),
            P("patch", None),
            P("patch"),
            P("patch", None),
            P("patch", None),
            P("patch"),
        ),
        check_vma=False,
    )
```

time: 160 us -> 136 us (0.85); the launches traced: 157 us -> 135 us
  Pallas kernels: 77.9 us -> 54.5 us
  blocking collectives: 0 us -> 22.5 us
  starting transfers between devices: 44.7 us -> 31.4 us
  waiting for transfers between devices: 22.2 us -> 15 us
    pallas_call x14 -> x9, Pallas kernels: 77.1 us -> 54.5 us  [call(): pl.pallas_call(body, out_shape=shapes[0] if single else shapes, in_specs=...]
    all_to_all x0 -> x1, blocking collectives: none -> 22.5 us  [along_depth(): lax.all_to_all(x.reshape(depth, rows, width), 'patch', 0, 0, axis_index_g...]
    all_to_all x2 -> x0, starting transfers between devices: 13.6 us -> none  [along_depth(): lax.all_to_all(x.reshape(depth, rows, width), 'patch', 0, 0, axis_index_g...]
    all_to_all x2 -> x0, waiting for transfers between devices: 12.2 us -> none  [along_depth(): lax.all_to_all(x.reshape(depth, rows, width), 'patch', 0, 0, axis_index_g...]
    all_to_all x1, waiting for transfers between devices: 6.01 us -> 0.01 us  [local(): lax.all_to_all(outward, 'patch', split_axis=0, concat_axis=0, tiled=True)]
    ppermute x6 -> x3, waiting for transfers between devices: 3.93 us -> 9.26 us  [to_column(): lax.ppermute(x, 'patch', [(i, (i + shift * column) % patches) for i in ra...]
    ppermute x3, waiting for transfers between devices: 0.01 us -> 4.78 us  [to_member(): lax.ppermute(x, 'group', [(g, (g + shift) % members) for g in range(membe...]
    all_to_all x1, starting transfers between devices: 5.78 us -> 9.6 us  [local(): lax.all_to_all(outward, 'patch', split_axis=0, concat_axis=0, tiled=True)]
  transfers between devices with their start and end apart: 15 -> 9, of which waited for: 3 -> 6; matrix products, arithmetic and copies ran while one was open for 0% -> 0% of each run, Pallas kernels for 31% -> 15%
where the time goes in v2:
time: 136 us; the launch traced here: 135 us
  Pallas kernels  54.5 us (40%)
  starting transfers between devices  31.4 us (23%)
  blocking collectives  22.5 us (17%)
  waiting for transfers between devices  15 us (11%)
  local copies, waits for them, and re-layouts  9.69 us (7%)
  between operations  1.42 us (1%)
    pallas_call x9, Pallas kernels, call(): pl.pallas_call(body, out_shape=shapes[0] if single else shapes, in_specs=...  54.5 us
    all_to_all x1, blocking collectives, along_depth(): lax.all_to_all(x.reshape(depth, rows, width), 'patch', 0, 0, axis_index_g...  22.5 us
    all_to_all x1, starting transfers between devices, local(): lax.all_to_all(outgoing, 'patch', split_axis=0, concat_axis=0, tiled=True)  12.1 us
    all_to_all x1, starting transfers between devices, local(): lax.all_to_all(outward, 'patch', split_axis=0, concat_axis=0, tiled=True)  9.6 us
    ppermute x3, waiting for transfers between devices, to_column(): lax.ppermute(x, 'patch', [(i, (i + shift * column) % patches) for i in ra...  9.26 us
    ppermute x3, starting transfers between devices, to_column(): lax.ppermute(x, 'patch', [(i, (i + shift * column) % patches) for i in ra...  4.9 us
    ppermute x3, waiting for transfers between devices, to_member(): lax.ppermute(x, 'group', [(g, (g + shift) % members) for g in range(membe...  4.78 us
    ppermute x3, starting transfers between devices, to_member(): lax.ppermute(x, 'group', [(g, (g + shift) % members) for g in range(membe...  4.53 us
  transfers between devices with their start and end apart: 9, of which 6 were waited for; matrix products, arithmetic and copies ran while one was open for 0% of the time, Pallas kernels for 15%

profile of v2, /device:TPU:8, one launch (start us, length us, event | category | flops | bytes accessed | tf_op | source)
XLA Modules:
  0.0 135.1 jit_solution(2308868487917610492)
XLA Ops:
  0.6 1.2 copy-done.1
  1.9 0.7 copy-done.5
  2.5 0.5 shard_map.197
  3.0 0.8 all_to_all.17
  3.8 12.1 %all-to-all-start = ((bf16[64,4,512]{2,1,0:T(4,128)(2,1)}), bf16[64,4,512]{2,1,0:T(4,128)(2,1)S(1)}, u32[]{:S(2)}, u32[]{:S(2)}) async-start(bf16[64,4,512]{2,1,0:T(4,128)(2,1)} %all_to_all.17), calls=%async_computation | async-start | bytes 524288 | tf_op jit(solution)/shard_map/all_to_all | solution.py:547
  16.6 0.6 pad_add_fusion.refs_0_
  17.2 9.3 %shard_map.198 = (bf16[512,1024]{1,0:T(8,128)(2,1)}, bf16[512,1024]{1,0:T(8,128)(2,1)}, f32[1024,512]{1,0:T(8,128)}) custom-call(s32[8,128]{1,0:T(8,128)} %refs_2_.1, s32[8,128]{1,0:T(8,128)} %refs_3_.1, bf16[1024,512]{1,0:T(8,128)(2,1)} %bitcast.15, bf16[1024,512]{1,0:T(8,128)(2,1)} %bitcast.20, bf16[1536,512]{1,0:T(8,128)(2,1)} %refs_1_.6), custom_call_target="tpu_custom_call" | custom-call | flops 3758096384 | bytes 4202496 | tf_op jit(solution)/shard_map/pallas_call | solution.py:468
  26.5 0.9 all-to-all-done
  27.4 0.8 all_to_all.19.refs_6_
  28.2 31.6 %shard_map.199 = (bf16[1024,512]{1,0:T(8,128)(2,1)}, bf16[1024,512]{1,0:T(8,128)(2,1)}, bf16[1280,512]{1,0:T(8,128)(2,1)}, bf16[1024,512]{1,0:T(8,128)(2,1)}, bf...) custom-call(s32[3]{0:T(128)} %pad_add_fusion.refs_0_, ...), custom_call_target="tpu_custom_call" | custom-call | flops 13958643712 | bytes 8531984 | tf_op jit(solution)/shard_map/pallas_call | solution.py:468
  60.1 1.7 %all_to_all.20 = bf16[64,4,512]{2,1,0:T(4,128)(2,1)} reshape(bf16[256,512]{1,0:T(8,128)(2,1)} %get-tuple-element.36) | data formatting | bytes 524288 | tf_op jit(solution)/shard_map/all_to_all | solution.py:607
  61.8 9.6 %all-to-all-start.1 = ((bf16[64,4,512]{2,1,0:T(4,128)(2,1)}), bf16[64,4,512]{2,1,0:T(4,128)(2,1)}, u32[]{:S(2)}, u32[]{:S(2)}) async-start(bf16[64,4,512]{2,1,0:T(4,128)(2,1)} %all_to_all.20), calls=%async_computation.1 | async-start | bytes 524288 | tf_op jit(solution)/shard_map/all_to_all | solution.py:607
  71.4 1.5 %copy-done = bf16[4,464,512]{2,1,0:T(8,128)(2,1)S(1)} copy-done((bf16[4,464,512]{2,1,0:T(8,128)(2,1)S(1)}, bf16[4,464,512]{2,1,0:T(8,128)(2,1)}, u32[]{:S(2)}) %copy-start) | copy-done | bytes 1900568
  72.9 1.1 shard_map.202
  74.1 1.6 %collective-permute-start.1 = (bf16[464,512]{1,0:T(8,128)(2,1)}, bf16[464,512]{1,0:T(8,128)(2,1)S(1)}, u32[]{:S(2)}, u32[]{:S(2)}) collective-permute-start(bf16[464,512]{1,0:T(8,128)(2,1)} %get-tuple-element.44), channel_id=1, source_target_pairs={{0,16},{1,17},{2,18},{3,19},{4,20},{5,21},{6,22},{7,23},{8,24},{9,... | collective-permute-start | bytes 1425416 | tf_op jit(solution)/shard_map/ppermute | solution.py:523
  75.6 1.0 collective-permute-start.2
  76.7 2.3 %collective-permute-start.3 = (bf16[464,512]{1,0:T(8,128)(2,1)S(1)}, bf16[464,512]{1,0:T(8,128)(2,1)S(1)}, u32[]{:S(2)}, u32[]{:S(2)}) collective-permute-start(bf16[464,512]{1,0:T(8,128)(2,1)S(1)} %get-tuple-element.46), channel_id=1, source_target_pairs={{0,48},{1,49},{2,50},{3,51},{4,52},{5,53},{6,54},{7,55},{8,56},{9,... | collective-permute-start | bytes 1425416 | tf_op jit(solution)/shard_map/ppermute | solution.py:523
  79.0 4.0 %shard_map.200 = (bf16[1024,512]{1,0:T(8,128)(2,1)}, f32[8,128]{1,0:T(8,128)}) custom-call(s32[1]{0:T(128)S(6)} %copy.22.refs_1_.refs_0_, bf16[1536,512]{1,0:T(8,128)(2,1)} %refs_1_.6, bf16[1024,512]{1,0:T(8,128)(2,1)} %get-tuple-element.34.refs_2_, bf16[1024,512]{1,0:T(8,128)(2,1)} %bitcast.19), custom_call_target="tpu_custom_call" | custom-call | flops 536870912 | bytes 1052676 | tf_op jit(solution)/shard_map/pallas_call | solution.py:468
  83.0 1.7 %all_to_all.22.refs_2_ = bf16[256,512]{1,0:T(8,128)(2,1)} reshape(bf16[64,4,512]{2,1,0:T(4,128)(2,1)} %all-to-all-done.1) | data formatting | bytes 524288 | tf_op jit(solution)/shard_map/all_to_all | solution.py:607
  84.7 6.4 %shard_map.201 = (bf16[1024,512]{1,0:T(8,128)(2,1)}, f32[8,128]{1,0:T(8,128)}) custom-call(s32[1,256]{1,0:T(1,128)} %refs_0_.6, bf16[1536,512]{1,0:T(8,128)(2,1)} %refs_1_.6, bf16[256,512]{1,0:T(8,128)(2,1)} %all_to_all.22.refs_2_, bf16[1024,512]{1,0:T(8,128)(2,1)} %get-tuple-element.37.refs_3_, bf16[1280,512]{1,0:T(8,128)(2,1)} %get-tuple-element.38.refs_4_, ...), custom_call_target="tpu_custom_call" | custom-call | flops 1610612736 | bytes 1053696 | tf_op jit(solution)/shard_map/pallas_call | solution.py:468
  91.1 0.3 collective-permute-done.2.refs_2_
  91.4 9.0 %collective-permute-done.3.refs_3_ = bf16[464,512]{1,0:T(8,128)(2,1)S(1)} collective-permute-done((bf16[464,512]{1,0:T(8,128)(2,1)S(1)}, bf16[464,512]{1,0:T(8,128)(2,1)S(1)}, u32[]{:S(2)}, u32[]{:S(2)}) %collective-permute-start.3) | collective-permute-done | bytes 475168 | tf_op jit(solution)/shard_map/ppermute | solution.py:523
  100.4 0.7 copy-done.3
  101.0 0.2 shard_map.203
  101.3 22.5 %all_to_all.27.refs_0_ = bf16[8,64,512]{2,1,0:T(8,128)(2,1)S(1)} all-to-all(bf16[8,64,512]{2,1,0:T(8,128)(2,1)S(1)} %shard_map.203), channel_id=1, replica_groups={{0,2,4,6,8,10,12,14},{1,3,5,7,9,11,13,15},{16,18,20,22,24,26,28,30},{17..., dimensions={0} | all-to-all | bytes 1048576 | tf_op jit(solution)/shard_map/all_to_all | solution.py:526
  123.9 2.8 %collective-permute-start.6 = (bf16[64,512]{1,0:T(8,128)(2,1)S(1)}, bf16[64,512]{1,0:T(8,128)(2,1)S(1)}, u32[]{:S(2)}, u32[]{:S(2)}) collective-permute-start(bf16[64,512]{1,0:T(8,128)(2,1)S(1)} %shard_map.204.refs_1_), channel_id=1, source_target_pairs={{0,192},{64,0},{128,64},{192,128},{1,193},{65,1},{129,65},{193,129... | collective-permute-start | bytes 196616 | tf_op jit(solution)/shard_map/ppermute | solution.py:520
  126.7 0.8 collective-permute-start.5
  127.5 0.9 collective-permute-start.4
  128.6 3.9 %collective-permute-done.5.refs_3_ = bf16[64,512]{1,0:T(8,128)(2,1)S(1)} collective-permute-done((bf16[64,512]{1,0:T(8,128)(2,1)S(1)}, bf16[64,512]{1,0:T(8,128)(2,1)S(1)}, u32[]{:S(2)}, u32[]{:S(2)}) %collective-permute-start.5) | collective-permute-done | bytes 65568 | tf_op jit(solution)/shard_map/ppermute | solution.py:520
  132.5 0.7 collective-permute-done.4.refs_2_
  133.2 1.3 shard_map.205
  134.5 0.5 slice_bitcast_fusion
  (15 shorter events, 0.6 us)
Async XLA Ops:
  0.6 1.2 copy-start.1
  1.9 0.7 copy-start.5
  3.8 23.7 %all-to-all-start = ((bf16[64,4,512]{2,1,0:T(4,128)(2,1)}), bf16[64,4,512]{2,1,0:T(4,128)(2,1)S(1)}, u32[]{:S(2)}, u32[]{:S(2)}) async-start(bf16[64,4,512]{2,1,0:T(4,128)(2,1)} %all_to_all.17), calls=%async_computation | async-start | bytes 524288 | tf_op jit(solution)/shard_map/all_to_all | solution.py:547
  59.8 11.6 %collective-permute-start = (bf16[4,464,512]{2,1,0:T(8,128)(2,1)}, bf16[4,464,512]{2,1,0:T(8,128)(2,1)S(1)}, u32[]{:S(2)}, u32[]{:S(2)}) collective-permute-start(bf16[4,464,512]{2,1,0:T(8,128)(2,1)} %get-tuple-element.42), channel_id=1, source_target_pairs={{0,1},{1,0},{2,3},{3,2},{4,5},{5,4},{6,7},{7,6},{8,9},{9,8},{10,11... | collective-permute-start | bytes 5701640 | tf_op jit(solution)/shard_map/ppermute | solution.py:604
  61.8 21.2 %all-to-all-start.1 = ((bf16[64,4,512]{2,1,0:T(4,128)(2,1)}), bf16[64,4,512]{2,1,0:T(4,128)(2,1)}, u32[]{:S(2)}, u32[]{:S(2)}) async-start(bf16[64,4,512]{2,1,0:T(4,128)(2,1)} %all_to_all.20), calls=%async_computation.1 | async-start | bytes 524288 | tf_op jit(solution)/shard_map/all_to_all | solution.py:607
  71.4 1.5 %copy-start = (bf16[4,464,512]{2,1,0:T(8,128)(2,1)S(1)}, bf16[4,464,512]{2,1,0:T(8,128)(2,1)}, u32[]{:S(2)}) copy-start(bf16[4,464,512]{2,1,0:T(8,128)(2,1)} %get-tuple-element.41.refs_0_) | copy-start | bytes 5701636
  74.1 17.0 %collective-permute-start.1 = (bf16[464,512]{1,0:T(8,128)(2,1)}, bf16[464,512]{1,0:T(8,128)(2,1)S(1)}, u32[]{:S(2)}, u32[]{:S(2)}) collective-permute-start(bf16[464,512]{1,0:T(8,128)(2,1)} %get-tuple-element.44), channel_id=1, source_target_pairs={{0,16},{1,17},{2,18},{3,19},{4,20},{5,21},{6,22},{7,23},{8,24},{9,... | collective-permute-start | bytes 1425416 | tf_op jit(solution)/shard_map/ppermute | solution.py:523
  75.6 15.7 %collective-permute-start.2 = (bf16[464,512]{1,0:T(8,128)(2,1)S(1)}, bf16[464,512]{1,0:T(8,128)(2,1)S(1)}, u32[]{:S(2)}, u32[]{:S(2)}) collective-permute-start(bf16[464,512]{1,0:T(8,128)(2,1)S(1)} %get-tuple-element.45), channel_id=1, source_target_pairs={{0,32},{1,33},{2,34},{3,35},{4,36},{5,37},{6,38},{7,39},{8,40},{9,... | collective-permute-start | bytes 1425416 | tf_op jit(solution)/shard_map/ppermute | solution.py:523
  76.7 23.7 %collective-permute-start.3 = (bf16[464,512]{1,0:T(8,128)(2,1)S(1)}, bf16[464,512]{1,0:T(8,128)(2,1)S(1)}, u32[]{:S(2)}, u32[]{:S(2)}) collective-permute-start(bf16[464,512]{1,0:T(8,128)(2,1)S(1)} %get-tuple-element.46), channel_id=1, source_target_pairs={{0,48},{1,49},{2,50},{3,51},{4,52},{5,53},{6,54},{7,55},{8,56},{9,... | collective-permute-start | bytes 1425416 | tf_op jit(solution)/shard_map/ppermute | solution.py:523
  84.7 15.6 %copy-start.2 = (f32[8,128]{1,0:T(8,128)S(1)}, f32[8,128]{1,0:T(8,128)}, u32[]{:S(2)}) copy-start(f32[8,128]{1,0:T(8,128)} %get-tuple-element.47.refs_4_) | copy-start | bytes 12292
  100.4 0.7 copy-start.3
  101.0 32.2 %copy-start.4 = (s32[3]{0:T(128)S(1)}, s32[3]{0:T(128)}, u32[]{:S(2)}) copy-start(s32[3]{0:T(128)} %pad_add_fusion.refs_0_) | copy-start | bytes 40
  123.9 4.7 %collective-permute-start.6 = (bf16[64,512]{1,0:T(8,128)(2,1)S(1)}, bf16[64,512]{1,0:T(8,128)(2,1)S(1)}, u32[]{:S(2)}, u32[]{:S(2)}) collective-permute-start(bf16[64,512]{1,0:T(8,128)(2,1)S(1)} %shard_map.204.refs_1_), channel_id=1, source_target_pairs={{0,192},{64,0},{128,64},{192,128},{1,193},{65,1},{129,65},{193,129... | collective-permute-start | bytes 196616 | tf_op jit(solution)/shard_map/ppermute | solution.py:520
  126.7 5.8 %collective-permute-start.5 = (bf16[64,512]{1,0:T(8,128)(2,1)S(1)}, bf16[64,512]{1,0:T(8,128)(2,1)S(1)}, u32[]{:S(2)}, u32[]{:S(2)}) collective-permute-start(bf16[64,512]{1,0:T(8,128)(2,1)S(1)} %shard_map.204.refs_1_), channel_id=1, source_target_pairs={{0,128},{64,192},{128,0},{192,64},{1,129},{65,193},{129,1},{193,65... | collective-permute-start | bytes 196616 | tf_op jit(solution)/shard_map/ppermute | solution.py:520
  127.5 5.7 %collective-permute-start.4 = (bf16[64,512]{1,0:T(8,128)(2,1)S(1)}, bf16[64,512]{1,0:T(8,128)(2,1)S(1)}, u32[]{:S(2)}, u32[]{:S(2)}) collective-permute-start(bf16[64,512]{1,0:T(8,128)(2,1)S(1)} %shard_map.204.refs_1_), channel_id=1, source_target_pairs={{0,64},{64,128},{128,192},{192,0},{1,65},{65,129},{129,193},{193,1... | collective-permute-start | bytes 196616 | tf_op jit(solution)/shard_map/ppermute | solution.py:520

commit v3 on v2

--- a/solution.py
+++ b/solution.py
@@ -12,6 +12,7 @@
 F32 = jnp.float32
 LANE = 128
 ROWS = 256
+BIG = 1024
 FULL = 60 * 2**20
 
 
@@ -80,12 +81,15 @@
     )
 
 
-def loop(count, body):
+def loop(count, body, rows=ROWS):
     def step(i, carry):
-        body(pl.multiple_of(i * ROWS, ROWS), i)
+        body(pl.multiple_of(i * rows, rows), i)
         return carry
 
-    lax.fori_loop(0, count // ROWS, step, 0)
+    if count == rows:
+        body(0, 0)
+    else:
+        lax.fori_loop(0, count // rows, step, 0)
 
 
 def outgoing_kernel(rows_ref, node_ref, out_ref):
@@ -112,9 +116,9 @@
     node_ref, edge_ref, w_ref = node.ready(), edge.ready(), w_edge.ready()
 
     def body(start, i):
-        here = pl.ds(start, ROWS)
-        from_send = dot(pick_rows(send_cols, start, ROWS, 0, nodes), node_ref[...]).astype(BF)
-        from_recv = dot(pick_rows(recv_cols, start, ROWS, 0, nodes), node_ref[...]).astype(BF)
+        here = pl.ds(start, BIG)
+        from_send = dot(pick_rows(send_cols, start, BIG, 0, nodes), node_ref[...]).astype(BF)
+        from_recv = dot(pick_rows(recv_cols, start, BIG, 0, nodes), node_ref[...]).astype(BF)
         begun.buffer[here, :] = (
             dot(edge_ref[here, :], w_ref[0:width, :])
             + dot(from_send, w_ref[width : 2 * width, :])
@@ -122,10 +126,10 @@
         )
         begun.send(i)
 
-    loop(edge_ref.shape[0], body)
+    loop(edge_ref.shape[0], body, BIG)
     for source, out in ((node_ref, node_turned), (edge_ref, edge_turned)):
-        for i in range(0, source.shape[0], ROWS):
-            out.buffer[:, i : i + ROWS] = source[i : i + ROWS, :].T
+        for i in range(0, source.shape[0], BIG):
+            out.buffer[:, i : i + BIG] = source[i : i + BIG, :].T
         out.send(0)
 
 
@@ -198,12 +202,15 @@
     halo = incoming.shape[0]
     columns_of(send_ref, send_cols)
     columns_of(recv_ref, recv_cols)
-    halo_ref, w_send_ref, w_edge_out_ref = incoming.ready(), w_edge_send.ready(), None
-    w_edge_out_ref = w_edge_out.ready()
+    halo_ref, w_send_ref, w_edge_out_ref = (
+        incoming.ready(),
+        w_edge_send.ready(),
+        w_edge_out.ready(),
+    )
 
     def edge_body(start, i):
-        here = pl.ds(start, ROWS)
-        latent = dot(pick_rows(send_cols, start, ROWS, nodes, halo), halo_ref[...])
+        here = pl.ds(start, BIG)
+        latent = dot(pick_rows(send_cols, start, BIG, nodes, halo), halo_ref[...])
         first = begun.part(i)[here, :] + dot(latent.astype(BF), w_send_ref[...])
         squash = sigmoid(first)
         hidden = (first * squash).astype(BF)
@@ -211,17 +218,17 @@
         slope_ref[here, :] = (squash * (1.0 + first * (1.0 - squash))).astype(BF)
         normed, inverse = normalize(dot(hidden, w_edge_out_ref[...]))
         normed_ref[here, :] = normed.astype(BF)
-        inverse_ref[here, :] = jnp.broadcast_to(inverse, (ROWS, LANE))
-        live = live_rows(count_ref, start, ROWS)
+        inverse_ref[here, :] = jnp.broadcast_to(inverse, (BIG, LANE))
+        live = live_rows(count_ref, start, BIG)
         message[here, :] = (live * (gain_edge_ref[...] * normed)).astype(BF)
 
-    loop(edges, edge_body)
+    loop(edges, edge_body, BIG)
     gains[...] = jnp.zeros_like(gains)
     node_ref, w_node_ref, w_node_out_ref = node.ready(), w_node.ready(), w_node_out.ready()
 
     def node_body(start, i):
-        here = pl.ds(start, ROWS)
-        taken = dot(spread_rows(recv_ref, start, ROWS), message[...]).astype(BF)
+        here = pl.ds(start, BIG)
+        taken = dot(spread_rows(recv_ref, start, BIG), message[...]).astype(BF)
         gathered[here, :] = taken
         first = dot(node_ref[here, :], w_node_ref[0:width, :]) + dot(
             taken, w_node_ref[width : 2 * width, :]
@@ -241,16 +248,23 @@
         back_ref[here, :] = dot_rt(grad, w_node_ref[width : 2 * width, :]).astype(BF)
         node_acc.send(i)
 
-    loop(nodes, node_body)
+    loop(nodes, node_body, BIG)
     node_turned_ref = node_turned.ready()
     sum_out[...] = dot_lt(node_hidden[...], grad_second[...])
     sum_in[0:width, :] = dot(node_turned_ref[...], grad_first[...])
     sum_in[width : 2 * width, :] = dot_lt(gathered[...], grad_first[...])
+    depth = patches // 8
+    each = width // patches
+    pieces = ((sum_in, 2 * each), (sum_out, each))
+    deal(place_ref, depth, pieces, 0, piece_send, piece_keep)
+    for s in range(4):
+        piece_send.send(s)
+        piece_keep.send(s)
 
     def back_body(start, i):
-        here = pl.ds(start, ROWS)
-        live = live_rows(count_ref, start, ROWS)
-        taken = dot(pick_rows(recv_cols, start, ROWS, 0, nodes), back_ref[...])
+        here = pl.ds(start, BIG)
+        live = live_rows(count_ref, start, BIG)
+        taken = dot(pick_rows(recv_cols, start, BIG, 0, nodes), back_ref[...])
         arrived = live * (edge_cot.part(i)[here, :].astype(F32) + taken)
         normed = normed_ref[here, :].astype(F32)
         gains[0:1, :] += jnp.sum(arrived * normed, axis=0, keepdims=True)
@@ -263,17 +277,18 @@
         ).astype(BF)
         first_out.send(i)
 
-    loop(edges, back_body)
+    loop(edges, back_body, BIG)
     first_ref = first_out.buffer
     for out, index_ref in ((from_send, send_ref), (from_recv, recv_ref)):
 
         def body(start, i):
-            out.buffer[pl.ds(start, ROWS), :] = dot(
-                spread_rows(index_ref, start, ROWS), first_ref[...]
+            count = out.shape[0]
+            out.buffer[pl.ds(start, count), :] = dot(
+                spread_rows(index_ref, start, count), first_ref[...]
             ).astype(BF)
             out.send(i)
 
-        loop(out.shape[0], body)
+        loop(out.shape[0], body, out.shape[0])
     sent, received = from_send.buffer, from_recv.buffer
     outward.buffer[...] = dot_rt(sent[nodes : nodes + halo, :], w_send_ref[...]).astype(BF)
     outward.send(0)
@@ -288,15 +303,12 @@
     for out in (piece_send, piece_keep):
         for s in range(4):
             out.buffer[s, rows - 16 : rows, :] = extra
-    depth = patches // 8
-    each = width // patches
-    pieces = ((sum_in, 2 * each), (sum_out, each))
-    deal(place_ref, depth, pieces, 0, piece_send, piece_keep)
     pieces = ((edge_sum_in, 3 * each), (edge_sum_out, each))
     deal(place_ref, depth, pieces, depth * 3 * each, piece_send, piece_keep)
     for s in range(4):
-        piece_send.send(s)
-        piece_keep.send(s)
+        piece_send.send(s + 4)
+    for s in range(4):
+        piece_keep.send(s + 4)
 
 
 def edge_grad_kernel(count_ref, w_own, first, cot, edge_grad, token):
@@ -391,13 +403,19 @@
 
 
 class Moved:
-    def __init__(self, far, buffer, semaphores, parts, first, outward):
-        self.far, self.buffer, self.semaphores = far, buffer, semaphores
+    def __init__(self, far, buffer, semaphores, parts, first, outward, cuts=None):
+        self.far, self.buffer, self.semaphores, self.cuts = far, buffer, semaphores, cuts
         self.parts, self.first, self.outward = parts, first, outward
         self.shape = buffer.shape
         self.step = buffer.shape[0] // parts
 
     def copy(self, i):
+        if self.cuts is not None:
+            lead, cut = i % self.shape[0], i // self.shape[0]
+            rows = pl.ds(self.cuts[cut], self.cuts[cut + 1] - self.cuts[cut])
+            return pltpu.make_async_copy(
+                self.buffer.at[lead, rows], self.far.at[lead, rows], self.semaphores.at[i]
+            )
         near = self.buffer.at[pl.ds(i * self.step, self.step)]
         far = self.far.at[pl.ds(self.first + i * self.step, self.step)]
         ends = (near, far) if self.outward else (far, near)
@@ -456,7 +474,7 @@
             for i in range(one.parts):
                 one.send(i)
         leaving = [
-            Moved(t, room, end, o[2], 0, True)
+            Moved(t, room, end, o[2], 0, True, *o[3:])
             for t, room, end, o in zip(targets, rooms, ends, store)
         ]
         kernel(*args, *arriving, *results, *leaving, *own)
@@ -481,6 +499,77 @@
         ),
         cost_estimate=pl.CostEstimate(flops=flops, bytes_accessed=size, transcendentals=0),
     )(*ins, *after, *[f.array for f in fetch])
+
+
+def main_call(
+    patches,
+    piece,
+    place,
+    tile_count,
+    senders,
+    receivers,
+    gain_edge,
+    gain_node,
+    incoming,
+    begun,
+    node,
+    n_cot,
+    node_turned,
+    e_cot,
+    edge_turned,
+    w_edge_in,
+    w_edge_out,
+    w_node_in,
+    w_node_out,
+):
+    nodes, width = node.shape
+    edges, halo = e_cot.shape[0], incoming.shape[0]
+
+    def wide(rows, kind=BF, step=ROWS):
+        return ((rows, width), kind, rows // step)
+
+    return call(
+        functools.partial(main_kernel, patches),
+        [],
+        [place, tile_count, senders, receivers, gain_edge, gain_node],
+        [((edges, LANE), jnp.int32)] * 2
+        + [((edges, width), BF)] * 3
+        + [((edges, LANE), F32)]
+        + [((edges, width), BF)]
+        + [((nodes, width), BF)] * 5
+        + [
+            ((8, width), F32),
+            ((2 * width, width), F32),
+            ((width, width), F32),
+            ((3 * width, width), F32),
+            ((width, width), F32),
+        ],
+        scalars=2,
+        flops=52 * nodes * width * width,
+        fetch=[
+            incoming,
+            Part(w_edge_in, 1, width, width),
+            Part(begun, edges // BIG),
+            w_edge_out,
+            node,
+            w_node_in,
+            w_node_out,
+            Part(n_cot, nodes // BIG),
+            node_turned,
+            Part(e_cot, edges // BIG),
+            edge_turned,
+        ],
+        store=[
+            wide(nodes, BF, BIG),
+            wide(edges, BF, BIG),
+            wide(nodes + halo, BF, nodes + halo),
+            wide(nodes, BF, nodes),
+            ((halo, width), BF, 1),
+            piece,
+            piece,
+        ],
+        limit=FULL,
+    )
 
 
 def local(
@@ -552,54 +641,33 @@
         [((edges, LANE), jnp.int32)] * 2,
         flops=7 * edges * unit,
         fetch=[node, edge, w_edge_in],
-        store=[((width, nodes), BF, 1), ((width, edges), BF, 1), wide(edges, F32)],
+        store=[((width, nodes), BF, 1), ((width, edges), BF, 1), ((edges, width), F32, edges // BIG)],
         limit=FULL,
     )
     each = width // patches
     per_node, per_edge = 3 * each, 4 * each
-    piece = ((4, depth * (per_node + per_edge) + 16, width), BF, 4)
-    w_send = Part(w_edge_in, 1, width, width)
-    node_acc, grad_first, from_send, from_recv, outward, send, keep = call(
-        functools.partial(main_kernel, patches),
-        [],
-        [place, tile_count, senders, receivers, gain_edge, gain_node],
-        [((edges, LANE), jnp.int32)] * 2
-        + [((edges, width), BF)] * 3
-        + [((edges, LANE), F32)]
-        + [((edges, width), BF)]
-        + [((nodes, width), BF)] * 5
-        + [
-            ((8, width), F32),
-            ((2 * width, width), F32),
-            ((width, width), F32),
-            ((3 * width, width), F32),
-            ((width, width), F32),
-        ],
-        scalars=2,
-        flops=26 * nodes * unit,
-        fetch=[
-            incoming,
-            w_send,
-            Part(begun, parts),
-            w_edge_out,
-            node,
-            w_node_in,
-            w_node_out,
-            Part(n_cot, nodes // ROWS),
-            node_turned,
-            Part(e_cot, parts),
-            edge_turned,
-        ],
-        store=[
-            wide(nodes),
-            wide(edges),
-            wide(nodes + halo),
-            wide(nodes),
-            ((halo, width), BF, 1),
-            piece,
-            piece,
-        ],
-        limit=FULL,
+    all_rows = depth * (per_node + per_edge) + 16
+    piece = ((4, all_rows, width), BF, 8, (0, depth * per_node, all_rows))
+    node_acc, grad_first, from_send, from_recv, outward, send, keep = main_call(
+        patches,
+        piece,
+        place,
+        tile_count,
+        senders,
+        receivers,
+        gain_edge,
+        gain_node,
+        incoming,
+        begun,
+        node,
+        n_cot,
+        node_turned,
+        e_cot,
+        edge_turned,
+        w_edge_in,
+        w_edge_out,
+        w_node_in,
+        w_node_out,
     )
     got = lax.ppermute(send, "patch", twins)
     sums = call(pair_kernel, [(keep.shape[1:], BF)] * 4, [keep, got])
@@ -616,6 +684,14 @@
         limit=FULL,
     )
     rows = per_node + per_edge + 8
+    blocks = call(
+        functools.partial(four_kernel, (per_node, per_edge)),
+        [((depth, rows, width), BF)],
+        columns,
+        flops=40 * nodes * unit,
+        after=[],
+    )
+    lines_got = along_depth(blocks, rows)
     node_grad, node_token = call(
         node_grad_kernel,
         [],
@@ -630,15 +706,9 @@
         ],
         store=[wide(nodes), TOKEN],
         limit=FULL,
-    )
-    blocks = call(
-        functools.partial(four_kernel, (per_node, per_edge)),
-        [((depth, rows, width), BF)],
-        columns,
-        after=[edge_token, node_token],
-    )
-    lines_got = along_depth(blocks, rows)
-    mine = call(depth_kernel, [((rows, width), BF)], [lines_got])
+        after=[edge_token],
+    )
+    mine = call(depth_kernel, [((rows, width), BF)], [lines_got], after=[node_token])
     shared = [mine] + [to_member(mine, s) for s in range(1, 4)]
     factor = float(members * patches * edges) ** (-0.5)
     out_edge_in, out_edge_out, out_node_in, out_node_out, out_gain = call(

time: 136 us -> 122 us (0.90)
  blocking collectives: 22.5 us -> 0 us
  waiting for transfers between devices: 15 us -> 30.1 us
  Pallas kernels: 54.5 us -> 45.5 us
  starting transfers between devices: 31.4 us -> 33.7 us
    all_to_all x1 -> x0, blocking collectives: 22.5 us -> none  [along_depth(): lax.all_to_all(x.reshape(depth, rows, width), 'patch', 0, 0, axis_index_g...]
    pallas_call x9, Pallas kernels: 54.5 us -> 45.5 us  [call(): pl.pallas_call(body, out_shape=shapes[0] if single else shapes, in_specs=...]
    all_to_all x0 -> x1, waiting for transfers between devices: none -> 5.19 us  [along_depth(): lax.all_to_all(x.reshape(depth, rows, width), 'patch', 0, 0, axis_index_g...]
    ppermute x3, waiting for transfers between devices: 9.26 us -> 14.3 us  [to_column(): lax.ppermute(x, 'patch', [(i, (i + shift * column) % patches) for i in ra...]
    all_to_all x0 -> x1, starting transfers between devices: none -> 4.68 us  [along_depth(): lax.all_to_all(x.reshape(depth, rows, width), 'patch', 0, 0, axis_index_g...]
    ppermute x1, waiting for transfers between devices: 0.01 us -> 3.97 us  [local(): got = lax.ppermute(send, 'patch', twins)]
    all_to_all x1, starting transfers between devices: 9.6 us -> 7.16 us  [local(): lax.all_to_all(outward, 'patch', split_axis=0, concat_axis=0, tiled=True)]
    unnamed x12 -> x10, local copies, waits for them, and re-layouts: 4.11 us -> 4.11 us
  transfers between devices with their start and end apart: 9 -> 10, of which waited for: 6 -> 8; matrix products, arithmetic and copies ran while one was open for 0% -> 0% of each run, Pallas kernels for 15% -> 16%
where the time goes in v3:
time: 122 us; the launch traced here: 121 us
  Pallas kernels  45.5 us (37%)
  starting transfers between devices  33.7 us (28%)
  waiting for transfers between devices  30.1 us (25%)
  local copies, waits for them, and re-layouts  9.7 us (8%)
  between operations  1.39 us (1%)
    pallas_call x9, Pallas kernels, call(): pl.pallas_call(body, out_shape=shapes[0] if single else shapes, in_specs=...  45.5 us
    ppermute x3, waiting for transfers between devices, to_column(): lax.ppermute(x, 'patch', [(i, (i + shift * column) % patches) for i in ra...  14.3 us
    all_to_all x1, starting transfers between devices, local(): lax.all_to_all(outgoing, 'patch', split_axis=0, concat_axis=0, tiled=True)  12.1 us
    all_to_all x1, starting transfers between devices, local(): lax.all_to_all(outward, 'patch', split_axis=0, concat_axis=0, tiled=True)  7.16 us
    all_to_all x1, waiting for transfers between devices, along_depth(): lax.all_to_all(x.reshape(depth, rows, width), 'patch', 0, 0, axis_index_g...  5.19 us
    ppermute x3, starting transfers between devices, to_column(): lax.ppermute(x, 'patch', [(i, (i + shift * column) % patches) for i in ra...  4.99 us
    ppermute x3, waiting for transfers between devices, to_member(): lax.ppermute(x, 'group', [(g, (g + shift) % members) for g in range(membe...  4.84 us
    all_to_all x1, starting transfers between devices, along_depth(): lax.all_to_all(x.reshape(depth, rows, width), 'patch', 0, 0, axis_index_g...  4.68 us
  transfers between devices with their start and end apart: 10, of which 8 were waited for; matrix products, arithmetic and copies ran while one was open for 0% of the time, Pallas kernels for 16%

profile of v3, /device:TPU:8, one launch (start us, length us, event | category | flops | bytes accessed | tf_op | source)
XLA Modules:
  0.0 120.9 jit_solution(183971713304509371)
XLA Ops:
  0.6 1.2 %copy-done.1 = bf16[1,1024,512]{2,1,0:T(8,128)(2,1)S(1)} copy-done((bf16[1,1024,512]{2,1,0:T(8,128)(2,1)S(1)}, bf16[1,1024,512]{2,1,0:T(8,128)(2,1)}, u32[]{:S(2)}) %copy-start.1) | copy-done | bytes 1048600
  1.9 0.7 copy-done.4
  3.0 0.8 all_to_all.17
  3.8 12.1 %all-to-all-start = ((bf16[64,4,512]{2,1,0:T(4,128)(2,1)}), bf16[64,4,512]{2,1,0:T(4,128)(2,1)S(1)}, u32[]{:S(2)}, u32[]{:S(2)}) async-start(bf16[64,4,512]{2,1,0:T(4,128)(2,1)} %all_to_all.17), calls=%async_computation | async-start | bytes 524288 | tf_op jit(solution)/shard_map/all_to_all | solution.py:636
  16.6 0.6 pad_add_fusion.refs_0_
  17.2 8.5 %shard_map.198 = (bf16[512,1024]{1,0:T(8,128)(2,1)}, bf16[512,1024]{1,0:T(8,128)(2,1)}, f32[1024,512]{1,0:T(8,128)}) custom-call(s32[8,128]{1,0:T(8,128)} %refs_2_.2, s32[8,128]{1,0:T(8,128)} %refs_3_.1, bf16[1024,512]{1,0:T(8,128)(2,1)} %bitcast.15, bf16[1024,512]{1,0:T(8,128)(2,1)} %bitcast.20, bf16[1536,512]{1,0:T(8,128)(2,1)} %refs_2_.3), custom_call_target="tpu_custom_call" | custom-call | flops 3758096384 | bytes 4202496 | tf_op jit(solution)/shard_map/pallas_call | solution.py:486
  25.7 1.8 %all-to-all-done = bf16[64,4,512]{2,1,0:T(4,128)(2,1)S(1)} async-done(((bf16[64,4,512]{2,1,0:T(4,128)(2,1)}), bf16[64,4,512]{2,1,0:T(4,128)(2,1)S(1)}, u32[]{:S(2)}, u32[]{:S(2)}) %all-to-all-start) | async-done | bytes 262176 | tf_op jit(solution)/shard_map/all_to_all | solution.py:636
  27.4 0.8 all_to_all.19.refs_6_
  28.2 23.3 %shard_map.199 = (bf16[1024,512]{1,0:T(8,128)(2,1)}, bf16[1024,512]{1,0:T(8,128)(2,1)}, bf16[1280,512]{1,0:T(8,128)(2,1)}, bf16[1024,512]{1,0:T(8,128)(2,1)}, bf...) custom-call(s32[3]{0:T(128)} %pad_add_fusion.refs_0_, ...), custom_call_target="tpu_custom_call" | custom-call | flops 13958643712 | bytes 8531984 | tf_op jit(solution)/shard_map/pallas_call | solution.py:486
  51.8 4.0 %collective-permute-done.refs_1_ = bf16[4,464,512]{2,1,0:T(8,128)(2,1)S(1)} collective-permute-done((bf16[4,464,512]{2,1,0:T(8,128)(2,1)}, bf16[4,464,512]{2,1,0:T(8,128)(2,1)S(1)}, u32[]{:S(2)}, u32[]{:S(2)}) %collective-permute-start) | collective-permute-done | bytes 1900576 | tf_op jit(solution)/shard_map/ppermute | solution.py:672
  55.8 1.5 %copy-done = bf16[4,464,512]{2,1,0:T(8,128)(2,1)S(1)} copy-done((bf16[4,464,512]{2,1,0:T(8,128)(2,1)S(1)}, bf16[4,464,512]{2,1,0:T(8,128)(2,1)}, u32[]{:S(2)}) %copy-start) | copy-done | bytes 1900568
  57.7 1.6 %collective-permute-start.1 = (bf16[464,512]{1,0:T(8,128)(2,1)S(1)}, bf16[464,512]{1,0:T(8,128)(2,1)S(1)}, u32[]{:S(2)}, u32[]{:S(2)}) collective-permute-start(bf16[464,512]{1,0:T(8,128)(2,1)S(1)} %get-tuple-element.45), channel_id=1, source_target_pairs={{0,16},{1,17},{2,18},{3,19},{4,20},{5,21},{6,22},{7,23},{8,24},{9,... | collective-permute-start | bytes 1425416 | tf_op jit(solution)/shard_map/ppermute | solution.py:612
  59.4 1.4 %collective-permute-start.2 = (bf16[464,512]{1,0:T(8,128)(2,1)S(1)}, bf16[464,512]{1,0:T(8,128)(2,1)S(1)}, u32[]{:S(2)}, u32[]{:S(2)}) collective-permute-start(bf16[464,512]{1,0:T(8,128)(2,1)S(1)} %get-tuple-element.46), channel_id=1, source_target_pairs={{0,32},{1,33},{2,34},{3,35},{4,36},{5,37},{6,38},{7,39},{8,40},{9,... | collective-permute-start | bytes 1425416 | tf_op jit(solution)/shard_map/ppermute | solution.py:612
  60.7 2.0 %collective-permute-start.3 = (bf16[464,512]{1,0:T(8,128)(2,1)S(1)}, bf16[464,512]{1,0:T(8,128)(2,1)S(1)}, u32[]{:S(2)}, u32[]{:S(2)}) collective-permute-start(bf16[464,512]{1,0:T(8,128)(2,1)S(1)} %get-tuple-element.47), channel_id=1, source_target_pairs={{0,48},{1,49},{2,50},{3,51},{4,52},{5,53},{6,54},{7,55},{8,56},{9,... | collective-permute-start | bytes 1425416 | tf_op jit(solution)/shard_map/ppermute | solution.py:612
  62.7 1.7 %all_to_all.20 = bf16[64,4,512]{2,1,0:T(4,128)(2,1)} reshape(bf16[256,512]{1,0:T(8,128)(2,1)} %get-tuple-element.37) | data formatting | bytes 524288 | tf_op jit(solution)/shard_map/all_to_all | solution.py:675
  64.4 7.2 %all-to-all-start.1 = ((bf16[64,4,512]{2,1,0:T(4,128)(2,1)}), bf16[64,4,512]{2,1,0:T(4,128)(2,1)}, u32[]{:S(2)}, u32[]{:S(2)}) async-start(bf16[64,4,512]{2,1,0:T(4,128)(2,1)} %all_to_all.20), calls=%async_computation.1 | async-start | bytes 524288 | tf_op jit(solution)/shard_map/all_to_all | solution.py:675
  71.6 3.0 %collective-permute-done.2.refs_2_ = bf16[464,512]{1,0:T(8,128)(2,1)S(1)} collective-permute-done((bf16[464,512]{1,0:T(8,128)(2,1)S(1)}, bf16[464,512]{1,0:T(8,128)(2,1)S(1)}, u32[]{:S(2)}, u32[]{:S(2)}) %collective-permute-start.2) | collective-permute-done | bytes 475168 | tf_op jit(solution)/shard_map/ppermute | solution.py:612
  74.6 11.3 %collective-permute-done.3.refs_3_ = bf16[464,512]{1,0:T(8,128)(2,1)S(1)} collective-permute-done((bf16[464,512]{1,0:T(8,128)(2,1)S(1)}, bf16[464,512]{1,0:T(8,128)(2,1)S(1)}, u32[]{:S(2)}, u32[]{:S(2)}) %collective-permute-start.3) | collective-permute-done | bytes 475168 | tf_op jit(solution)/shard_map/ppermute | solution.py:612
  85.9 1.0 shard_map.203
  86.9 4.7 %all-to-all-start.2 = ((bf16[8,64,512]{2,1,0:T(8,128)(2,1)}), bf16[8,64,512]{2,1,0:T(8,128)(2,1)S(1)}, u32[]{:S(2)}, u32[]{:S(2)}) async-start(bf16[8,64,512]{2,1,0:T(8,128)(2,1)} %shard_map.203), calls=%async_computation.2 | async-start | bytes 1048576 | tf_op jit(solution)/shard_map/all_to_all | solution.py:615
  91.6 4.0 %shard_map.200 = (bf16[1024,512]{1,0:T(8,128)(2,1)}, f32[8,128]{1,0:T(8,128)}) custom-call(s32[1]{0:T(128)S(6)} %copy.22.refs_1_.refs_0_, bf16[1536,512]{1,0:T(8,128)(2,1)} %refs_2_.3, bf16[1024,512]{1,0:T(8,128)(2,1)} %get-tuple-element.34.refs_2_, bf16[1024,512]{1,0:T(8,128)(2,1)} %bitcast.19), custom_call_target="tpu_custom_call" | custom-call | flops 536870912 | bytes 1052676 | tf_op jit(solution)/shard_map/pallas_call | solution.py:486
  95.7 1.7 %all_to_all.22.refs_3_ = bf16[256,512]{1,0:T(8,128)(2,1)} reshape(bf16[64,4,512]{2,1,0:T(4,128)(2,1)} %all-to-all-done.1) | data formatting | bytes 524288 | tf_op jit(solution)/shard_map/all_to_all | solution.py:675
  97.4 6.4 %shard_map.201 = (bf16[1024,512]{1,0:T(8,128)(2,1)}, f32[8,128]{1,0:T(8,128)}) custom-call(s32[1,256]{1,0:T(1,128)} %refs_0_.6, f32[8,128]{1,0:T(8,128)} %get-tuple-element.36.refs_1_, bf16[1536,512]{1,0:T(8,128)(2,1)} %refs_2_.3, bf16[256,512]{1,0:T(8,128)(2,1)} %all_to_all.22.refs_3_, bf16[1024,512]{1,0:T(8,128)(2,1)} %get-tuple-element.38.refs_4_, ...), custom_call_target="tpu_custom_call" | custom-call | flops 1610612736 | bytes 1053696 | tf_op jit(solution)/shard_map/pallas_call | solution.py:486
  103.7 5.2 %all-to-all-done.2.refs_0_ = bf16[8,64,512]{2,1,0:T(8,128)(2,1)S(1)} async-done(((bf16[8,64,512]{2,1,0:T(8,128)(2,1)}), bf16[8,64,512]{2,1,0:T(8,128)(2,1)S(1)}, u32[]{:S(2)}, u32[]{:S(2)}) %all-to-all-start.2) | async-done | bytes 524320 | tf_op jit(solution)/shard_map/all_to_all | solution.py:615
  108.9 0.7 copy-done.2
  109.7 2.8 %collective-permute-start.6 = (bf16[64,512]{1,0:T(8,128)(2,1)S(1)}, bf16[64,512]{1,0:T(8,128)(2,1)S(1)}, u32[]{:S(2)}, u32[]{:S(2)}) collective-permute-start(bf16[64,512]{1,0:T(8,128)(2,1)S(1)} %shard_map.204.refs_1_), channel_id=1, source_target_pairs={{0,192},{64,0},{128,64},{192,128},{1,193},{65,1},{129,65},{193,129... | collective-permute-start | bytes 196616 | tf_op jit(solution)/shard_map/ppermute | solution.py:609
  112.5 0.8 collective-permute-start.5
  113.3 0.9 collective-permute-start.4
  114.2 0.6 collective-permute-done.6.refs_4_
  114.8 3.6 %collective-permute-done.5.refs_3_ = bf16[64,512]{1,0:T(8,128)(2,1)S(1)} collective-permute-done((bf16[64,512]{1,0:T(8,128)(2,1)S(1)}, bf16[64,512]{1,0:T(8,128)(2,1)S(1)}, u32[]{:S(2)}, u32[]{:S(2)}) %collective-permute-start.5) | collective-permute-done | bytes 65568 | tf_op jit(solution)/shard_map/ppermute | solution.py:609
  118.4 0.7 collective-permute-done.4.refs_2_
  119.1 1.3 %shard_map.205 = (f32[24,512]{1,0:T(8,128)}, f32[8,512]{1,0:T(8,128)}, f32[16,512]{1,0:T(8,128)}, f32[8,512]{1,0:T(8,128)}, f32[8,512]{1,0:T(8,128)S(1)}) custom-call(s32[3]{0:T(128)S(1)} %copy-done.3, bf16[64,512]{1,0:T(8,128)(2,1)S(1)} %shard_map.204.refs_1_, bf16[64,512]{1,0:T(8,128)(2,1)S(1)} %collective-permute-done.4.refs_2_, ...), custom_call_target="tpu_custom_call" | custom-call | bytes 393228 | tf_op jit(solution)/shard_map/pallas_call | solution.py:486
  (14 shorter events, 1.8 us)
Async XLA Ops:
  0.6 1.2 %copy-start.1 = (bf16[1,1024,512]{2,1,0:T(8,128)(2,1)S(1)}, bf16[1,1024,512]{2,1,0:T(8,128)(2,1)}, u32[]{:S(2)}) copy-start(bf16[1,1024,512]{2,1,0:T(8,128)(2,1)} %param.14) | copy-start | bytes 3145732
  1.9 0.7 copy-start.4
  3.8 23.7 %all-to-all-start = ((bf16[64,4,512]{2,1,0:T(4,128)(2,1)}), bf16[64,4,512]{2,1,0:T(4,128)(2,1)S(1)}, u32[]{:S(2)}, u32[]{:S(2)}) async-start(bf16[64,4,512]{2,1,0:T(4,128)(2,1)} %all_to_all.17), calls=%async_computation | async-start | bytes 524288 | tf_op jit(solution)/shard_map/all_to_all | solution.py:636
  51.6 4.2 %collective-permute-start = (bf16[4,464,512]{2,1,0:T(8,128)(2,1)}, bf16[4,464,512]{2,1,0:T(8,128)(2,1)S(1)}, u32[]{:S(2)}, u32[]{:S(2)}) collective-permute-start(bf16[4,464,512]{2,1,0:T(8,128)(2,1)} %get-tuple-element.43), channel_id=1, source_target_pairs={{0,1},{1,0},{2,3},{3,2},{4,5},{5,4},{6,7},{7,6},{8,9},{9,8},{10,11... | collective-permute-start | bytes 5701640 | tf_op jit(solution)/shard_map/ppermute | solution.py:672
  55.8 1.5 %copy-start = (bf16[4,464,512]{2,1,0:T(8,128)(2,1)S(1)}, bf16[4,464,512]{2,1,0:T(8,128)(2,1)}, u32[]{:S(2)}) copy-start(bf16[4,464,512]{2,1,0:T(8,128)(2,1)} %get-tuple-element.42.refs_0_) | copy-start | bytes 5701636
  57.7 13.9 %collective-permute-start.1 = (bf16[464,512]{1,0:T(8,128)(2,1)S(1)}, bf16[464,512]{1,0:T(8,128)(2,1)S(1)}, u32[]{:S(2)}, u32[]{:S(2)}) collective-permute-start(bf16[464,512]{1,0:T(8,128)(2,1)S(1)} %get-tuple-element.45), channel_id=1, source_target_pairs={{0,16},{1,17},{2,18},{3,19},{4,20},{5,21},{6,22},{7,23},{8,24},{9,... | collective-permute-start | bytes 1425416 | tf_op jit(solution)/shard_map/ppermute | solution.py:612
  59.4 15.3 %collective-permute-start.2 = (bf16[464,512]{1,0:T(8,128)(2,1)S(1)}, bf16[464,512]{1,0:T(8,128)(2,1)S(1)}, u32[]{:S(2)}, u32[]{:S(2)}) collective-permute-start(bf16[464,512]{1,0:T(8,128)(2,1)S(1)} %get-tuple-element.46), channel_id=1, source_target_pairs={{0,32},{1,33},{2,34},{3,35},{4,36},{5,37},{6,38},{7,39},{8,40},{9,... | collective-permute-start | bytes 1425416 | tf_op jit(solution)/shard_map/ppermute | solution.py:612
  60.7 25.2 %collective-permute-start.3 = (bf16[464,512]{1,0:T(8,128)(2,1)S(1)}, bf16[464,512]{1,0:T(8,128)(2,1)S(1)}, u32[]{:S(2)}, u32[]{:S(2)}) collective-permute-start(bf16[464,512]{1,0:T(8,128)(2,1)S(1)} %get-tuple-element.47), channel_id=1, source_target_pairs={{0,48},{1,49},{2,50},{3,51},{4,52},{5,53},{6,54},{7,55},{8,56},{9,... | collective-permute-start | bytes 1425416 | tf_op jit(solution)/shard_map/ppermute | solution.py:612
  64.4 22.5 %all-to-all-start.1 = ((bf16[64,4,512]{2,1,0:T(4,128)(2,1)}), bf16[64,4,512]{2,1,0:T(4,128)(2,1)}, u32[]{:S(2)}, u32[]{:S(2)}) async-start(bf16[64,4,512]{2,1,0:T(4,128)(2,1)} %all_to_all.20), calls=%async_computation.1 | async-start | bytes 524288 | tf_op jit(solution)/shard_map/all_to_all | solution.py:675
  86.9 22.0 %all-to-all-start.2 = ((bf16[8,64,512]{2,1,0:T(8,128)(2,1)}), bf16[8,64,512]{2,1,0:T(8,128)(2,1)S(1)}, u32[]{:S(2)}, u32[]{:S(2)}) async-start(bf16[8,64,512]{2,1,0:T(8,128)(2,1)} %shard_map.203), calls=%async_computation.2 | async-start | bytes 1048576 | tf_op jit(solution)/shard_map/all_to_all | solution.py:615
  97.4 21.7 %copy-start.3 = (s32[3]{0:T(128)S(1)}, s32[3]{0:T(128)}, u32[]{:S(2)}) copy-start(s32[3]{0:T(128)} %pad_add_fusion.refs_0_) | copy-start | bytes 40
  108.9 0.7 copy-start.2
  109.7 5.1 %collective-permute-start.6 = (bf16[64,512]{1,0:T(8,128)(2,1)S(1)}, bf16[64,512]{1,0:T(8,128)(2,1)S(1)}, u32[]{:S(2)}, u32[]{:S(2)}) collective-permute-start(bf16[64,512]{1,0:T(8,128)(2,1)S(1)} %shard_map.204.refs_1_), channel_id=1, source_target_pairs={{0,192},{64,0},{128,64},{192,128},{1,193},{65,1},{129,65},{193,129... | collective-permute-start | bytes 196616 | tf_op jit(solution)/shard_map/ppermute | solution.py:609
  112.5 5.9 %collective-permute-start.5 = (bf16[64,512]{1,0:T(8,128)(2,1)S(1)}, bf16[64,512]{1,0:T(8,128)(2,1)S(1)}, u32[]{:S(2)}, u32[]{:S(2)}) collective-permute-start(bf16[64,512]{1,0:T(8,128)(2,1)S(1)} %shard_map.204.refs_1_), channel_id=1, source_target_pairs={{0,128},{64,192},{128,0},{192,64},{1,129},{65,193},{129,1},{193,65... | collective-permute-start | bytes 196616 | tf_op jit(solution)/shard_map/ppermute | solution.py:609
  113.3 5.7 %collective-permute-start.4 = (bf16[64,512]{1,0:T(8,128)(2,1)S(1)}, bf16[64,512]{1,0:T(8,128)(2,1)S(1)}, u32[]{:S(2)}, u32[]{:S(2)}) collective-permute-start(bf16[64,512]{1,0:T(8,128)(2,1)S(1)} %shard_map.204.refs_1_), channel_id=1, source_target_pairs={{0,64},{64,128},{128,192},{192,0},{1,65},{65,129},{129,193},{193,1... | collective-permute-start | bytes 196616 | tf_op jit(solution)/shard_map/ppermute | solution.py:609

commit v4 on v3

--- a/solution.py
+++ b/solution.py
@@ -133,24 +133,36 @@
         out.send(0)
 
 
-def deal(place_ref, depth, pieces, first, send, keep):
-    core, column = place_ref[0], place_ref[1]
-    each = sum(rows for _, rows in pieces)
-    batch = 1 if each % 16 == 0 else 2
+def deal(place_ref, depth, pieces, send, keep):
+    core, column, member = place_ref[0], place_ref[1], place_ref[2]
+    half = pieces[0][0].shape[1] // 2
+    rows = sum(count for _, count in pieces)
+    part = rows // 4
     for which, out in ((1 - core, send), (core, keep)):
 
         def step(s, carry):
-            for i in range(0, depth, batch):
+            line = (column + s) % 4
+            for z in range(depth):
+                patch = (line * depth + z) * 2 + which
                 found = []
-                for b in range(batch):
-                    patch = (((column + s) % 4) * depth + i + b) * 2 + which
-                    for ref, rows in pieces:
-                        found.append(ref[pl.ds(pl.multiple_of(patch * rows, 8), rows), :])
-                at = first + i * each
-                out.buffer[s, at : at + batch * each, :] = jnp.concatenate(found, axis=0).astype(BF)
+                for ref, count in pieces:
+                    if ref.shape[0] == count:
+                        found.append(ref[...])
+                    else:
+                        found.append(ref[pl.ds(pl.multiple_of(patch * count, 8), count), :])
+                block = jnp.concatenate(found, axis=0).astype(BF)
+                out.buffer[s, z * rows : (z + 1) * rows, :] = block[:, 0:half]
+                at = pl.multiple_of((s * depth + z) * part, 16)
+                for x in range(4):
+                    out.buffer[4 + (x - member + 4) % 4, pl.ds(at, part), :] = block[
+                        x * part : (x + 1) * part, half:
+                    ]
+            out.send(s)
             return carry
 
         lax.fori_loop(0, 4, step, 0)
+        for s in range(4, 8):
+            out.send(s)
 
 
 def main_kernel(
@@ -253,13 +265,6 @@
     sum_out[...] = dot_lt(node_hidden[...], grad_second[...])
     sum_in[0:width, :] = dot(node_turned_ref[...], grad_first[...])
     sum_in[width : 2 * width, :] = dot_lt(gathered[...], grad_first[...])
-    depth = patches // 8
-    each = width // patches
-    pieces = ((sum_in, 2 * each), (sum_out, each))
-    deal(place_ref, depth, pieces, 0, piece_send, piece_keep)
-    for s in range(4):
-        piece_send.send(s)
-        piece_keep.send(s)
 
     def back_body(start, i):
         here = pl.ds(start, BIG)
@@ -298,17 +303,15 @@
         halo_ref[...], sent[nodes : nodes + halo, :]
     )
     edge_sum_in[2 * width : 3 * width, :] = dot(node_turned_ref[...], received[...])
-    extra = jnp.concatenate([gains[...], jnp.zeros((8, width), F32)], axis=0).astype(BF)
-    rows = piece_keep.shape[1]
-    for out in (piece_send, piece_keep):
-        for s in range(4):
-            out.buffer[s, rows - 16 : rows, :] = extra
-    pieces = ((edge_sum_in, 3 * each), (edge_sum_out, each))
-    deal(place_ref, depth, pieces, depth * 3 * each, piece_send, piece_keep)
-    for s in range(4):
-        piece_send.send(s + 4)
-    for s in range(4):
-        piece_keep.send(s + 4)
+    each = width // patches
+    pieces = (
+        (sum_in, 2 * each),
+        (sum_out, each),
+        (edge_sum_in, 3 * each),
+        (edge_sum_out, each),
+        (gains, 8),
+    )
+    deal(place_ref, patches // 8, pieces, piece_send, piece_keep)
 
 
 def edge_grad_kernel(count_ref, w_own, first, cot, edge_grad, token):
@@ -349,20 +352,30 @@
 
 
 def pair_kernel(keep_ref, got_ref, *outs):
+    for s in range(8):
+        outs[s][...] = (keep_ref[s].astype(F32) + got_ref[s].astype(F32)).astype(BF)
+
+
+def sum_of(refs):
+    a, b, c, d = [ref[...].astype(F32) for ref in refs]
+    return (a + b) + (c + d)
+
+
+def right_kernel(a, b, c, d, *outs):
+    total = sum_of((a, b, c, d))
+    rows = total.shape[0] // 4
     for s in range(4):
-        outs[s][...] = (keep_ref[s].astype(F32) + got_ref[s].astype(F32)).astype(BF)
-
-
-def four_kernel(counts, a, b, c, d, out_ref):
-    total = a[...].astype(F32) + b[...].astype(F32) + c[...].astype(F32) + d[...].astype(F32)
-    depth = out_ref.shape[0]
-    last = total[depth * sum(counts) :][0:8]
+        outs[s][...] = total[s * rows : (s + 1) * rows].astype(BF)
+
+
+def four_kernel(*refs):
+    left, right, out = sum_of(refs[0:4]), sum_of(refs[4:8]), refs[8]
+    depth = out.shape[0]
+    many, few = left.shape[0] // depth, right.shape[0] // depth
     for z in range(depth):
-        found, base = [], 0
-        for rows in counts:
-            found.append(total[base + z * rows : base + (z + 1) * rows])
-            base += depth * rows
-        out_ref[z] = jnp.concatenate(found + [last], axis=0).astype(BF)
+        out[z] = jnp.concatenate(
+            [left[z * many : (z + 1) * many], right[z * few : (z + 1) * few]], axis=0
+        ).astype(BF)
 
 
 def depth_kernel(got_ref, out_ref):
@@ -384,15 +397,22 @@
     node_in_ref,
     node_out_ref,
     gain_ref,
-    rows,
+    left,
+    right,
 ):
     member = place_ref[2]
+    rows, half = left.shape[1:]
     for s, ref in enumerate((a, b, c, d)):
-        rows[(member - s + 4) % 4] = ref[...].astype(F32)
-    total = ((rows[0] + rows[1]) + (rows[2] + rows[3])) * factor
+        source = (member - s + 4) % 4
+        values = ref[...].astype(F32)
+        left[source] = values[0:rows]
+        right[source] = values[rows : rows + right.shape[1]]
+    total = ((left[0] + left[1]) + (left[2] + left[3])) * factor
+    other = right[...].reshape(rows, half) * factor
     at = 0
     for out in (node_in_ref, node_out_ref, edge_in_ref, edge_out_ref, gain_ref):
-        out[...] = total[at : at + out.shape[0], :]
+        out[:, 0:half] = total[at : at + out.shape[0], :]
+        out[:, half : 2 * half] = other[at : at + out.shape[0], :]
         at += out.shape[0]
 
 
@@ -403,19 +423,13 @@
 
 
 class Moved:
-    def __init__(self, far, buffer, semaphores, parts, first, outward, cuts=None):
-        self.far, self.buffer, self.semaphores, self.cuts = far, buffer, semaphores, cuts
+    def __init__(self, far, buffer, semaphores, parts, first, outward):
+        self.far, self.buffer, self.semaphores = far, buffer, semaphores
         self.parts, self.first, self.outward = parts, first, outward
         self.shape = buffer.shape
         self.step = buffer.shape[0] // parts
 
     def copy(self, i):
-        if self.cuts is not None:
-            lead, cut = i % self.shape[0], i // self.shape[0]
-            rows = pl.ds(self.cuts[cut], self.cuts[cut + 1] - self.cuts[cut])
-            return pltpu.make_async_copy(
-                self.buffer.at[lead, rows], self.far.at[lead, rows], self.semaphores.at[i]
-            )
         near = self.buffer.at[pl.ds(i * self.step, self.step)]
         far = self.far.at[pl.ds(self.first + i * self.step, self.step)]
         ends = (near, far) if self.outward else (far, near)
@@ -474,7 +488,7 @@
             for i in range(one.parts):
                 one.send(i)
         leaving = [
-            Moved(t, room, end, o[2], 0, True, *o[3:])
+            Moved(t, room, end, o[2], 0, True)
             for t, room, end, o in zip(targets, rooms, ends, store)
         ]
         kernel(*args, *arriving, *results, *leaving, *own)
@@ -611,10 +625,8 @@
     def to_column(x, shift):
         return lax.ppermute(x, "patch", [(i, (i + shift * column) % patches) for i in range(patches)])
 
-    def along_depth(x, rows):
-        return lax.all_to_all(
-            x.reshape(depth, rows, width), "patch", 0, 0, axis_index_groups=lines, tiled=True
-        )
+    def along_depth(x):
+        return lax.all_to_all(x, "patch", 0, 0, axis_index_groups=lines, tiled=True)
 
     parts = edges // ROWS
 
@@ -645,9 +657,8 @@
         limit=FULL,
     )
     each = width // patches
-    per_node, per_edge = 3 * each, 4 * each
-    all_rows = depth * (per_node + per_edge) + 16
-    piece = ((4, all_rows, width), BF, 8, (0, depth * per_node, all_rows))
+    rows, half = 8 * each, width // 2
+    piece = ((8, depth * rows, half), BF, 8)
     node_acc, grad_first, from_send, from_recv, outward, send, keep = main_call(
         patches,
         piece,
@@ -670,8 +681,14 @@
         w_node_out,
     )
     got = lax.ppermute(send, "patch", twins)
-    sums = call(pair_kernel, [(keep.shape[1:], BF)] * 4, [keep, got])
+    sums = call(pair_kernel, [(keep.shape[1:], BF)] * 8, [keep, got])
     columns = [sums[0]] + [to_column(sums[s], s) for s in range(1, 4)]
+    rights = call(
+        right_kernel,
+        [((depth * rows // 4, half), BF)] * 4,
+        [sums[4]] + [to_member(sums[4 + s], s) for s in range(1, 4)],
+    )
+    columns += [rights[0]] + [to_column(rights[s], s) for s in range(1, 4)]
     returned = lax.all_to_all(outward, "patch", split_axis=0, concat_axis=0, tiled=True)
     edge_grad, edge_token = call(
         edge_grad_kernel,
@@ -683,15 +700,13 @@
         store=[wide(edges), TOKEN],
         limit=FULL,
     )
-    rows = per_node + per_edge + 8
     blocks = call(
-        functools.partial(four_kernel, (per_node, per_edge)),
-        [((depth, rows, width), BF)],
+        four_kernel,
+        [((depth, rows + rows // 4, half), BF)],
         columns,
-        flops=40 * nodes * unit,
-        after=[],
-    )
-    lines_got = along_depth(blocks, rows)
+        flops=8 * nodes * unit,
+    )
+    lines_got = along_depth(blocks)
     node_grad, node_token = call(
         node_grad_kernel,
         [],
@@ -708,7 +723,12 @@
         limit=FULL,
         after=[edge_token],
     )
-    mine = call(depth_kernel, [((rows, width), BF)], [lines_got], after=[node_token])
+    mine = call(
+        depth_kernel,
+        [((rows + rows // 4, half), BF)],
+        [lines_got],
+        after=[node_token],
+    )
     shared = [mine] + [to_member(mine, s) for s in range(1, 4)]
     factor = float(members * patches * edges) ** (-0.5)
     out_edge_in, out_edge_out, out_node_in, out_node_out, out_gain = call(
@@ -721,7 +741,7 @@
             ((8, width), F32),
         ],
         [place] + shared,
-        [((4, rows, width), F32)],
+        [((4, rows, half), F32), ((4, rows // 4, half), F32)],
         scalars=1,
     )
     out_gain = lax.dynamic_slice(out_gain, (0, here * each), (2, each))

time: 122 us -> 121 us (level)
  waiting for transfers between devices: 30.1 us -> 17.8 us
  starting transfers between devices: 33.7 us -> 45.1 us
    ppermute x3 -> x6, waiting for transfers between devices: 14.3 us -> 4.64 us  [to_column(): lax.ppermute(x, 'patch', [(i, (i + shift * column) % patches) for i in ra...]
    ppermute x3 -> x6, starting transfers between devices: 4.53 us -> 9.85 us  [to_member(): lax.ppermute(x, 'group', [(g, (g + shift) % members) for g in range(membe...]
    all_to_all x1, waiting for transfers between devices: 5.19 us -> 1.14 us  [along_depth(): return lax.all_to_all(x, 'patch', 0, 0, axis_index_groups=lines, tiled=True)]
    ppermute x3 -> x6, starting transfers between devices: 4.99 us -> 8.97 us  [to_column(): lax.ppermute(x, 'patch', [(i, (i + shift * column) % patches) for i in ra...]
    ppermute x3 -> x6, waiting for transfers between devices: 4.84 us -> 5.26 us  [to_member(): lax.ppermute(x, 'group', [(g, (g + shift) % members) for g in range(membe...]
    pallas_call x9 -> x10, Pallas kernels: 45.5 us -> 45.5 us  [call(): pl.pallas_call(body, out_shape=shapes[0] if single else shapes, in_specs=...]
  transfers between devices with their start and end apart: 10 -> 16, of which waited for: 8 -> 9; matrix products, arithmetic and copies ran while one was open for 0% -> 0% of each run, Pallas kernels for 16% -> 17%
where the time goes in v4:
time: 121 us; the launch traced here: 120 us
  Pallas kernels  45.5 us (38%)
  starting transfers between devices  45.1 us (37%)
  waiting for transfers between devices  17.8 us (15%)
  local copies, waits for them, and re-layouts  9.73 us (8%)
  between operations  1.42 us (1%)
    pallas_call x10, Pallas kernels, call(): pl.pallas_call(body, out_shape=shapes[0] if single else shapes, in_specs=...  45.5 us
    all_to_all x1, starting transfers between devices, local(): lax.all_to_all(outgoing, 'patch', split_axis=0, concat_axis=0, tiled=True)  12.1 us
    ppermute x6, starting transfers between devices, to_member(): lax.ppermute(x, 'group', [(g, (g + shift) % members) for g in range(membe...  9.85 us
    ppermute x6, starting transfers between devices, to_column(): lax.ppermute(x, 'patch', [(i, (i + shift * column) % patches) for i in ra...  8.97 us
    all_to_all x1, starting transfers between devices, local(): lax.all_to_all(outward, 'patch', split_axis=0, concat_axis=0, tiled=True)  8.3 us
    all_to_all x1, starting transfers between devices, along_depth(): return lax.all_to_all(x, 'patch', 0, 0, axis_index_groups=lines, tiled=True)  5.65 us
    ppermute x6, waiting for transfers between devices, to_member(): lax.ppermute(x, 'group', [(g, (g + shift) % members) for g in range(membe...  5.26 us
    ppermute x6, waiting for transfers between devices, to_column(): lax.ppermute(x, 'patch', [(i, (i + shift * column) % patches) for i in ra...  4.64 us
  transfers between devices with their start and end apart: 16, of which 9 were waited for; matrix products, arithmetic and copies ran while one was open for 0% of the time, Pallas kernels for 17%

profile of v4, /device:TPU:8, one launch (start us, length us, event | category | flops | bytes accessed | tf_op | source)
XLA Modules:
  0.0 120.1 jit_solution(9460822678874055415)
XLA Ops:
  0.6 1.2 %copy-done.1 = bf16[1,1024,512]{2,1,0:T(8,128)(2,1)S(1)} copy-done((bf16[1,1024,512]{2,1,0:T(8,128)(2,1)S(1)}, bf16[1,1024,512]{2,1,0:T(8,128)(2,1)}, u32[]{:S(2)}) %copy-start.1) | copy-done | bytes 1048600
  3.8 12.1 %all-to-all-start = ((bf16[64,4,512]{2,1,0:T(4,128)(2,1)}), bf16[64,4,512]{2,1,0:T(4,128)(2,1)S(1)}, u32[]{:S(2)}, u32[]{:S(2)}) async-start(bf16[64,4,512]{2,1,0:T(4,128)(2,1)} %all_to_all.17), calls=%async_computation | async-start | bytes 524288 | tf_op jit(solution)/shard_map/all_to_all | solution.py:648
  17.2 8.5 %shard_map.198 = (bf16[512,1024]{1,0:T(8,128)(2,1)}, bf16[512,1024]{1,0:T(8,128)(2,1)}, f32[1024,512]{1,0:T(8,128)}) custom-call(s32[8,128]{1,0:T(8,128)} %refs_2_.2, s32[8,128]{1,0:T(8,128)} %refs_3_.1, bf16[1024,512]{1,0:T(8,128)(2,1)} %bitcast.15, bf16[1024,512]{1,0:T(8,128)(2,1)} %bitcast.20, bf16[1536,512]{1,0:T(8,128)(2,1)} %refs_2_.3), custom_call_target="tpu_custom_call" | custom-call | flops 3758096384 | bytes 4202496 | tf_op jit(solution)/shard_map/pallas_call | solution.py:500
  25.7 1.8 %all-to-all-done = bf16[64,4,512]{2,1,0:T(4,128)(2,1)S(1)} async-done(((bf16[64,4,512]{2,1,0:T(4,128)(2,1)}), bf16[64,4,512]{2,1,0:T(4,128)(2,1)S(1)}, u32[]{:S(2)}, u32[]{:S(2)}) %all-to-all-start) | async-done | bytes 262176 | tf_op jit(solution)/shard_map/all_to_all | solution.py:648
  28.2 23.3 %shard_map.199 = (bf16[1024,512]{1,0:T(8,128)(2,1)}, bf16[1024,512]{1,0:T(8,128)(2,1)}, bf16[1280,512]{1,0:T(8,128)(2,1)}, bf16[1024,512]{1,0:T(8,128)(2,1)}, bf...) custom-call(s32[3]{0:T(128)} %pad_add_fusion.refs_0_, ...), custom_call_target="tpu_custom_call" | custom-call | flops 13958643712 | bytes 8925200 | tf_op jit(solution)/shard_map/pallas_call | solution.py:500
  51.8 4.2 %collective-permute-done.refs_1_ = bf16[8,512,256]{2,1,0:T(8,128)(2,1)S(1)} collective-permute-done((bf16[8,512,256]{2,1,0:T(8,128)(2,1)}, bf16[8,512,256]{2,1,0:T(8,128)(2,1)S(1)}, u32[]{:S(2)}, u32[]{:S(2)}) %collective-permute-start) | collective-permute-done | bytes 2097184 | tf_op jit(solution)/shard_map/ppermute | solution.py:683
  56.0 1.6 %copy-done = bf16[8,512,256]{2,1,0:T(8,128)(2,1)S(1)} copy-done((bf16[8,512,256]{2,1,0:T(8,128)(2,1)S(1)}, bf16[8,512,256]{2,1,0:T(8,128)(2,1)}, u32[]{:S(2)}) %copy-start) | copy-done | bytes 2097176
  58.1 1.6 %collective-permute-start.4 = (bf16[512,256]{1,0:T(8,128)(2,1)S(1)}, bf16[512,256]{1,0:T(8,128)(2,1)S(1)}, u32[]{:S(2)}, u32[]{:S(2)}) collective-permute-start(bf16[512,256]{1,0:T(8,128)(2,1)S(1)} %get-tuple-element.57), channel_id=1, source_target_pairs={{0,64},{64,128},{128,192},{192,0},{1,65},{65,129},{129,193},{193,1... | collective-permute-start | bytes 786440 | tf_op jit(solution)/shard_map/ppermute | solution.py:623
  59.6 2.7 %collective-permute-start.5 = (bf16[512,256]{1,0:T(8,128)(2,1)S(1)}, bf16[512,256]{1,0:T(8,128)(2,1)S(1)}, u32[]{:S(2)}, u32[]{:S(2)}) collective-permute-start(bf16[512,256]{1,0:T(8,128)(2,1)S(1)} %get-tuple-element.58), channel_id=1, source_target_pairs={{0,128},{64,192},{128,0},{192,64},{1,129},{65,193},{129,1},{193,65... | collective-permute-start | bytes 786440 | tf_op jit(solution)/shard_map/ppermute | solution.py:623
  62.4 1.4 %collective-permute-start.6 = (bf16[512,256]{1,0:T(8,128)(2,1)S(1)}, bf16[512,256]{1,0:T(8,128)(2,1)S(1)}, u32[]{:S(2)}, u32[]{:S(2)}) collective-permute-start(bf16[512,256]{1,0:T(8,128)(2,1)S(1)} %get-tuple-element.59), channel_id=1, source_target_pairs={{0,192},{64,0},{128,64},{192,128},{1,193},{65,1},{129,65},{193,129... | collective-permute-start | bytes 786440 | tf_op jit(solution)/shard_map/ppermute | solution.py:623
  63.8 1.6 %collective-permute-start.1 = (bf16[512,256]{1,0:T(8,128)(2,1)S(1)}, bf16[512,256]{1,0:T(8,128)(2,1)S(1)}, u32[]{:S(2)}, u32[]{:S(2)}) collective-permute-start(bf16[512,256]{1,0:T(8,128)(2,1)S(1)} %get-tuple-element.53), channel_id=1, source_target_pairs={{0,16},{1,17},{2,18},{3,19},{4,20},{5,21},{6,22},{7,23},{8,24},{9,... | collective-permute-start | bytes 786440 | tf_op jit(solution)/shard_map/ppermute | solution.py:626
  65.4 1.4 %collective-permute-start.2 = (bf16[512,256]{1,0:T(8,128)(2,1)S(1)}, bf16[512,256]{1,0:T(8,128)(2,1)S(1)}, u32[]{:S(2)}, u32[]{:S(2)}) collective-permute-start(bf16[512,256]{1,0:T(8,128)(2,1)S(1)} %get-tuple-element.54), channel_id=1, source_target_pairs={{0,32},{1,33},{2,34},{3,35},{4,36},{5,37},{6,38},{7,39},{8,40},{9,... | collective-permute-start | bytes 786440 | tf_op jit(solution)/shard_map/ppermute | solution.py:626
  66.8 0.9 collective-permute-done.4.refs_1_
  67.7 1.0 collective-permute-start.3
  68.7 1.7 %all_to_all.20 = bf16[64,4,512]{2,1,0:T(4,128)(2,1)} reshape(bf16[256,512]{1,0:T(8,128)(2,1)} %get-tuple-element.45) | data formatting | bytes 524288 | tf_op jit(solution)/shard_map/all_to_all | solution.py:692
  70.4 8.3 %all-to-all-start.1 = ((bf16[64,4,512]{2,1,0:T(4,128)(2,1)}), bf16[64,4,512]{2,1,0:T(4,128)(2,1)}, u32[]{:S(2)}, u32[]{:S(2)}) async-start(bf16[64,4,512]{2,1,0:T(4,128)(2,1)} %all_to_all.20), calls=%async_computation.1 | async-start | bytes 524288 | tf_op jit(solution)/shard_map/all_to_all | solution.py:692
  78.9 1.6 %collective-permute-start.7 = (bf16[128,256]{1,0:T(8,128)(2,1)S(1)}, bf16[128,256]{1,0:T(8,128)(2,1)S(1)}, u32[]{:S(2)}, u32[]{:S(2)}) collective-permute-start(bf16[128,256]{1,0:T(8,128)(2,1)S(1)} %get-tuple-element.61), channel_id=1, source_target_pairs={{0,16},{1,17},{2,18},{3,19},{4,20},{5,21},{6,22},{7,23},{8,24},{9,... | collective-permute-start | bytes 196616 | tf_op jit(solution)/shard_map/ppermute | solution.py:626
  80.5 1.3 %collective-permute-start.8 = (bf16[128,256]{1,0:T(8,128)(2,1)S(1)}, bf16[128,256]{1,0:T(8,128)(2,1)S(1)}, u32[]{:S(2)}, u32[]{:S(2)}) collective-permute-start(bf16[128,256]{1,0:T(8,128)(2,1)S(1)} %get-tuple-element.62), channel_id=1, source_target_pairs={{0,32},{1,33},{2,34},{3,35},{4,36},{5,37},{6,38},{7,39},{8,40},{9,... | collective-permute-start | bytes 196616 | tf_op jit(solution)/shard_map/ppermute | solution.py:626
  81.8 2.1 %collective-permute-start.9 = (bf16[128,256]{1,0:T(8,128)(2,1)S(1)}, bf16[128,256]{1,0:T(8,128)(2,1)S(1)}, u32[]{:S(2)}, u32[]{:S(2)}) collective-permute-start(bf16[128,256]{1,0:T(8,128)(2,1)S(1)} %get-tuple-element.63), channel_id=1, source_target_pairs={{0,48},{1,49},{2,50},{3,51},{4,52},{5,53},{6,54},{7,55},{8,56},{9,... | collective-permute-start | bytes 196616 | tf_op jit(solution)/shard_map/ppermute | solution.py:626
  83.9 4.4 %collective-permute-done.8.refs_6_ = bf16[128,256]{1,0:T(8,128)(2,1)S(1)} collective-permute-done((bf16[128,256]{1,0:T(8,128)(2,1)S(1)}, bf16[128,256]{1,0:T(8,128)(2,1)S(1)}, u32[]{:S(2)}, u32[]{:S(2)}) %collective-permute-start.8) | collective-permute-done | bytes 65568 | tf_op jit(solution)/shard_map/ppermute | solution.py:626
  88.5 0.9 shard_map.204
  89.4 0.8 all-to-all-done.1
  90.2 5.7 %all-to-all-start.2 = ((bf16[8,80,256]{2,1,0:T(8,128)(2,1)}), bf16[8,80,256]{2,1,0:T(8,128)(2,1)S(1)}, u32[]{:S(2)}, u32[]{:S(2)}) async-start(bf16[8,80,256]{2,1,0:T(8,128)(2,1)} %shard_map.204), calls=%async_computation.2 | async-start | bytes 655360 | tf_op jit(solution)/shard_map/all_to_all | solution.py:629
  95.9 4.0 %shard_map.200 = (bf16[1024,512]{1,0:T(8,128)(2,1)}, f32[8,128]{1,0:T(8,128)}) custom-call(s32[1]{0:T(128)S(6)} %copy.22.refs_1_.refs_0_, bf16[1536,512]{1,0:T(8,128)(2,1)} %refs_2_.3, bf16[1024,512]{1,0:T(8,128)(2,1)} %get-tuple-element.42.refs_2_, bf16[1024,512]{1,0:T(8,128)(2,1)} %bitcast.19), custom_call_target="tpu_custom_call" | custom-call | flops 536870912 | bytes 1052676 | tf_op jit(solution)/shard_map/pallas_call | solution.py:500
  99.9 1.7 %all_to_all.22.refs_3_ = bf16[256,512]{1,0:T(8,128)(2,1)} reshape(bf16[64,4,512]{2,1,0:T(4,128)(2,1)} %all-to-all-done.1) | data formatting | bytes 524288 | tf_op jit(solution)/shard_map/all_to_all | solution.py:692
  101.6 6.4 %shard_map.201 = (bf16[1024,512]{1,0:T(8,128)(2,1)}, f32[8,128]{1,0:T(8,128)}) custom-call(s32[1,256]{1,0:T(1,128)} %refs_0_.6, f32[8,128]{1,0:T(8,128)} %get-tuple-element.44.refs_1_, bf16[1536,512]{1,0:T(8,128)(2,1)} %refs_2_.3, bf16[256,512]{1,0:T(8,128)(2,1)} %all_to_all.22.refs_3_, bf16[1024,512]{1,0:T(8,128)(2,1)} %get-tuple-element.46.refs_4_, ...), custom_call_target="tpu_custom_call" | custom-call | flops 1610612736 | bytes 1053696 | tf_op jit(solution)/shard_map/pallas_call | solution.py:500
  108.0 1.1 all-to-all-done.2.refs_0_
  109.9 2.4 %collective-permute-start.12 = (bf16[80,256]{1,0:T(8,128)(2,1)S(1)}, bf16[80,256]{1,0:T(8,128)(2,1)S(1)}, u32[]{:S(2)}, u32[]{:S(2)}) collective-permute-start(bf16[80,256]{1,0:T(8,128)(2,1)S(1)} %shard_map.205.refs_1_), channel_id=1, source_target_pairs={{0,192},{64,0},{128,64},{192,128},{1,193},{65,1},{129,65},{193,129... | collective-permute-start | bytes 122888 | tf_op jit(solution)/shard_map/ppermute | solution.py:623
  112.3 0.8 collective-permute-start.11
  113.1 0.9 collective-permute-start.10
  114.0 3.8 %collective-permute-done.11.refs_3_ = bf16[80,256]{1,0:T(8,128)(2,1)S(1)} collective-permute-done((bf16[80,256]{1,0:T(8,128)(2,1)S(1)}, bf16[80,256]{1,0:T(8,128)(2,1)S(1)}, u32[]{:S(2)}, u32[]{:S(2)}) %collective-permute-start.11) | collective-permute-done | bytes 40992 | tf_op jit(solution)/shard_map/ppermute | solution.py:623
  118.3 1.2 %shard_map.206 = (f32[24,512]{1,0:T(8,128)}, f32[8,512]{1,0:T(8,128)}, f32[16,512]{1,0:T(8,128)}, f32[8,512]{1,0:T(8,128)}, f32[8,512]{1,0:T(8,128)S(1)}) custom-call(s32[3]{0:T(128)S(1)} %copy-done.3, bf16[80,256]{1,0:T(8,128)(2,1)S(1)} %shard_map.205.refs_1_, bf16[80,256]{1,0:T(8,128)(2,1)S(1)} %collective-permute-done.10.refs_2_, ...), custom_call_target="tpu_custom_call" | custom-call | bytes 294924 | tf_op jit(solution)/shard_map/pallas_call | solution.py:500
  (27 shorter events, 6.2 us)
Async XLA Ops:
  0.6 1.2 %copy-start.1 = (bf16[1,1024,512]{2,1,0:T(8,128)(2,1)S(1)}, bf16[1,1024,512]{2,1,0:T(8,128)(2,1)}, u32[]{:S(2)}) copy-start(bf16[1,1024,512]{2,1,0:T(8,128)(2,1)} %param.14) | copy-start | bytes 3145732
  1.9 0.7 copy-start.4
  3.8 23.7 %all-to-all-start = ((bf16[64,4,512]{2,1,0:T(4,128)(2,1)}), bf16[64,4,512]{2,1,0:T(4,128)(2,1)S(1)}, u32[]{:S(2)}, u32[]{:S(2)}) async-start(bf16[64,4,512]{2,1,0:T(4,128)(2,1)} %all_to_all.17), calls=%async_computation | async-start | bytes 524288 | tf_op jit(solution)/shard_map/all_to_all | solution.py:648
  51.5 4.5 %collective-permute-start = (bf16[8,512,256]{2,1,0:T(8,128)(2,1)}, bf16[8,512,256]{2,1,0:T(8,128)(2,1)S(1)}, u32[]{:S(2)}, u32[]{:S(2)}) collective-permute-start(bf16[8,512,256]{2,1,0:T(8,128)(2,1)} %get-tuple-element.51), channel_id=1, source_target_pairs={{0,1},{1,0},{2,3},{3,2},{4,5},{5,4},{6,7},{7,6},{8,9},{9,8},{10,11... | collective-permute-start | bytes 6291464 | tf_op jit(solution)/shard_map/ppermute | solution.py:683
  56.0 1.6 %copy-start = (bf16[8,512,256]{2,1,0:T(8,128)(2,1)S(1)}, bf16[8,512,256]{2,1,0:T(8,128)(2,1)}, u32[]{:S(2)}) copy-start(bf16[8,512,256]{2,1,0:T(8,128)(2,1)} %get-tuple-element.50.refs_0_) | copy-start | bytes 6291460
  58.1 9.6 %collective-permute-start.4 = (bf16[512,256]{1,0:T(8,128)(2,1)S(1)}, bf16[512,256]{1,0:T(8,128)(2,1)S(1)}, u32[]{:S(2)}, u32[]{:S(2)}) collective-permute-start(bf16[512,256]{1,0:T(8,128)(2,1)S(1)} %get-tuple-element.57), channel_id=1, source_target_pairs={{0,64},{64,128},{128,192},{192,0},{1,65},{65,129},{129,193},{193,1... | collective-permute-start | bytes 786440 | tf_op jit(solution)/shard_map/ppermute | solution.py:623
  59.6 19.1 %collective-permute-start.5 = (bf16[512,256]{1,0:T(8,128)(2,1)S(1)}, bf16[512,256]{1,0:T(8,128)(2,1)S(1)}, u32[]{:S(2)}, u32[]{:S(2)}) collective-permute-start(bf16[512,256]{1,0:T(8,128)(2,1)S(1)} %get-tuple-element.58), channel_id=1, source_target_pairs={{0,128},{64,192},{128,0},{192,64},{1,129},{65,193},{129,1},{193,65... | collective-permute-start | bytes 786440 | tf_op jit(solution)/shard_map/ppermute | solution.py:623
  62.4 16.4 %collective-permute-start.6 = (bf16[512,256]{1,0:T(8,128)(2,1)S(1)}, bf16[512,256]{1,0:T(8,128)(2,1)S(1)}, u32[]{:S(2)}, u32[]{:S(2)}) collective-permute-start(bf16[512,256]{1,0:T(8,128)(2,1)S(1)} %get-tuple-element.59), channel_id=1, source_target_pairs={{0,192},{64,0},{128,64},{192,128},{1,193},{65,1},{129,65},{193,129... | collective-permute-start | bytes 786440 | tf_op jit(solution)/shard_map/ppermute | solution.py:623
  63.8 18.0 %collective-permute-start.1 = (bf16[512,256]{1,0:T(8,128)(2,1)S(1)}, bf16[512,256]{1,0:T(8,128)(2,1)S(1)}, u32[]{:S(2)}, u32[]{:S(2)}) collective-permute-start(bf16[512,256]{1,0:T(8,128)(2,1)S(1)} %get-tuple-element.53), channel_id=1, source_target_pairs={{0,16},{1,17},{2,18},{3,19},{4,20},{5,21},{6,22},{7,23},{8,24},{9,... | collective-permute-start | bytes 786440 | tf_op jit(solution)/shard_map/ppermute | solution.py:626
  65.4 18.5 %collective-permute-start.2 = (bf16[512,256]{1,0:T(8,128)(2,1)S(1)}, bf16[512,256]{1,0:T(8,128)(2,1)S(1)}, u32[]{:S(2)}, u32[]{:S(2)}) collective-permute-start(bf16[512,256]{1,0:T(8,128)(2,1)S(1)} %get-tuple-element.54), channel_id=1, source_target_pairs={{0,32},{1,33},{2,34},{3,35},{4,36},{5,37},{6,38},{7,39},{8,40},{9,... | collective-permute-start | bytes 786440 | tf_op jit(solution)/shard_map/ppermute | solution.py:626
  67.7 16.2 %collective-permute-start.3 = (bf16[512,256]{1,0:T(8,128)(2,1)S(1)}, bf16[512,256]{1,0:T(8,128)(2,1)S(1)}, u32[]{:S(2)}, u32[]{:S(2)}) collective-permute-start(bf16[512,256]{1,0:T(8,128)(2,1)S(1)} %get-tuple-element.55), channel_id=1, source_target_pairs={{0,48},{1,49},{2,50},{3,51},{4,52},{5,53},{6,54},{7,55},{8,56},{9,... | collective-permute-start | bytes 786440 | tf_op jit(solution)/shard_map/ppermute | solution.py:626
  70.4 19.8 %all-to-all-start.1 = ((bf16[64,4,512]{2,1,0:T(4,128)(2,1)}), bf16[64,4,512]{2,1,0:T(4,128)(2,1)}, u32[]{:S(2)}, u32[]{:S(2)}) async-start(bf16[64,4,512]{2,1,0:T(4,128)(2,1)} %all_to_all.20), calls=%async_computation.1 | async-start | bytes 524288 | tf_op jit(solution)/shard_map/all_to_all | solution.py:692
  78.9 5.0 %collective-permute-start.7 = (bf16[128,256]{1,0:T(8,128)(2,1)S(1)}, bf16[128,256]{1,0:T(8,128)(2,1)S(1)}, u32[]{:S(2)}, u32[]{:S(2)}) collective-permute-start(bf16[128,256]{1,0:T(8,128)(2,1)S(1)} %get-tuple-element.61), channel_id=1, source_target_pairs={{0,16},{1,17},{2,18},{3,19},{4,20},{5,21},{6,22},{7,23},{8,24},{9,... | collective-permute-start | bytes 196616 | tf_op jit(solution)/shard_map/ppermute | solution.py:626
  80.5 7.8 %collective-permute-start.8 = (bf16[128,256]{1,0:T(8,128)(2,1)S(1)}, bf16[128,256]{1,0:T(8,128)(2,1)S(1)}, u32[]{:S(2)}, u32[]{:S(2)}) collective-permute-start(bf16[128,256]{1,0:T(8,128)(2,1)S(1)} %get-tuple-element.62), channel_id=1, source_target_pairs={{0,32},{1,33},{2,34},{3,35},{4,36},{5,37},{6,38},{7,39},{8,40},{9,... | collective-permute-start | bytes 196616 | tf_op jit(solution)/shard_map/ppermute | solution.py:626
  81.8 6.7 %collective-permute-start.9 = (bf16[128,256]{1,0:T(8,128)(2,1)S(1)}, bf16[128,256]{1,0:T(8,128)(2,1)S(1)}, u32[]{:S(2)}, u32[]{:S(2)}) collective-permute-start(bf16[128,256]{1,0:T(8,128)(2,1)S(1)} %get-tuple-element.63), channel_id=1, source_target_pairs={{0,48},{1,49},{2,50},{3,51},{4,52},{5,53},{6,54},{7,55},{8,56},{9,... | collective-permute-start | bytes 196616 | tf_op jit(solution)/shard_map/ppermute | solution.py:626
  90.2 18.9 %all-to-all-start.2 = ((bf16[8,80,256]{2,1,0:T(8,128)(2,1)}), bf16[8,80,256]{2,1,0:T(8,128)(2,1)S(1)}, u32[]{:S(2)}, u32[]{:S(2)}) async-start(bf16[8,80,256]{2,1,0:T(8,128)(2,1)} %shard_map.204), calls=%async_computation.2 | async-start | bytes 655360 | tf_op jit(solution)/shard_map/all_to_all | solution.py:629
  101.6 16.7 %copy-start.3 = (s32[3]{0:T(128)S(1)}, s32[3]{0:T(128)}, u32[]{:S(2)}) copy-start(s32[3]{0:T(128)} %pad_add_fusion.refs_0_) | copy-start | bytes 40
  109.1 0.7 copy-start.2
  109.9 4.1 %collective-permute-start.12 = (bf16[80,256]{1,0:T(8,128)(2,1)S(1)}, bf16[80,256]{1,0:T(8,128)(2,1)S(1)}, u32[]{:S(2)}, u32[]{:S(2)}) collective-permute-start(bf16[80,256]{1,0:T(8,128)(2,1)S(1)} %shard_map.205.refs_1_), channel_id=1, source_target_pairs={{0,192},{64,0},{128,64},{192,128},{1,193},{65,1},{129,65},{193,129... | collective-permute-start | bytes 122888 | tf_op jit(solution)/shard_map/ppermute | solution.py:623
  112.3 5.5 %collective-permute-start.11 = (bf16[80,256]{1,0:T(8,128)(2,1)S(1)}, bf16[80,256]{1,0:T(8,128)(2,1)S(1)}, u32[]{:S(2)}, u32[]{:S(2)}) collective-permute-start(bf16[80,256]{1,0:T(8,128)(2,1)S(1)} %shard_map.205.refs_1_), channel_id=1, source_target_pairs={{0,128},{64,192},{128,0},{192,64},{1,129},{65,193},{129,1},{193,65... | collective-permute-start | bytes 122888 | tf_op jit(solution)/shard_map/ppermute | solution.py:623
  113.1 5.2 %collective-permute-start.10 = (bf16[80,256]{1,0:T(8,128)(2,1)S(1)}, bf16[80,256]{1,0:T(8,128)(2,1)S(1)}, u32[]{:S(2)}, u32[]{:S(2)}) collective-permute-start(bf16[80,256]{1,0:T(8,128)(2,1)S(1)} %shard_map.205.refs_1_), channel_id=1, source_target_pairs={{0,64},{64,128},{128,192},{192,0},{1,65},{65,129},{129,193},{193,1... | collective-permute-start | bytes 122888 | tf_op jit(solution)/shard_map/ppermute | solution.py:623

commit v5 on v4

--- a/solution.py
+++ b/solution.py
@@ -95,7 +95,7 @@
 def outgoing_kernel(rows_ref, node_ref, out_ref):
     nodes, halo = node_ref.shape[0], rows_ref.shape[1]
     spread = one_hot(rows_ref[...] == iota((nodes, halo), 0))
-    out_ref[...] = dot_lt(spread, node_ref[...]).astype(BF)
+    out_ref[...] = dot_lt(spread, node_ref[...]).reshape(out_ref.shape).astype(BF)
 
 
 def own_kernel(
@@ -211,18 +211,18 @@
 ):
     nodes, width = node.shape
     edges = begun.shape[0]
-    halo = incoming.shape[0]
+    halo = incoming.shape[0] * incoming.shape[1]
     columns_of(send_ref, send_cols)
     columns_of(recv_ref, recv_cols)
     halo_ref, w_send_ref, w_edge_out_ref = (
-        incoming.ready(),
+        incoming.ready()[...].astype(F32).reshape(halo, width).astype(BF),
         w_edge_send.ready(),
         w_edge_out.ready(),
     )
 
     def edge_body(start, i):
         here = pl.ds(start, BIG)
-        latent = dot(pick_rows(send_cols, start, BIG, nodes, halo), halo_ref[...])
+        latent = dot(pick_rows(send_cols, start, BIG, nodes, halo), halo_ref)
         first = begun.part(i)[here, :] + dot(latent.astype(BF), w_send_ref[...])
         squash = sigmoid(first)
         hidden = (first * squash).astype(BF)
@@ -295,12 +295,13 @@
 
         loop(out.shape[0], body, out.shape[0])
     sent, received = from_send.buffer, from_recv.buffer
-    outward.buffer[...] = dot_rt(sent[nodes : nodes + halo, :], w_send_ref[...]).astype(BF)
+    back = dot_rt(sent[nodes : nodes + halo, :], w_send_ref[...])
+    outward.buffer[...] = back.reshape(outward.shape).astype(BF)
     outward.send(0)
     edge_sum_out[...] = dot_lt(hidden_ref[...], grad_second[...])
     edge_sum_in[0:width, :] = dot(edge_turned.ready()[...], first_ref[...])
     edge_sum_in[width : 2 * width, :] = dot(node_turned_ref[...], sent[0:nodes, :]) + dot_lt(
-        halo_ref[...], sent[nodes : nodes + halo, :]
+        halo_ref, sent[nodes : nodes + halo, :]
     )
     edge_sum_in[2 * width : 3 * width, :] = dot(node_turned_ref[...], received[...])
     each = width // patches
@@ -334,15 +335,16 @@
     token.buffer[...] = jnp.zeros(token.shape, F32)
     token.send(0)
     nodes, width = acc.shape
-    halo = returned.shape[0]
-    w_ref, returned_ref = w_both.ready(), returned.ready()
+    halo = returned.shape[0] * returned.shape[1]
+    w_ref = w_both.ready()
+    returned_ref = returned.ready()[...].astype(F32).reshape(halo, width).astype(BF)
 
     def body(start, i):
         here = pl.ds(start, ROWS)
         spread = one_hot(rows_ref[...] == iota((ROWS, halo), 0) + start)
         out.buffer[here, :] = (
             acc.part(i)[here, :].astype(F32)
-            + dot(spread, returned_ref[...])
+            + dot(spread, returned_ref)
             + dot_rt(from_send.part(i)[here, :], w_ref[0:width, :])
             + dot_rt(from_recv.part(i)[here, :], w_ref[width : 2 * width, :])
         ).astype(BF)
@@ -537,7 +539,7 @@
     w_node_out,
 ):
     nodes, width = node.shape
-    edges, halo = e_cot.shape[0], incoming.shape[0]
+    edges, halo = e_cot.shape[0], incoming.shape[0] * incoming.shape[1]
 
     def wide(rows, kind=BF, step=ROWS):
         return ((rows, width), kind, rows // step)
@@ -578,7 +580,7 @@
             wide(edges, BF, BIG),
             wide(nodes + halo, BF, nodes + halo),
             wide(nodes, BF, nodes),
-            ((halo, width), BF, 1),
+            ((patches, halo // patches, width), BF, 1),
             piece,
             piece,
         ],
@@ -640,7 +642,7 @@
 
     outgoing = call(
         outgoing_kernel,
-        [((halo, width), BF)],
+        [((patches, halo // patches, width), BF)],
         [send_rows, node],
         flops=2 * halo * nodes * width,
         limit=16 * 2**20,
@@ -681,15 +683,6 @@
         w_node_out,
     )
     got = lax.ppermute(send, "patch", twins)
-    sums = call(pair_kernel, [(keep.shape[1:], BF)] * 8, [keep, got])
-    columns = [sums[0]] + [to_column(sums[s], s) for s in range(1, 4)]
-    rights = call(
-        right_kernel,
-        [((depth * rows // 4, half), BF)] * 4,
-        [sums[4]] + [to_member(sums[4 + s], s) for s in range(1, 4)],
-    )
-    columns += [rights[0]] + [to_column(rights[s], s) for s in range(1, 4)]
-    returned = lax.all_to_all(outward, "patch", split_axis=0, concat_axis=0, tiled=True)
     edge_grad, edge_token = call(
         edge_grad_kernel,
         [],
@@ -700,6 +693,15 @@
         store=[wide(edges), TOKEN],
         limit=FULL,
     )
+    sums = call(pair_kernel, [(keep.shape[1:], BF)] * 8, [keep, got], after=[edge_token])
+    columns = [sums[0]] + [to_column(sums[s], s) for s in range(1, 4)]
+    rights = call(
+        right_kernel,
+        [((depth * rows // 4, half), BF)] * 4,
+        [sums[4]] + [to_member(sums[4 + s], s) for s in range(1, 4)],
+    )
+    columns += [rights[0]] + [to_column(rights[s], s) for s in range(1, 4)]
+    returned = lax.all_to_all(outward, "patch", split_axis=0, concat_axis=0, tiled=True)
     blocks = call(
         four_kernel,
         [((depth, rows + rows // 4, half), BF)],
@@ -721,7 +723,6 @@
         ],
         store=[wide(nodes), TOKEN],
         limit=FULL,
-        after=[edge_token],
     )
     mine = call(
         depth_kernel,

time: 121 us -> 120 us (level)
  local copies, waits for them, and re-layouts: 9.73 us -> 4.57 us
  Pallas kernels: 45.5 us -> 48.2 us
  waiting for transfers between devices: 17.8 us -> 19.7 us
    all_to_all x1, waiting for transfers between devices: 1.14 us -> 6.93 us  [along_depth(): return lax.all_to_all(x, 'patch', 0, 0, axis_index_groups=lines, tiled=True)]
    all_to_all x4 -> x0, local copies, waits for them, and re-layouts: 4.96 us -> none  [the longest x2 3.43 us: local(): lax.all_to_all(outward, 'patch', split_axis=0, concat_axis=0, tiled=True)]
    ppermute x1, waiting for transfers between devices: 4.22 us -> 0.22 us  [local(): got = lax.ppermute(send, 'patch', twins)]
    pallas_call x10, Pallas kernels: 45.5 us -> 48.2 us  [call(): pl.pallas_call(body, out_shape=shapes[0] if single else shapes, in_specs=...]
    unnamed x10 -> x14, local copies, waits for them, and re-layouts: 4.18 us -> 3.97 us
where the time goes in v5:
time: 120 us
  Pallas kernels  48.2 us (40%)
  starting transfers between devices  45.2 us (38%)
  waiting for transfers between devices  19.7 us (16%)
  local copies, waits for them, and re-layouts  4.57 us (4%)
  between operations  1.42 us (1%)
    pallas_call x10, Pallas kernels, call(): pl.pallas_call(body, out_shape=shapes[0] if single else shapes, in_specs=...  48.2 us
    all_to_all x1, starting transfers between devices, local(): lax.all_to_all(outgoing, 'patch', split_axis=0, concat_axis=0, tiled=True)  12.1 us
    ppermute x6, starting transfers between devices, to_member(): lax.ppermute(x, 'group', [(g, (g + shift) % members) for g in range(membe...  9.68 us
    ppermute x6, starting transfers between devices, to_column(): lax.ppermute(x, 'patch', [(i, (i + shift * column) % patches) for i in ra...  8.9 us
    all_to_all x1, starting transfers between devices, local(): lax.all_to_all(outward, 'patch', split_axis=0, concat_axis=0, tiled=True)  8.62 us
    all_to_all x1, waiting for transfers between devices, along_depth(): return lax.all_to_all(x, 'patch', 0, 0, axis_index_groups=lines, tiled=True)  6.93 us
    all_to_all x1, starting transfers between devices, along_depth(): return lax.all_to_all(x, 'patch', 0, 0, axis_index_groups=lines, tiled=True)  5.65 us
    ppermute x6, waiting for transfers between devices, to_member(): lax.ppermute(x, 'group', [(g, (g + shift) % members) for g in range(membe...  5.33 us
  transfers between devices with their start and end apart: 16, of which 9 were waited for; matrix products, arithmetic and copies ran while one was open for 0% of the time, Pallas kernels for 17%

profile of v5, /device:TPU:8, one launch (start us, length us, event | category | flops | bytes accessed | tf_op | source)
XLA Modules:
  0.0 119.7 jit_solution(4521606567415107138)
XLA Ops:
  0.6 1.2 %copy-done.1 = bf16[1,1024,512]{2,1,0:T(8,128)(2,1)S(1)} copy-done((bf16[1,1024,512]{2,1,0:T(8,128)(2,1)S(1)}, bf16[1,1024,512]{2,1,0:T(8,128)(2,1)}, u32[]{:S(2)}) %copy-start.1) | copy-done | bytes 1048600
  2.5 1.2 shard_map.197
  3.7 12.1 %all-to-all-start = ((bf16[64,4,512]{2,1,0:T(4,128)(2,1)}), bf16[64,4,512]{2,1,0:T(4,128)(2,1)S(1)}, u32[]{:S(2)}, u32[]{:S(2)}) async-start(bf16[64,4,512]{2,1,0:T(4,128)(2,1)} %shard_map.197), calls=%async_computation | async-start | bytes 524288 | tf_op jit(solution)/shard_map/all_to_all | solution.py:650
  17.1 8.5 %shard_map.198 = (bf16[512,1024]{1,0:T(8,128)(2,1)}, bf16[512,1024]{1,0:T(8,128)(2,1)}, f32[1024,512]{1,0:T(8,128)}) custom-call(s32[8,128]{1,0:T(8,128)} %refs_2_.1, s32[8,128]{1,0:T(8,128)} %refs_3_.1, bf16[1024,512]{1,0:T(8,128)(2,1)} %bitcast.15, bf16[1024,512]{1,0:T(8,128)(2,1)} %bitcast.20, bf16[1536,512]{1,0:T(8,128)(2,1)} %refs_1_.6), custom_call_target="tpu_custom_call" | custom-call | flops 3758096384 | bytes 4202496 | tf_op jit(solution)/shard_map/pallas_call | solution.py:502
  25.6 1.8 %all-to-all-done.refs_6_ = bf16[64,4,512]{2,1,0:T(4,128)(2,1)S(1)} async-done(((bf16[64,4,512]{2,1,0:T(4,128)(2,1)}), bf16[64,4,512]{2,1,0:T(4,128)(2,1)S(1)}, u32[]{:S(2)}, u32[]{:S(2)}) %all-to-all-start) | async-done | bytes 262176 | tf_op jit(solution)/shard_map/all_to_all | solution.py:650
  27.4 0.7 copy-done.6
  28.1 23.4 %shard_map.199 = (bf16[1024,512]{1,0:T(8,128)(2,1)}, bf16[1024,512]{1,0:T(8,128)(2,1)}, bf16[1280,512]{1,0:T(8,128)(2,1)}, bf16[1024,512]{1,0:T(8,128)(2,1)}, bf...) custom-call(s32[3]{0:T(128)} %pad_add_fusion.refs_0_, ...), custom_call_target="tpu_custom_call" | custom-call | flops 13958643712 | bytes 8925200 | tf_op jit(solution)/shard_map/pallas_call | solution.py:502
  51.7 4.1 %shard_map.200 = (bf16[1024,512]{1,0:T(8,128)(2,1)}, f32[8,128]{1,0:T(8,128)}) custom-call(s32[1]{0:T(128)S(6)} %copy.22.refs_1_.refs_0_, bf16[1536,512]{1,0:T(8,128)(2,1)} %refs_1_.6, bf16[1024,512]{1,0:T(8,128)(2,1)} %get-tuple-element.42.refs_2_, bf16[1024,512]{1,0:T(8,128)(2,1)} %bitcast.19), custom_call_target="tpu_custom_call" | custom-call | flops 536870912 | bytes 1052676 | tf_op jit(solution)/shard_map/pallas_call | solution.py:502
  56.1 0.7 copy-done.2
  56.7 2.4 %shard_map.202 = (bf16[512,256]{1,0:T(8,128)(2,1)S(1)}, bf16[512,256]{1,0:T(8,128)(2,1)S(1)}, bf16[512,256]{1,0:T(8,128)(2,1)S(1)}, bf16[512,256]{1,0:T(8,128)(2...) custom-call(bf16[8,512,256]{2,1,0:T(8,128)(2,1)S(1)} %copy-done, ...), custom_call_target="tpu_custom_call" | custom-call | bytes 6291456 | tf_op jit(solution)/shard_map/pallas_call | solution.py:502
  59.2 1.5 %collective-permute-start.4 = (bf16[512,256]{1,0:T(8,128)(2,1)S(1)}, bf16[512,256]{1,0:T(8,128)(2,1)S(1)}, u32[]{:S(2)}, u32[]{:S(2)}) collective-permute-start(bf16[512,256]{1,0:T(8,128)(2,1)S(1)} %get-tuple-element.57), channel_id=1, source_target_pairs={{0,64},{64,128},{128,192},{192,0},{1,65},{65,129},{129,193},{193,1... | collective-permute-start | bytes 786440 | tf_op jit(solution)/shard_map/ppermute | solution.py:625
  60.7 2.7 %collective-permute-start.5 = (bf16[512,256]{1,0:T(8,128)(2,1)}, bf16[512,256]{1,0:T(8,128)(2,1)S(1)}, u32[]{:S(2)}, u32[]{:S(2)}) collective-permute-start(bf16[512,256]{1,0:T(8,128)(2,1)} %get-tuple-element.58), channel_id=1, source_target_pairs={{0,128},{64,192},{128,0},{192,64},{1,129},{65,193},{129,1},{193,65... | collective-permute-start | bytes 786440 | tf_op jit(solution)/shard_map/ppermute | solution.py:625
  63.4 1.4 %collective-permute-start.6 = (bf16[512,256]{1,0:T(8,128)(2,1)S(1)}, bf16[512,256]{1,0:T(8,128)(2,1)S(1)}, u32[]{:S(2)}, u32[]{:S(2)}) collective-permute-start(bf16[512,256]{1,0:T(8,128)(2,1)S(1)} %get-tuple-element.59), channel_id=1, source_target_pairs={{0,192},{64,0},{128,64},{192,128},{1,193},{65,1},{129,65},{193,129... | collective-permute-start | bytes 786440 | tf_op jit(solution)/shard_map/ppermute | solution.py:625
  64.8 1.6 %collective-permute-start.1 = (bf16[512,256]{1,0:T(8,128)(2,1)S(1)}, bf16[512,256]{1,0:T(8,128)(2,1)S(1)}, u32[]{:S(2)}, u32[]{:S(2)}) collective-permute-start(bf16[512,256]{1,0:T(8,128)(2,1)S(1)} %get-tuple-element.53), channel_id=1, source_target_pairs={{0,16},{1,17},{2,18},{3,19},{4,20},{5,21},{6,22},{7,23},{8,24},{9,... | collective-permute-start | bytes 786440 | tf_op jit(solution)/shard_map/ppermute | solution.py:628
  66.4 1.4 %collective-permute-start.2 = (bf16[512,256]{1,0:T(8,128)(2,1)S(1)}, bf16[512,256]{1,0:T(8,128)(2,1)S(1)}, u32[]{:S(2)}, u32[]{:S(2)}) collective-permute-start(bf16[512,256]{1,0:T(8,128)(2,1)S(1)} %get-tuple-element.54), channel_id=1, source_target_pairs={{0,32},{1,33},{2,34},{3,35},{4,36},{5,37},{6,38},{7,39},{8,40},{9,... | collective-permute-start | bytes 786440 | tf_op jit(solution)/shard_map/ppermute | solution.py:628
  67.8 1.0 collective-permute-done.4.refs_1_
  68.8 0.9 collective-permute-start.3
  69.7 8.6 %all-to-all-start.1 = ((bf16[64,4,512]{2,1,0:T(4,128)(2,1)}), bf16[64,4,512]{2,1,0:T(4,128)(2,1)}, u32[]{:S(2)}, u32[]{:S(2)}) async-start(bf16[64,4,512]{2,1,0:T(4,128)(2,1)} %get-tuple-element.44), calls=%async_computation.1 | async-start | bytes 524288 | tf_op jit(solution)/shard_map/all_to_all | solution.py:704
  78.5 1.6 %collective-permute-start.7 = (bf16[128,256]{1,0:T(8,128)(2,1)S(1)}, bf16[128,256]{1,0:T(8,128)(2,1)S(1)}, u32[]{:S(2)}, u32[]{:S(2)}) collective-permute-start(bf16[128,256]{1,0:T(8,128)(2,1)S(1)} %get-tuple-element.61), channel_id=1, source_target_pairs={{0,16},{1,17},{2,18},{3,19},{4,20},{5,21},{6,22},{7,23},{8,24},{9,... | collective-permute-start | bytes 196616 | tf_op jit(solution)/shard_map/ppermute | solution.py:628
  80.2 1.0 collective-permute-start.8
  81.2 2.3 %collective-permute-start.9 = (bf16[128,256]{1,0:T(8,128)(2,1)S(1)}, bf16[128,256]{1,0:T(8,128)(2,1)S(1)}, u32[]{:S(2)}, u32[]{:S(2)}) collective-permute-start(bf16[128,256]{1,0:T(8,128)(2,1)S(1)} %get-tuple-element.63), channel_id=1, source_target_pairs={{0,48},{1,49},{2,50},{3,51},{4,52},{5,53},{6,54},{7,55},{8,56},{9,... | collective-permute-start | bytes 196616 | tf_op jit(solution)/shard_map/ppermute | solution.py:628
  83.5 4.4 %collective-permute-done.8.refs_6_ = bf16[128,256]{1,0:T(8,128)(2,1)S(1)} collective-permute-done((bf16[128,256]{1,0:T(8,128)(2,1)S(1)}, bf16[128,256]{1,0:T(8,128)(2,1)S(1)}, u32[]{:S(2)}, u32[]{:S(2)}) %collective-permute-start.8) | collective-permute-done | bytes 65568 | tf_op jit(solution)/shard_map/ppermute | solution.py:628
  88.1 0.9 shard_map.204
  89.0 0.8 all-to-all-done.1.refs_2_
  89.8 5.7 %all-to-all-start.2 = ((bf16[8,80,256]{2,1,0:T(8,128)(2,1)}), bf16[8,80,256]{2,1,0:T(8,128)(2,1)S(1)}, u32[]{:S(2)}, u32[]{:S(2)}) async-start(bf16[8,80,256]{2,1,0:T(8,128)(2,1)} %shard_map.204), calls=%async_computation.2 | async-start | bytes 655360 | tf_op jit(solution)/shard_map/all_to_all | solution.py:631
  95.5 6.3 %shard_map.201 = (bf16[1024,512]{1,0:T(8,128)(2,1)}, f32[8,128]{1,0:T(8,128)}) custom-call(s32[1,256]{1,0:T(1,128)} %refs_0_.6, bf16[1536,512]{1,0:T(8,128)(2,1)} %refs_1_.6, bf16[64,4,512]{2,1,0:T(4,128)(2,1)} %all-to-all-done.1.refs_2_, bf16[1024,512]{1,0:T(8,128)(2,1)} %get-tuple-element.45.refs_3_, bf16[1280,512]{1,0:T(8,128)(2,1)} %get-tuple-element.46.refs_4_, ...), custom_call_target="tpu_custom_call" | custom-call | flops 1610612736 | bytes 1053696 | tf_op jit(solution)/shard_map/pallas_call | solution.py:502
  101.8 6.9 %all-to-all-done.2.refs_0_ = bf16[8,80,256]{2,1,0:T(8,128)(2,1)S(1)} async-done(((bf16[8,80,256]{2,1,0:T(8,128)(2,1)}), bf16[8,80,256]{2,1,0:T(8,128)(2,1)S(1)}, u32[]{:S(2)}, u32[]{:S(2)}) %all-to-all-start.2) | async-done | bytes 327712 | tf_op jit(solution)/shard_map/all_to_all | solution.py:631
  109.5 2.3 %collective-permute-start.12 = (bf16[80,256]{1,0:T(8,128)(2,1)S(1)}, bf16[80,256]{1,0:T(8,128)(2,1)S(1)}, u32[]{:S(2)}, u32[]{:S(2)}) collective-permute-start(bf16[80,256]{1,0:T(8,128)(2,1)S(1)} %shard_map.205.refs_1_), channel_id=1, source_target_pairs={{0,192},{64,0},{128,64},{192,128},{1,193},{65,1},{129,65},{193,129... | collective-permute-start | bytes 122888 | tf_op jit(solution)/shard_map/ppermute | solution.py:625
  111.8 0.8 collective-permute-start.11
  112.6 0.9 collective-permute-start.10
  113.5 3.8 %collective-permute-done.11.refs_3_ = bf16[80,256]{1,0:T(8,128)(2,1)S(1)} collective-permute-done((bf16[80,256]{1,0:T(8,128)(2,1)S(1)}, bf16[80,256]{1,0:T(8,128)(2,1)S(1)}, u32[]{:S(2)}, u32[]{:S(2)}) %collective-permute-start.11) | collective-permute-done | bytes 40992 | tf_op jit(solution)/shard_map/ppermute | solution.py:625
  117.8 1.2 %shard_map.206 = (f32[24,512]{1,0:T(8,128)}, f32[8,512]{1,0:T(8,128)}, f32[16,512]{1,0:T(8,128)}, f32[8,512]{1,0:T(8,128)}, f32[8,512]{1,0:T(8,128)S(1)}) custom-call(s32[3]{0:T(128)S(1)} %copy-done.4, bf16[80,256]{1,0:T(8,128)(2,1)S(1)} %shard_map.205.refs_1_, bf16[80,256]{1,0:T(8,128)(2,1)S(1)} %collective-permute-done.10.refs_2_, ...), custom_call_target="tpu_custom_call" | custom-call | bytes 294924 | tf_op jit(solution)/shard_map/pallas_call | solution.py:502
  (27 shorter events, 4.0 us)
Async XLA Ops:
  0.6 1.2 %copy-start.1 = (bf16[1,1024,512]{2,1,0:T(8,128)(2,1)S(1)}, bf16[1,1024,512]{2,1,0:T(8,128)(2,1)}, u32[]{:S(2)}) copy-start(bf16[1,1024,512]{2,1,0:T(8,128)(2,1)} %param.14) | copy-start | bytes 3145732
  1.9 0.7 copy-start.5
  3.7 23.7 %all-to-all-start = ((bf16[64,4,512]{2,1,0:T(4,128)(2,1)}), bf16[64,4,512]{2,1,0:T(4,128)(2,1)S(1)}, u32[]{:S(2)}, u32[]{:S(2)}) async-start(bf16[64,4,512]{2,1,0:T(4,128)(2,1)} %shard_map.197), calls=%async_computation | async-start | bytes 524288 | tf_op jit(solution)/shard_map/all_to_all | solution.py:650
  27.4 0.7 copy-start.6
  51.5 4.6 %copy-start = (bf16[8,512,256]{2,1,0:T(8,128)(2,1)S(1)}, bf16[8,512,256]{2,1,0:T(8,128)(2,1)}, u32[]{:S(2)}) copy-start(bf16[8,512,256]{2,1,0:T(8,128)(2,1)} %get-tuple-element.49.refs_0_) | copy-start | bytes 6291460
  51.5 4.6 %collective-permute-start = (bf16[8,512,256]{2,1,0:T(8,128)(2,1)}, bf16[8,512,256]{2,1,0:T(8,128)(2,1)}, u32[]{:S(2)}, u32[]{:S(2)}) collective-permute-start(bf16[8,512,256]{2,1,0:T(8,128)(2,1)} %get-tuple-element.50), channel_id=1, source_target_pairs={{0,1},{1,0},{2,3},{3,2},{4,5},{5,4},{6,7},{7,6},{8,9},{9,8},{10,11... | collective-permute-start | bytes 6291464 | tf_op jit(solution)/shard_map/ppermute | solution.py:685
  56.1 0.7 copy-start.2
  59.2 9.6 %collective-permute-start.4 = (bf16[512,256]{1,0:T(8,128)(2,1)S(1)}, bf16[512,256]{1,0:T(8,128)(2,1)S(1)}, u32[]{:S(2)}, u32[]{:S(2)}) collective-permute-start(bf16[512,256]{1,0:T(8,128)(2,1)S(1)} %get-tuple-element.57), channel_id=1, source_target_pairs={{0,64},{64,128},{128,192},{192,0},{1,65},{65,129},{129,193},{193,1... | collective-permute-start | bytes 786440 | tf_op jit(solution)/shard_map/ppermute | solution.py:625
  60.7 17.7 %collective-permute-start.5 = (bf16[512,256]{1,0:T(8,128)(2,1)}, bf16[512,256]{1,0:T(8,128)(2,1)S(1)}, u32[]{:S(2)}, u32[]{:S(2)}) collective-permute-start(bf16[512,256]{1,0:T(8,128)(2,1)} %get-tuple-element.58), channel_id=1, source_target_pairs={{0,128},{64,192},{128,0},{192,64},{1,129},{65,193},{129,1},{193,65... | collective-permute-start | bytes 786440 | tf_op jit(solution)/shard_map/ppermute | solution.py:625
  63.4 15.0 %collective-permute-start.6 = (bf16[512,256]{1,0:T(8,128)(2,1)S(1)}, bf16[512,256]{1,0:T(8,128)(2,1)S(1)}, u32[]{:S(2)}, u32[]{:S(2)}) collective-permute-start(bf16[512,256]{1,0:T(8,128)(2,1)S(1)} %get-tuple-element.59), channel_id=1, source_target_pairs={{0,192},{64,0},{128,64},{192,128},{1,193},{65,1},{129,65},{193,129... | collective-permute-start | bytes 786440 | tf_op jit(solution)/shard_map/ppermute | solution.py:625
  64.8 16.4 %collective-permute-start.1 = (bf16[512,256]{1,0:T(8,128)(2,1)S(1)}, bf16[512,256]{1,0:T(8,128)(2,1)S(1)}, u32[]{:S(2)}, u32[]{:S(2)}) collective-permute-start(bf16[512,256]{1,0:T(8,128)(2,1)S(1)} %get-tuple-element.53), channel_id=1, source_target_pairs={{0,16},{1,17},{2,18},{3,19},{4,20},{5,21},{6,22},{7,23},{8,24},{9,... | collective-permute-start | bytes 786440 | tf_op jit(solution)/shard_map/ppermute | solution.py:628
  66.4 17.1 %collective-permute-start.2 = (bf16[512,256]{1,0:T(8,128)(2,1)S(1)}, bf16[512,256]{1,0:T(8,128)(2,1)S(1)}, u32[]{:S(2)}, u32[]{:S(2)}) collective-permute-start(bf16[512,256]{1,0:T(8,128)(2,1)S(1)} %get-tuple-element.54), channel_id=1, source_target_pairs={{0,32},{1,33},{2,34},{3,35},{4,36},{5,37},{6,38},{7,39},{8,40},{9,... | collective-permute-start | bytes 786440 | tf_op jit(solution)/shard_map/ppermute | solution.py:628
  68.8 14.7 %collective-permute-start.3 = (bf16[512,256]{1,0:T(8,128)(2,1)S(1)}, bf16[512,256]{1,0:T(8,128)(2,1)S(1)}, u32[]{:S(2)}, u32[]{:S(2)}) collective-permute-start(bf16[512,256]{1,0:T(8,128)(2,1)S(1)} %get-tuple-element.55), channel_id=1, source_target_pairs={{0,48},{1,49},{2,50},{3,51},{4,52},{5,53},{6,54},{7,55},{8,56},{9,... | collective-permute-start | bytes 786440 | tf_op jit(solution)/shard_map/ppermute | solution.py:628
  69.7 20.1 %all-to-all-start.1 = ((bf16[64,4,512]{2,1,0:T(4,128)(2,1)}), bf16[64,4,512]{2,1,0:T(4,128)(2,1)}, u32[]{:S(2)}, u32[]{:S(2)}) async-start(bf16[64,4,512]{2,1,0:T(4,128)(2,1)} %get-tuple-element.44), calls=%async_computation.1 | async-start | bytes 524288 | tf_op jit(solution)/shard_map/all_to_all | solution.py:704
  78.5 5.0 %collective-permute-start.7 = (bf16[128,256]{1,0:T(8,128)(2,1)S(1)}, bf16[128,256]{1,0:T(8,128)(2,1)S(1)}, u32[]{:S(2)}, u32[]{:S(2)}) collective-permute-start(bf16[128,256]{1,0:T(8,128)(2,1)S(1)} %get-tuple-element.61), channel_id=1, source_target_pairs={{0,16},{1,17},{2,18},{3,19},{4,20},{5,21},{6,22},{7,23},{8,24},{9,... | collective-permute-start | bytes 196616 | tf_op jit(solution)/shard_map/ppermute | solution.py:628
  80.2 7.8 %collective-permute-start.8 = (bf16[128,256]{1,0:T(8,128)(2,1)S(1)}, bf16[128,256]{1,0:T(8,128)(2,1)S(1)}, u32[]{:S(2)}, u32[]{:S(2)}) collective-permute-start(bf16[128,256]{1,0:T(8,128)(2,1)S(1)} %get-tuple-element.62), channel_id=1, source_target_pairs={{0,32},{1,33},{2,34},{3,35},{4,36},{5,37},{6,38},{7,39},{8,40},{9,... | collective-permute-start | bytes 196616 | tf_op jit(solution)/shard_map/ppermute | solution.py:628
  81.2 7.0 %collective-permute-start.9 = (bf16[128,256]{1,0:T(8,128)(2,1)S(1)}, bf16[128,256]{1,0:T(8,128)(2,1)S(1)}, u32[]{:S(2)}, u32[]{:S(2)}) collective-permute-start(bf16[128,256]{1,0:T(8,128)(2,1)S(1)} %get-tuple-element.63), channel_id=1, source_target_pairs={{0,48},{1,49},{2,50},{3,51},{4,52},{5,53},{6,54},{7,55},{8,56},{9,... | collective-permute-start | bytes 196616 | tf_op jit(solution)/shard_map/ppermute | solution.py:628
  89.8 18.9 %all-to-all-start.2 = ((bf16[8,80,256]{2,1,0:T(8,128)(2,1)}), bf16[8,80,256]{2,1,0:T(8,128)(2,1)S(1)}, u32[]{:S(2)}, u32[]{:S(2)}) async-start(bf16[8,80,256]{2,1,0:T(8,128)(2,1)} %shard_map.204), calls=%async_computation.2 | async-start | bytes 655360 | tf_op jit(solution)/shard_map/all_to_all | solution.py:631
  95.5 22.4 %copy-start.4 = (s32[3]{0:T(128)S(1)}, s32[3]{0:T(128)}, u32[]{:S(2)}) copy-start(s32[3]{0:T(128)} %pad_add_fusion.refs_0_) | copy-start | bytes 40
  108.7 0.7 copy-start.3
  109.5 4.1 %collective-permute-start.12 = (bf16[80,256]{1,0:T(8,128)(2,1)S(1)}, bf16[80,256]{1,0:T(8,128)(2,1)S(1)}, u32[]{:S(2)}, u32[]{:S(2)}) collective-permute-start(bf16[80,256]{1,0:T(8,128)(2,1)S(1)} %shard_map.205.refs_1_), channel_id=1, source_target_pairs={{0,192},{64,0},{128,64},{192,128},{1,193},{65,1},{129,65},{193,129... | collective-permute-start | bytes 122888 | tf_op jit(solution)/shard_map/ppermute | solution.py:625
  111.8 5.5 %collective-permute-start.11 = (bf16[80,256]{1,0:T(8,128)(2,1)S(1)}, bf16[80,256]{1,0:T(8,128)(2,1)S(1)}, u32[]{:S(2)}, u32[]{:S(2)}) collective-permute-start(bf16[80,256]{1,0:T(8,128)(2,1)S(1)} %shard_map.205.refs_1_), channel_id=1, source_target_pairs={{0,128},{64,192},{128,0},{192,64},{1,129},{65,193},{129,1},{193,65... | collective-permute-start | bytes 122888 | tf_op jit(solution)/shard_map/ppermute | solution.py:625
  112.6 5.2 %collective-permute-start.10 = (bf16[80,256]{1,0:T(8,128)(2,1)S(1)}, bf16[80,256]{1,0:T(8,128)(2,1)S(1)}, u32[]{:S(2)}, u32[]{:S(2)}) collective-permute-start(bf16[80,256]{1,0:T(8,128)(2,1)S(1)} %shard_map.205.refs_1_), channel_id=1, source_target_pairs={{0,64},{64,128},{128,192},{192,0},{1,65},{65,129},{129,193},{193,1... | collective-permute-start | bytes 122888 | tf_op jit(solution)/shard_map/ppermute | solution.py:625

commit v6 on v5

--- a/solution.py
+++ b/solution.py
@@ -102,8 +102,8 @@
     send_ref,
     recv_ref,
     node,
+    w_edge,
     edge,
-    w_edge,
     node_turned,
     edge_turned,
     begun,
@@ -113,21 +113,22 @@
     nodes, width = node.shape
     columns_of(send_ref, send_cols)
     columns_of(recv_ref, recv_cols)
-    node_ref, edge_ref, w_ref = node.ready(), edge.ready(), w_edge.ready()
+    node_ref = node.ready()
 
     def body(start, i):
         here = pl.ds(start, BIG)
         from_send = dot(pick_rows(send_cols, start, BIG, 0, nodes), node_ref[...]).astype(BF)
         from_recv = dot(pick_rows(recv_cols, start, BIG, 0, nodes), node_ref[...]).astype(BF)
-        begun.buffer[here, :] = (
-            dot(edge_ref[here, :], w_ref[0:width, :])
-            + dot(from_send, w_ref[width : 2 * width, :])
-            + dot(from_recv, w_ref[2 * width : 3 * width, :])
+        w_ref = w_edge.ready()
+        found = dot(from_send, w_ref[width : 2 * width, :]) + dot(
+            from_recv, w_ref[2 * width : 3 * width, :]
         )
+        edge_ref = edge.ready()
+        begun.buffer[here, :] = found + dot(edge_ref[here, :], w_ref[0:width, :])
         begun.send(i)
 
-    loop(edge_ref.shape[0], body, BIG)
-    for source, out in ((node_ref, node_turned), (edge_ref, edge_turned)):
+    loop(edge.shape[0], body, edge.shape[0])
+    for source, out in ((node_ref, node_turned), (edge.buffer, edge_turned)):
         for i in range(0, source.shape[0], BIG):
             out.buffer[:, i : i + BIG] = source[i : i + BIG, :].T
         out.send(0)
@@ -184,7 +185,7 @@
     node_turned,
     edge_cot,
     edge_turned,
-    node_acc,
+    grad_first,
     first_out,
     from_send,
     from_recv,
@@ -201,7 +202,7 @@
     gathered,
     node_hidden,
     grad_second,
-    grad_first,
+    spread_recv,
     back_ref,
     gains,
     sum_in,
@@ -223,7 +224,8 @@
     def edge_body(start, i):
         here = pl.ds(start, BIG)
         latent = dot(pick_rows(send_cols, start, BIG, nodes, halo), halo_ref)
-        first = begun.part(i)[here, :] + dot(latent.astype(BF), w_send_ref[...])
+        more = dot(latent.astype(BF), w_send_ref[...])
+        first = begun.part(i)[here, :] + more
         squash = sigmoid(first)
         hidden = (first * squash).astype(BF)
         hidden_ref[here, :] = hidden
@@ -240,7 +242,9 @@
 
     def node_body(start, i):
         here = pl.ds(start, BIG)
-        taken = dot(spread_rows(recv_ref, start, BIG), message[...]).astype(BF)
+        spread = spread_rows(recv_ref, start, BIG)
+        spread_recv[here, :] = spread
+        taken = dot(spread, message[...]).astype(BF)
         gathered[here, :] = taken
         first = dot(node_ref[here, :], w_node_ref[0:width, :]) + dot(
             taken, w_node_ref[width : 2 * width, :]
@@ -255,16 +259,15 @@
         second = normalize_back(upstream * gain_node_ref[...], normed, inverse).astype(BF)
         grad_second[here, :] = second
         grad = (dot_rt(second, w_node_out_ref[...]) * slope).astype(BF)
-        grad_first[here, :] = grad
-        node_acc.buffer[here, :] = (upstream + dot_rt(grad, w_node_ref[0:width, :])).astype(BF)
+        grad_first.buffer[here, :] = grad
         back_ref[here, :] = dot_rt(grad, w_node_ref[width : 2 * width, :]).astype(BF)
-        node_acc.send(i)
+        grad_first.send(i)
 
     loop(nodes, node_body, BIG)
     node_turned_ref = node_turned.ready()
     sum_out[...] = dot_lt(node_hidden[...], grad_second[...])
-    sum_in[0:width, :] = dot(node_turned_ref[...], grad_first[...])
-    sum_in[width : 2 * width, :] = dot_lt(gathered[...], grad_first[...])
+    sum_in[0:width, :] = dot(node_turned_ref[...], grad_first.buffer[...])
+    sum_in[width : 2 * width, :] = dot_lt(gathered[...], grad_first.buffer[...])
 
     def back_body(start, i):
         here = pl.ds(start, BIG)
@@ -284,16 +287,12 @@
 
     loop(edges, back_body, BIG)
     first_ref = first_out.buffer
-    for out, index_ref in ((from_send, send_ref), (from_recv, recv_ref)):
-
-        def body(start, i):
-            count = out.shape[0]
-            out.buffer[pl.ds(start, count), :] = dot(
-                spread_rows(index_ref, start, count), first_ref[...]
-            ).astype(BF)
-            out.send(i)
-
-        loop(out.shape[0], body, out.shape[0])
+    from_send.buffer[...] = dot(
+        spread_rows(send_ref, 0, nodes + halo), first_ref[...]
+    ).astype(BF)
+    from_send.send(0)
+    from_recv.buffer[...] = dot(spread_recv[...], first_ref[...]).astype(BF)
+    from_recv.send(0)
     sent, received = from_send.buffer, from_recv.buffer
     back = dot_rt(sent[nodes : nodes + halo, :], w_send_ref[...])
     outward.buffer[...] = back.reshape(outward.shape).astype(BF)
@@ -331,19 +330,22 @@
     loop(cot.shape[0], edge_body)
 
 
-def node_grad_kernel(rows_ref, w_both, returned, acc, from_send, from_recv, out, token):
+def node_grad_kernel(
+    rows_ref, w_node, first, cot, w_both, from_send, from_recv, returned, out, token
+):
     token.buffer[...] = jnp.zeros(token.shape, F32)
     token.send(0)
-    nodes, width = acc.shape
+    nodes, width = first.shape
     halo = returned.shape[0] * returned.shape[1]
-    w_ref = w_both.ready()
+    w_node_ref, w_ref = w_node.ready(), w_both.ready()
     returned_ref = returned.ready()[...].astype(F32).reshape(halo, width).astype(BF)
 
     def body(start, i):
         here = pl.ds(start, ROWS)
         spread = one_hot(rows_ref[...] == iota((ROWS, halo), 0) + start)
         out.buffer[here, :] = (
-            acc.part(i)[here, :].astype(F32)
+            cot.part(i)[here, :].astype(F32)
+            + dot_rt(first.part(i)[here, :], w_node_ref[...])
             + dot(spread, returned_ref)
             + dot_rt(from_send.part(i)[here, :], w_ref[0:width, :])
             + dot_rt(from_recv.part(i)[here, :], w_ref[width : 2 * width, :])
@@ -552,7 +554,8 @@
         + [((edges, width), BF)] * 3
         + [((edges, LANE), F32)]
         + [((edges, width), BF)]
-        + [((nodes, width), BF)] * 5
+        + [((nodes, width), BF)] * 3
+        + [((nodes, edges), BF), ((nodes, width), BF)]
         + [
             ((8, width), F32),
             ((2 * width, width), F32),
@@ -654,14 +657,14 @@
         [senders, receivers],
         [((edges, LANE), jnp.int32)] * 2,
         flops=7 * edges * unit,
-        fetch=[node, edge, w_edge_in],
+        fetch=[node, w_edge_in, edge],
         store=[((width, nodes), BF, 1), ((width, edges), BF, 1), ((edges, width), F32, edges // BIG)],
         limit=FULL,
     )
     each = width // patches
     rows, half = 8 * each, width // 2
     piece = ((8, depth * rows, half), BF, 8)
-    node_acc, grad_first, from_send, from_recv, outward, send, keep = main_call(
+    node_first, grad_first, from_send, from_recv, outward, send, keep = main_call(
         patches,
         piece,
         place,
@@ -715,11 +718,13 @@
         [send_rows],
         flops=3 * nodes * unit,
         fetch=[
+            Part(w_node_in, 1, 0, width),
+            Part(node_first, nodes // ROWS),
+            Part(n_cot, nodes // ROWS),
             Part(w_edge_in, 1, width, 2 * width),
-            returned,
-            Part(node_acc, nodes // ROWS),
             Part(from_send, nodes // ROWS, 0, nodes),
             Part(from_recv, nodes // ROWS),
+            returned,
         ],
         store=[wide(nodes), TOKEN],
         limit=FULL,

time: 120 us -> 119 us (level)
    all_to_all x1, waiting for transfers between devices: 6.93 us -> 5.35 us  [along_depth(): return lax.all_to_all(x, 'patch', 0, 0, axis_index_groups=lines, tiled=True)]
  transfers between devices with their start and end apart: 16 -> 16, of which waited for: 9 -> 9; matrix products, arithmetic and copies ran while one was open for 0% -> 0% of each run, Pallas kernels for 17% -> 18%
where the time goes in v6:
time: 119 us; the launch traced here: 118 us
  Pallas kernels  48.6 us (41%)
  starting transfers between devices  44.4 us (37%)
  waiting for transfers between devices  18.6 us (16%)
  local copies, waits for them, and re-layouts  4.57 us (4%)
  between operations  1.42 us (1%)
    pallas_call x10, Pallas kernels, call(): pl.pallas_call(body, out_shape=shapes[0] if single else shapes, in_specs=...  48.6 us
    all_to_all x1, starting transfers between devices, local(): lax.all_to_all(outgoing, 'patch', split_axis=0, concat_axis=0, tiled=True)  12.1 us
    ppermute x6, starting transfers between devices, to_member(): lax.ppermute(x, 'group', [(g, (g + shift) % members) for g in range(membe...  9.72 us
    ppermute x6, starting transfers between devices, to_column(): lax.ppermute(x, 'patch', [(i, (i + shift * column) % patches) for i in ra...  8.87 us
    all_to_all x1, starting transfers between devices, local(): lax.all_to_all(outward, 'patch', split_axis=0, concat_axis=0, tiled=True)  7.82 us
    all_to_all x1, starting transfers between devices, along_depth(): return lax.all_to_all(x, 'patch', 0, 0, axis_index_groups=lines, tiled=True)  5.66 us
    all_to_all x1, waiting for transfers between devices, along_depth(): return lax.all_to_all(x, 'patch', 0, 0, axis_index_groups=lines, tiled=True)  5.35 us
    ppermute x6, waiting for transfers between devices, to_member(): lax.ppermute(x, 'group', [(g, (g + shift) % members) for g in range(membe...  5.34 us
  transfers between devices with their start and end apart: 16, of which 9 were waited for; matrix products, arithmetic and copies ran while one was open for 0% of the time, Pallas kernels for 18%

profile of v6, /device:TPU:8, one launch (start us, length us, event | category | flops | bytes accessed | tf_op | source)
XLA Modules:
  0.0 118.2 jit_solution(6500259824428749150)
XLA Ops:
  0.6 1.2 %copy-done.1 = bf16[1,1024,512]{2,1,0:T(8,128)(2,1)S(1)} copy-done((bf16[1,1024,512]{2,1,0:T(8,128)(2,1)S(1)}, bf16[1,1024,512]{2,1,0:T(8,128)(2,1)}, u32[]{:S(2)}) %copy-start.1) | copy-done | bytes 1048600
  2.5 1.2 %shard_map.197 = bf16[64,4,512]{2,1,0:T(4,128)(2,1)} custom-call(s32[1,256]{1,0:T(1,128)S(1)} %copy-done.4, bf16[1024,512]{1,0:T(8,128)(2,1)S(1)} %bitcast.17), custom_call_target="tpu_custom_call" | custom-call | flops 268435456 | bytes 1311744 | tf_op jit(solution)/shard_map/pallas_call | solution.py:504
  3.7 12.1 %all-to-all-start = ((bf16[64,4,512]{2,1,0:T(4,128)(2,1)}), bf16[64,4,512]{2,1,0:T(4,128)(2,1)S(1)}, u32[]{:S(2)}, u32[]{:S(2)}) async-start(bf16[64,4,512]{2,1,0:T(4,128)(2,1)} %shard_map.197), calls=%async_computation | async-start | bytes 524288 | tf_op jit(solution)/shard_map/all_to_all | solution.py:653
  17.1 7.9 %shard_map.198 = (bf16[512,1024]{1,0:T(8,128)(2,1)}, bf16[512,1024]{1,0:T(8,128)(2,1)}, f32[1024,512]{1,0:T(8,128)}) custom-call(s32[8,128]{1,0:T(8,128)} %refs_2_.1, s32[8,128]{1,0:T(8,128)} %refs_3_.3, bf16[1024,512]{1,0:T(8,128)(2,1)} %bitcast.15, bf16[1536,512]{1,0:T(8,128)(2,1)} %refs_4_.1, bf16[1024,512]{1,0:T(8,128)(2,1)} %bitcast.22), custom_call_target="tpu_custom_call" | custom-call | flops 3758096384 | bytes 4202496 | tf_op jit(solution)/shard_map/pallas_call | solution.py:504
  25.1 2.3 %all-to-all-done.refs_6_ = bf16[64,4,512]{2,1,0:T(4,128)(2,1)S(1)} async-done(((bf16[64,4,512]{2,1,0:T(4,128)(2,1)}), bf16[64,4,512]{2,1,0:T(4,128)(2,1)S(1)}, u32[]{:S(2)}, u32[]{:S(2)}) %all-to-all-start) | async-done | bytes 262176 | tf_op jit(solution)/shard_map/all_to_all | solution.py:653
  27.4 0.7 copy-done.6
  28.1 22.7 %shard_map.199 = (bf16[1024,512]{1,0:T(8,128)(2,1)}, bf16[1024,512]{1,0:T(8,128)(2,1)}, bf16[1280,512]{1,0:T(8,128)(2,1)}, bf16[1024,512]{1,0:T(8,128)(2,1)}, bf...) custom-call(s32[3]{0:T(128)} %pad_add_fusion.refs_0_, ...), custom_call_target="tpu_custom_call" | custom-call | flops 13958643712 | bytes 8925200 | tf_op jit(solution)/shard_map/pallas_call | solution.py:504
  51.1 4.1 %shard_map.200 = (bf16[1024,512]{1,0:T(8,128)(2,1)}, f32[8,128]{1,0:T(8,128)}) custom-call(s32[1]{0:T(128)S(6)} %copy.22.refs_1_.refs_0_, bf16[1536,512]{1,0:T(8,128)(2,1)} %refs_4_.1, bf16[1024,512]{1,0:T(8,128)(2,1)} %get-tuple-element.42.refs_2_, bf16[1024,512]{1,0:T(8,128)(2,1)} %bitcast.19), custom_call_target="tpu_custom_call" | custom-call | flops 536870912 | bytes 1052676 | tf_op jit(solution)/shard_map/pallas_call | solution.py:504
  55.4 0.7 copy-done.2
  56.1 2.4 %shard_map.202 = (bf16[512,256]{1,0:T(8,128)(2,1)S(1)}, bf16[512,256]{1,0:T(8,128)(2,1)S(1)}, bf16[512,256]{1,0:T(8,128)(2,1)S(1)}, bf16[512,256]{1,0:T(8,128)(2...) custom-call(bf16[8,512,256]{2,1,0:T(8,128)(2,1)S(1)} %copy-done, ...), custom_call_target="tpu_custom_call" | custom-call | bytes 6291456 | tf_op jit(solution)/shard_map/pallas_call | solution.py:504
  58.5 1.5 %collective-permute-start.4 = (bf16[512,256]{1,0:T(8,128)(2,1)S(1)}, bf16[512,256]{1,0:T(8,128)(2,1)S(1)}, u32[]{:S(2)}, u32[]{:S(2)}) collective-permute-start(bf16[512,256]{1,0:T(8,128)(2,1)S(1)} %get-tuple-element.57), channel_id=1, source_target_pairs={{0,64},{64,128},{128,192},{192,0},{1,65},{65,129},{129,193},{193,1... | collective-permute-start | bytes 786440 | tf_op jit(solution)/shard_map/ppermute | solution.py:628
  60.0 2.7 %collective-permute-start.5 = (bf16[512,256]{1,0:T(8,128)(2,1)}, bf16[512,256]{1,0:T(8,128)(2,1)S(1)}, u32[]{:S(2)}, u32[]{:S(2)}) collective-permute-start(bf16[512,256]{1,0:T(8,128)(2,1)} %get-tuple-element.58), channel_id=1, source_target_pairs={{0,128},{64,192},{128,0},{192,64},{1,129},{65,193},{129,1},{193,65... | collective-permute-start | bytes 786440 | tf_op jit(solution)/shard_map/ppermute | solution.py:628
  62.8 1.4 %collective-permute-start.6 = (bf16[512,256]{1,0:T(8,128)(2,1)S(1)}, bf16[512,256]{1,0:T(8,128)(2,1)S(1)}, u32[]{:S(2)}, u32[]{:S(2)}) collective-permute-start(bf16[512,256]{1,0:T(8,128)(2,1)S(1)} %get-tuple-element.59), channel_id=1, source_target_pairs={{0,192},{64,0},{128,64},{192,128},{1,193},{65,1},{129,65},{193,129... | collective-permute-start | bytes 786440 | tf_op jit(solution)/shard_map/ppermute | solution.py:628
  64.2 1.6 %collective-permute-start.1 = (bf16[512,256]{1,0:T(8,128)(2,1)S(1)}, bf16[512,256]{1,0:T(8,128)(2,1)S(1)}, u32[]{:S(2)}, u32[]{:S(2)}) collective-permute-start(bf16[512,256]{1,0:T(8,128)(2,1)S(1)} %get-tuple-element.53), channel_id=1, source_target_pairs={{0,16},{1,17},{2,18},{3,19},{4,20},{5,21},{6,22},{7,23},{8,24},{9,... | collective-permute-start | bytes 786440 | tf_op jit(solution)/shard_map/ppermute | solution.py:631
  65.8 1.4 %collective-permute-start.2 = (bf16[512,256]{1,0:T(8,128)(2,1)S(1)}, bf16[512,256]{1,0:T(8,128)(2,1)S(1)}, u32[]{:S(2)}, u32[]{:S(2)}) collective-permute-start(bf16[512,256]{1,0:T(8,128)(2,1)S(1)} %get-tuple-element.54), channel_id=1, source_target_pairs={{0,32},{1,33},{2,34},{3,35},{4,36},{5,37},{6,38},{7,39},{8,40},{9,... | collective-permute-start | bytes 786440 | tf_op jit(solution)/shard_map/ppermute | solution.py:631
  67.2 1.0 collective-permute-done.4.refs_1_
  68.2 0.9 collective-permute-start.3
  69.1 7.8 %all-to-all-start.1 = ((bf16[64,4,512]{2,1,0:T(4,128)(2,1)}), bf16[64,4,512]{2,1,0:T(4,128)(2,1)}, u32[]{:S(2)}, u32[]{:S(2)}) async-start(bf16[64,4,512]{2,1,0:T(4,128)(2,1)} %get-tuple-element.47), calls=%async_computation.1 | async-start | bytes 524288 | tf_op jit(solution)/shard_map/all_to_all | solution.py:707
  77.1 1.6 %collective-permute-start.7 = (bf16[128,256]{1,0:T(8,128)(2,1)S(1)}, bf16[128,256]{1,0:T(8,128)(2,1)S(1)}, u32[]{:S(2)}, u32[]{:S(2)}) collective-permute-start(bf16[128,256]{1,0:T(8,128)(2,1)S(1)} %get-tuple-element.61), channel_id=1, source_target_pairs={{0,16},{1,17},{2,18},{3,19},{4,20},{5,21},{6,22},{7,23},{8,24},{9,... | collective-permute-start | bytes 196616 | tf_op jit(solution)/shard_map/ppermute | solution.py:631
  78.7 1.2 %collective-permute-start.8 = (bf16[128,256]{1,0:T(8,128)(2,1)S(1)}, bf16[128,256]{1,0:T(8,128)(2,1)S(1)}, u32[]{:S(2)}, u32[]{:S(2)}) collective-permute-start(bf16[128,256]{1,0:T(8,128)(2,1)S(1)} %get-tuple-element.62), channel_id=1, source_target_pairs={{0,32},{1,33},{2,34},{3,35},{4,36},{5,37},{6,38},{7,39},{8,40},{9,... | collective-permute-start | bytes 196616 | tf_op jit(solution)/shard_map/ppermute | solution.py:631
  80.0 2.1 %collective-permute-start.9 = (bf16[128,256]{1,0:T(8,128)(2,1)S(1)}, bf16[128,256]{1,0:T(8,128)(2,1)S(1)}, u32[]{:S(2)}, u32[]{:S(2)}) collective-permute-start(bf16[128,256]{1,0:T(8,128)(2,1)S(1)} %get-tuple-element.63), channel_id=1, source_target_pairs={{0,48},{1,49},{2,50},{3,51},{4,52},{5,53},{6,54},{7,55},{8,56},{9,... | collective-permute-start | bytes 196616 | tf_op jit(solution)/shard_map/ppermute | solution.py:631
  82.1 4.4 %collective-permute-done.8.refs_6_ = bf16[128,256]{1,0:T(8,128)(2,1)S(1)} collective-permute-done((bf16[128,256]{1,0:T(8,128)(2,1)S(1)}, bf16[128,256]{1,0:T(8,128)(2,1)S(1)}, u32[]{:S(2)}, u32[]{:S(2)}) %collective-permute-start.8) | collective-permute-done | bytes 65568 | tf_op jit(solution)/shard_map/ppermute | solution.py:631
  86.7 0.9 shard_map.204
  87.6 0.8 all-to-all-done.1.refs_7_
  88.4 5.7 %all-to-all-start.2 = ((bf16[8,80,256]{2,1,0:T(8,128)(2,1)}), bf16[8,80,256]{2,1,0:T(8,128)(2,1)S(1)}, u32[]{:S(2)}, u32[]{:S(2)}) async-start(bf16[8,80,256]{2,1,0:T(8,128)(2,1)} %shard_map.204), calls=%async_computation.2 | async-start | bytes 655360 | tf_op jit(solution)/shard_map/all_to_all | solution.py:634
  94.0 7.9 %shard_map.201 = (bf16[1024,512]{1,0:T(8,128)(2,1)}, f32[8,128]{1,0:T(8,128)}) custom-call(s32[1,256]{1,0:T(1,128)} %refs_0_.6, bf16[1024,512]{1,0:T(8,128)(2,1)} %refs_1_.6, bf16[1024,512]{1,0:T(8,128)(2,1)} %get-tuple-element.44.refs_2_, bf16[1024,512]{1,0:T(8,128)(2,1)} %bitcast.21, bf16[1536,512]{1,0:T(8,128)(2,1)} %refs_4_.1, ...), custom_call_target="tpu_custom_call" | custom-call | flops 1610612736 | bytes 1053696 | tf_op jit(solution)/shard_map/pallas_call | solution.py:504
  102.0 5.4 %all-to-all-done.2.refs_0_ = bf16[8,80,256]{2,1,0:T(8,128)(2,1)S(1)} async-done(((bf16[8,80,256]{2,1,0:T(8,128)(2,1)}), bf16[8,80,256]{2,1,0:T(8,128)(2,1)S(1)}, u32[]{:S(2)}, u32[]{:S(2)}) %all-to-all-start.2) | async-done | bytes 327712 | tf_op jit(solution)/shard_map/all_to_all | solution.py:634
  108.0 2.3 %collective-permute-start.12 = (bf16[80,256]{1,0:T(8,128)(2,1)S(1)}, bf16[80,256]{1,0:T(8,128)(2,1)S(1)}, u32[]{:S(2)}, u32[]{:S(2)}) collective-permute-start(bf16[80,256]{1,0:T(8,128)(2,1)S(1)} %shard_map.205.refs_1_), channel_id=1, source_target_pairs={{0,192},{64,0},{128,64},{192,128},{1,193},{65,1},{129,65},{193,129... | collective-permute-start | bytes 122888 | tf_op jit(solution)/shard_map/ppermute | solution.py:628
  110.4 0.8 collective-permute-start.11
  111.2 0.9 collective-permute-start.10
  112.1 3.8 %collective-permute-done.11.refs_3_ = bf16[80,256]{1,0:T(8,128)(2,1)S(1)} collective-permute-done((bf16[80,256]{1,0:T(8,128)(2,1)S(1)}, bf16[80,256]{1,0:T(8,128)(2,1)S(1)}, u32[]{:S(2)}, u32[]{:S(2)}) %collective-permute-start.11) | collective-permute-done | bytes 40992 | tf_op jit(solution)/shard_map/ppermute | solution.py:628
  116.4 1.2 %shard_map.206 = (f32[24,512]{1,0:T(8,128)}, f32[8,512]{1,0:T(8,128)}, f32[16,512]{1,0:T(8,128)}, f32[8,512]{1,0:T(8,128)}, f32[8,512]{1,0:T(8,128)S(1)}) custom-call(s32[3]{0:T(128)S(1)} %copy-done.5, bf16[80,256]{1,0:T(8,128)(2,1)S(1)} %shard_map.205.refs_1_, bf16[80,256]{1,0:T(8,128)(2,1)S(1)} %collective-permute-done.10.refs_2_, ...), custom_call_target="tpu_custom_call" | custom-call | bytes 294924 | tf_op jit(solution)/shard_map/pallas_call | solution.py:504
  (27 shorter events, 3.9 us)
Async XLA Ops:
  0.6 1.2 %copy-start.1 = (bf16[1,1024,512]{2,1,0:T(8,128)(2,1)S(1)}, bf16[1,1024,512]{2,1,0:T(8,128)(2,1)}, u32[]{:S(2)}) copy-start(bf16[1,1024,512]{2,1,0:T(8,128)(2,1)} %param.14) | copy-start | bytes 3145732
  1.9 0.7 copy-start.4
  3.7 23.7 %all-to-all-start = ((bf16[64,4,512]{2,1,0:T(4,128)(2,1)}), bf16[64,4,512]{2,1,0:T(4,128)(2,1)S(1)}, u32[]{:S(2)}, u32[]{:S(2)}) async-start(bf16[64,4,512]{2,1,0:T(4,128)(2,1)} %shard_map.197), calls=%async_computation | async-start | bytes 524288 | tf_op jit(solution)/shard_map/all_to_all | solution.py:653
  27.4 0.7 copy-start.6
  50.8 4.6 %copy-start = (bf16[8,512,256]{2,1,0:T(8,128)(2,1)S(1)}, bf16[8,512,256]{2,1,0:T(8,128)(2,1)}, u32[]{:S(2)}) copy-start(bf16[8,512,256]{2,1,0:T(8,128)(2,1)} %get-tuple-element.49.refs_0_) | copy-start | bytes 6291460
  50.8 4.6 %collective-permute-start = (bf16[8,512,256]{2,1,0:T(8,128)(2,1)}, bf16[8,512,256]{2,1,0:T(8,128)(2,1)}, u32[]{:S(2)}, u32[]{:S(2)}) collective-permute-start(bf16[8,512,256]{2,1,0:T(8,128)(2,1)} %get-tuple-element.50), channel_id=1, source_target_pairs={{0,1},{1,0},{2,3},{3,2},{4,5},{5,4},{6,7},{7,6},{8,9},{9,8},{10,11... | collective-permute-start | bytes 6291464 | tf_op jit(solution)/shard_map/ppermute | solution.py:688
  55.4 0.7 copy-start.2
  58.5 9.6 %collective-permute-start.4 = (bf16[512,256]{1,0:T(8,128)(2,1)S(1)}, bf16[512,256]{1,0:T(8,128)(2,1)S(1)}, u32[]{:S(2)}, u32[]{:S(2)}) collective-permute-start(bf16[512,256]{1,0:T(8,128)(2,1)S(1)} %get-tuple-element.57), channel_id=1, source_target_pairs={{0,64},{64,128},{128,192},{192,0},{1,65},{65,129},{129,193},{193,1... | collective-permute-start | bytes 786440 | tf_op jit(solution)/shard_map/ppermute | solution.py:628
  60.0 16.9 %collective-permute-start.5 = (bf16[512,256]{1,0:T(8,128)(2,1)}, bf16[512,256]{1,0:T(8,128)(2,1)S(1)}, u32[]{:S(2)}, u32[]{:S(2)}) collective-permute-start(bf16[512,256]{1,0:T(8,128)(2,1)} %get-tuple-element.58), channel_id=1, source_target_pairs={{0,128},{64,192},{128,0},{192,64},{1,129},{65,193},{129,1},{193,65... | collective-permute-start | bytes 786440 | tf_op jit(solution)/shard_map/ppermute | solution.py:628
  62.8 14.2 %collective-permute-start.6 = (bf16[512,256]{1,0:T(8,128)(2,1)S(1)}, bf16[512,256]{1,0:T(8,128)(2,1)S(1)}, u32[]{:S(2)}, u32[]{:S(2)}) collective-permute-start(bf16[512,256]{1,0:T(8,128)(2,1)S(1)} %get-tuple-element.59), channel_id=1, source_target_pairs={{0,192},{64,0},{128,64},{192,128},{1,193},{65,1},{129,65},{193,129... | collective-permute-start | bytes 786440 | tf_op jit(solution)/shard_map/ppermute | solution.py:628
  64.2 15.8 %collective-permute-start.1 = (bf16[512,256]{1,0:T(8,128)(2,1)S(1)}, bf16[512,256]{1,0:T(8,128)(2,1)S(1)}, u32[]{:S(2)}, u32[]{:S(2)}) collective-permute-start(bf16[512,256]{1,0:T(8,128)(2,1)S(1)} %get-tuple-element.53), channel_id=1, source_target_pairs={{0,16},{1,17},{2,18},{3,19},{4,20},{5,21},{6,22},{7,23},{8,24},{9,... | collective-permute-start | bytes 786440 | tf_op jit(solution)/shard_map/ppermute | solution.py:631
  65.8 16.3 %collective-permute-start.2 = (bf16[512,256]{1,0:T(8,128)(2,1)S(1)}, bf16[512,256]{1,0:T(8,128)(2,1)S(1)}, u32[]{:S(2)}, u32[]{:S(2)}) collective-permute-start(bf16[512,256]{1,0:T(8,128)(2,1)S(1)} %get-tuple-element.54), channel_id=1, source_target_pairs={{0,32},{1,33},{2,34},{3,35},{4,36},{5,37},{6,38},{7,39},{8,40},{9,... | collective-permute-start | bytes 786440 | tf_op jit(solution)/shard_map/ppermute | solution.py:631
  68.2 13.9 %collective-permute-start.3 = (bf16[512,256]{1,0:T(8,128)(2,1)S(1)}, bf16[512,256]{1,0:T(8,128)(2,1)S(1)}, u32[]{:S(2)}, u32[]{:S(2)}) collective-permute-start(bf16[512,256]{1,0:T(8,128)(2,1)S(1)} %get-tuple-element.55), channel_id=1, source_target_pairs={{0,48},{1,49},{2,50},{3,51},{4,52},{5,53},{6,54},{7,55},{8,56},{9,... | collective-permute-start | bytes 786440 | tf_op jit(solution)/shard_map/ppermute | solution.py:631
  69.1 19.3 %all-to-all-start.1 = ((bf16[64,4,512]{2,1,0:T(4,128)(2,1)}), bf16[64,4,512]{2,1,0:T(4,128)(2,1)}, u32[]{:S(2)}, u32[]{:S(2)}) async-start(bf16[64,4,512]{2,1,0:T(4,128)(2,1)} %get-tuple-element.47), calls=%async_computation.1 | async-start | bytes 524288 | tf_op jit(solution)/shard_map/all_to_all | solution.py:707
  77.1 5.0 %collective-permute-start.7 = (bf16[128,256]{1,0:T(8,128)(2,1)S(1)}, bf16[128,256]{1,0:T(8,128)(2,1)S(1)}, u32[]{:S(2)}, u32[]{:S(2)}) collective-permute-start(bf16[128,256]{1,0:T(8,128)(2,1)S(1)} %get-tuple-element.61), channel_id=1, source_target_pairs={{0,16},{1,17},{2,18},{3,19},{4,20},{5,21},{6,22},{7,23},{8,24},{9,... | collective-permute-start | bytes 196616 | tf_op jit(solution)/shard_map/ppermute | solution.py:631
  78.7 7.8 %collective-permute-start.8 = (bf16[128,256]{1,0:T(8,128)(2,1)S(1)}, bf16[128,256]{1,0:T(8,128)(2,1)S(1)}, u32[]{:S(2)}, u32[]{:S(2)}) collective-permute-start(bf16[128,256]{1,0:T(8,128)(2,1)S(1)} %get-tuple-element.62), channel_id=1, source_target_pairs={{0,32},{1,33},{2,34},{3,35},{4,36},{5,37},{6,38},{7,39},{8,40},{9,... | collective-permute-start | bytes 196616 | tf_op jit(solution)/shard_map/ppermute | solution.py:631
  80.0 6.7 %collective-permute-start.9 = (bf16[128,256]{1,0:T(8,128)(2,1)S(1)}, bf16[128,256]{1,0:T(8,128)(2,1)S(1)}, u32[]{:S(2)}, u32[]{:S(2)}) collective-permute-start(bf16[128,256]{1,0:T(8,128)(2,1)S(1)} %get-tuple-element.63), channel_id=1, source_target_pairs={{0,48},{1,49},{2,50},{3,51},{4,52},{5,53},{6,54},{7,55},{8,56},{9,... | collective-permute-start | bytes 196616 | tf_op jit(solution)/shard_map/ppermute | solution.py:631
  88.4 18.9 %all-to-all-start.2 = ((bf16[8,80,256]{2,1,0:T(8,128)(2,1)}), bf16[8,80,256]{2,1,0:T(8,128)(2,1)S(1)}, u32[]{:S(2)}, u32[]{:S(2)}) async-start(bf16[8,80,256]{2,1,0:T(8,128)(2,1)} %shard_map.204), calls=%async_computation.2 | async-start | bytes 655360 | tf_op jit(solution)/shard_map/all_to_all | solution.py:634
  94.0 22.4 %copy-start.5 = (s32[3]{0:T(128)S(1)}, s32[3]{0:T(128)}, u32[]{:S(2)}) copy-start(s32[3]{0:T(128)} %pad_add_fusion.refs_0_) | copy-start | bytes 40
  107.3 0.7 copy-start.3
  108.0 4.1 %collective-permute-start.12 = (bf16[80,256]{1,0:T(8,128)(2,1)S(1)}, bf16[80,256]{1,0:T(8,128)(2,1)S(1)}, u32[]{:S(2)}, u32[]{:S(2)}) collective-permute-start(bf16[80,256]{1,0:T(8,128)(2,1)S(1)} %shard_map.205.refs_1_), channel_id=1, source_target_pairs={{0,192},{64,0},{128,64},{192,128},{1,193},{65,1},{129,65},{193,129... | collective-permute-start | bytes 122888 | tf_op jit(solution)/shard_map/ppermute | solution.py:628
  110.4 5.5 %collective-permute-start.11 = (bf16[80,256]{1,0:T(8,128)(2,1)S(1)}, bf16[80,256]{1,0:T(8,128)(2,1)S(1)}, u32[]{:S(2)}, u32[]{:S(2)}) collective-permute-start(bf16[80,256]{1,0:T(8,128)(2,1)S(1)} %shard_map.205.refs_1_), channel_id=1, source_target_pairs={{0,128},{64,192},{128,0},{192,64},{1,129},{65,193},{129,1},{193,65... | collective-permute-start | bytes 122888 | tf_op jit(solution)/shard_map/ppermute | solution.py:628
  111.2 5.2 %collective-permute-start.10 = (bf16[80,256]{1,0:T(8,128)(2,1)S(1)}, bf16[80,256]{1,0:T(8,128)(2,1)S(1)}, u32[]{:S(2)}, u32[]{:S(2)}) collective-permute-start(bf16[80,256]{1,0:T(8,128)(2,1)S(1)} %shard_map.205.refs_1_), channel_id=1, source_target_pairs={{0,64},{64,128},{128,192},{192,0},{1,65},{65,129},{129,193},{193,1... | collective-permute-start | bytes 122888 | tf_op jit(solution)/shard_map/ppermute | solution.py:628

commit v7 on v6

--- a/solution.py
+++ b/solution.py
@@ -314,9 +314,7 @@
     deal(place_ref, patches // 8, pieces, piece_send, piece_keep)
 
 
-def edge_grad_kernel(count_ref, w_own, first, cot, edge_grad, token):
-    token.buffer[...] = jnp.zeros(token.shape, F32)
-    token.send(0)
+def edge_grad_kernel(count_ref, w_own, first, cot, edge_grad):
     w_ref = w_own.ready()
 
     def edge_body(start, i):
@@ -458,10 +456,12 @@
         self.rows = array.shape[0] if rows is None else rows
 
 
-def call(kernel, outs, ins, scratch=(), scalars=0, flops=0, fetch=(), store=(), limit=None, after=()):
+def call(kernel, outs, ins, scratch=(), scalars=0, flops=0, fetch=(), store=(), limit=None, after=(), through=None):
     ins = list(ins)
+    passed = [] if through is None else [through]
     fetch = [f if isinstance(f, Part) else Part(f) for f in fetch]
     shapes = [jax.ShapeDtypeStruct(s, d) for s, d in list(outs) + [o[:2] for o in store]]
+    shapes += [jax.ShapeDtypeStruct(p.shape, p.dtype) for p in passed]
     single = len(shapes) == 1
     buffers = [((f.rows, *f.array.shape[1:]), f.array.dtype) for f in fetch]
     size = sum(int(a.size) * a.dtype.itemsize for a in ins + shapes)
@@ -478,8 +478,10 @@
         args, refs = take(refs, len(ins))
         _, refs = take(refs, len(after))
         sources, refs = take(refs, many)
+        _, refs = take(refs, len(passed))
         results, refs = take(refs, given)
         targets, refs = take(refs, kept)
+        _, refs = take(refs, len(passed))
         own, refs = take(refs, len(scratch))
         slots, refs = take(refs, many)
         rooms, refs = take(refs, kept)
@@ -500,14 +502,14 @@
             one.ready()
 
     far = pl.BlockSpec(memory_space=pltpu.HBM)
-    out_specs = [VM] * given + [far] * kept
+    out_specs = [VM] * given + [far] * (kept + len(passed))
     return pl.pallas_call(
         body,
         out_shape=shapes[0] if single else shapes,
         in_specs=[SM] * scalars
         + [VM] * (len(ins) - scalars)
         + [pl.BlockSpec(memory_space=pl.ANY)] * len(after)
-        + [far] * many,
+        + [far] * (many + len(passed)),
         out_specs=out_specs[0] if single else out_specs,
         scratch_shapes=[pltpu.VMEM(s, d) for s, d in held]
         + [pltpu.SemaphoreType.DMA((f.parts,)) for f in fetch]
@@ -516,7 +518,8 @@
             vmem_limit_bytes=bytes_here + 4 * 2**20 if limit is None else limit
         ),
         cost_estimate=pl.CostEstimate(flops=flops, bytes_accessed=size, transcendentals=0),
-    )(*ins, *after, *[f.array for f in fetch])
+        input_output_aliases={len(ins) + len(after) + many: given + kept} if passed else {},
+    )(*ins, *after, *[f.array for f in fetch], *passed)
 
 
 def main_call(
@@ -686,17 +689,18 @@
         w_node_out,
     )
     got = lax.ppermute(send, "patch", twins)
-    edge_grad, edge_token = call(
+    edge_grad, keep = call(
         edge_grad_kernel,
         [],
         [tile_count],
         scalars=1,
         flops=nodes * unit,
         fetch=[Part(w_edge_in, 1, 0, width), Part(grad_first, parts), Part(e_cot, parts)],
-        store=[wide(edges), TOKEN],
+        store=[wide(edges)],
         limit=FULL,
-    )
-    sums = call(pair_kernel, [(keep.shape[1:], BF)] * 8, [keep, got], after=[edge_token])
+        through=keep,
+    )
+    sums = call(pair_kernel, [(keep.shape[1:], BF)] * 8, [keep, got])
     columns = [sums[0]] + [to_column(sums[s], s) for s in range(1, 4)]
     rights = call(
         right_kernel,

time: 119 us -> 118 us (level)
  Pallas kernels: 48.6 us -> 47.1 us
    pallas_call x10, Pallas kernels: 48.6 us -> 47.1 us  [call(): pl.pallas_call(body, out_shape=shapes[0] if single else shapes, in_specs=...]
    unnamed x14 -> x12, local copies, waits for them, and re-layouts: 3.97 us -> 4.88 us
where the time goes in v7:
time: 118 us
  Pallas kernels  47.1 us (40%)
  starting transfers between devices  44.5 us (38%)
  waiting for transfers between devices  18.6 us (16%)
  local copies, waits for them, and re-layouts  5.47 us (5%)
  between operations  1.41 us (1%)
    pallas_call x10, Pallas kernels, call(): pl.pallas_call(body, out_shape=shapes[0] if single else shapes, in_specs=...  47.1 us
    all_to_all x1, starting transfers between devices, local(): lax.all_to_all(outgoing, 'patch', split_axis=0, concat_axis=0, tiled=True)  12.1 us
    ppermute x6, starting transfers between devices, to_member(): lax.ppermute(x, 'group', [(g, (g + shift) % members) for g in range(membe...  9.77 us
    ppermute x6, starting transfers between devices, to_column(): lax.ppermute(x, 'patch', [(i, (i + shift * column) % patches) for i in ra...  8.95 us
    all_to_all x1, starting transfers between devices, local(): lax.all_to_all(outward, 'patch', split_axis=0, concat_axis=0, tiled=True)  7.76 us
    all_to_all x1, starting transfers between devices, along_depth(): return lax.all_to_all(x, 'patch', 0, 0, axis_index_groups=lines, tiled=True)  5.66 us
    all_to_all x1, waiting for transfers between devices, along_depth(): return lax.all_to_all(x, 'patch', 0, 0, axis_index_groups=lines, tiled=True)  5.35 us
    ppermute x6, waiting for transfers between devices, to_member(): lax.ppermute(x, 'group', [(g, (g + shift) % members) for g in range(membe...  5.27 us
  transfers between devices with their start and end apart: 16, of which 9 were waited for; matrix products, arithmetic and copies ran while one was open for 0% of the time, Pallas kernels for 18%

profile of v7, /device:TPU:8, one launch (start us, length us, event | category | flops | bytes accessed | tf_op | source)
XLA Modules:
  0.0 117.7 jit_solution(2689432248467345713)
XLA Ops:
  0.6 1.2 %copy-done.1 = bf16[1,1024,512]{2,1,0:T(8,128)(2,1)S(1)} copy-done((bf16[1,1024,512]{2,1,0:T(8,128)(2,1)S(1)}, bf16[1,1024,512]{2,1,0:T(8,128)(2,1)}, u32[]{:S(2)}) %copy-start.1) | copy-done | bytes 1048600
  2.5 1.2 %shard_map.197 = bf16[64,4,512]{2,1,0:T(4,128)(2,1)} custom-call(s32[1,256]{1,0:T(1,128)S(1)} %copy-done.3, bf16[1024,512]{1,0:T(8,128)(2,1)S(1)} %bitcast.17), custom_call_target="tpu_custom_call" | custom-call | flops 268435456 | bytes 1311744 | tf_op jit(solution)/shard_map/pallas_call | solution.py:506
  3.7 12.1 %all-to-all-start = ((bf16[64,4,512]{2,1,0:T(4,128)(2,1)}), bf16[64,4,512]{2,1,0:T(4,128)(2,1)S(1)}, u32[]{:S(2)}, u32[]{:S(2)}) async-start(bf16[64,4,512]{2,1,0:T(4,128)(2,1)} %shard_map.197), calls=%async_computation | async-start | bytes 524288 | tf_op jit(solution)/shard_map/all_to_all | solution.py:656
  17.1 7.9 %shard_map.198 = (bf16[512,1024]{1,0:T(8,128)(2,1)}, bf16[512,1024]{1,0:T(8,128)(2,1)}, f32[1024,512]{1,0:T(8,128)}) custom-call(s32[8,128]{1,0:T(8,128)} %refs_2_.1, s32[8,128]{1,0:T(8,128)} %refs_3_.3, bf16[1024,512]{1,0:T(8,128)(2,1)} %bitcast.15, bf16[1536,512]{1,0:T(8,128)(2,1)} %refs_4_.1, bf16[1024,512]{1,0:T(8,128)(2,1)} %bitcast.22), custom_call_target="tpu_custom_call" | custom-call | flops 3758096384 | bytes 4202496 | tf_op jit(solution)/shard_map/pallas_call | solution.py:506
  25.1 2.3 %all-to-all-done.refs_6_ = bf16[64,4,512]{2,1,0:T(4,128)(2,1)S(1)} async-done(((bf16[64,4,512]{2,1,0:T(4,128)(2,1)}), bf16[64,4,512]{2,1,0:T(4,128)(2,1)S(1)}, u32[]{:S(2)}, u32[]{:S(2)}) %all-to-all-start) | async-done | bytes 262176 | tf_op jit(solution)/shard_map/all_to_all | solution.py:656
  27.4 0.7 copy-done.5
  28.1 22.7 %shard_map.199 = (bf16[1024,512]{1,0:T(8,128)(2,1)}, bf16[1024,512]{1,0:T(8,128)(2,1)}, bf16[1280,512]{1,0:T(8,128)(2,1)}, bf16[1024,512]{1,0:T(8,128)(2,1)}, bf...) custom-call(s32[3]{0:T(128)} %pad_add_fusion.refs_0_, ...), custom_call_target="tpu_custom_call" | custom-call | flops 13958643712 | bytes 8925200 | tf_op jit(solution)/shard_map/pallas_call | solution.py:506
  51.1 4.0 %shard_map.200 = (bf16[1024,512]{1,0:T(8,128)(2,1)}, bf16[8,512,256]{2,1,0:T(8,128)(2,1)}) custom-call(s32[1]{0:T(128)S(6)} %copy.24.refs_1_.refs_0_, bf16[1536,512]{1,0:T(8,128)(2,1)} %refs_4_.1, bf16[1024,512]{1,0:T(8,128)(2,1)} %get-tuple-element.42.refs_2_, bf16[1024,512]{1,0:T(8,128)(2,1)} %bitcast.19, ...), custom_call_target="tpu_custom_call", output_to_operand_aliasing={{1}: (4, {})} | custom-call | flops 536870912 | bytes 3145732 | tf_op jit(solution)/shard_map/pallas_call | solution.py:506
  55.3 1.6 %copy-done = bf16[8,512,256]{2,1,0:T(8,128)(2,1)S(1)} copy-done((bf16[8,512,256]{2,1,0:T(8,128)(2,1)S(1)}, bf16[8,512,256]{2,1,0:T(8,128)(2,1)}, u32[]{:S(2)}) %copy-start) | copy-done | bytes 2097176
  56.9 1.1 shard_map.202
  58.0 1.5 %collective-permute-start.4 = (bf16[512,256]{1,0:T(8,128)(2,1)S(1)}, bf16[512,256]{1,0:T(8,128)(2,1)S(1)}, u32[]{:S(2)}, u32[]{:S(2)}) collective-permute-start(bf16[512,256]{1,0:T(8,128)(2,1)S(1)} %get-tuple-element.57), channel_id=1, source_target_pairs={{0,64},{64,128},{128,192},{192,0},{1,65},{65,129},{129,193},{193,1... | collective-permute-start | bytes 786440 | tf_op jit(solution)/shard_map/ppermute | solution.py:631
  59.5 2.7 %collective-permute-start.5 = (bf16[512,256]{1,0:T(8,128)(2,1)}, bf16[512,256]{1,0:T(8,128)(2,1)S(1)}, u32[]{:S(2)}, u32[]{:S(2)}) collective-permute-start(bf16[512,256]{1,0:T(8,128)(2,1)} %get-tuple-element.58), channel_id=1, source_target_pairs={{0,128},{64,192},{128,0},{192,64},{1,129},{65,193},{129,1},{193,65... | collective-permute-start | bytes 786440 | tf_op jit(solution)/shard_map/ppermute | solution.py:631
  62.2 1.4 %collective-permute-start.6 = (bf16[512,256]{1,0:T(8,128)(2,1)S(1)}, bf16[512,256]{1,0:T(8,128)(2,1)S(1)}, u32[]{:S(2)}, u32[]{:S(2)}) collective-permute-start(bf16[512,256]{1,0:T(8,128)(2,1)S(1)} %get-tuple-element.59), channel_id=1, source_target_pairs={{0,192},{64,0},{128,64},{192,128},{1,193},{65,1},{129,65},{193,129... | collective-permute-start | bytes 786440 | tf_op jit(solution)/shard_map/ppermute | solution.py:631
  63.6 1.6 %collective-permute-start.1 = (bf16[512,256]{1,0:T(8,128)(2,1)S(1)}, bf16[512,256]{1,0:T(8,128)(2,1)S(1)}, u32[]{:S(2)}, u32[]{:S(2)}) collective-permute-start(bf16[512,256]{1,0:T(8,128)(2,1)S(1)} %get-tuple-element.53), channel_id=1, source_target_pairs={{0,16},{1,17},{2,18},{3,19},{4,20},{5,21},{6,22},{7,23},{8,24},{9,... | collective-permute-start | bytes 786440 | tf_op jit(solution)/shard_map/ppermute | solution.py:634
  65.2 1.4 %collective-permute-start.2 = (bf16[512,256]{1,0:T(8,128)(2,1)S(1)}, bf16[512,256]{1,0:T(8,128)(2,1)S(1)}, u32[]{:S(2)}, u32[]{:S(2)}) collective-permute-start(bf16[512,256]{1,0:T(8,128)(2,1)S(1)} %get-tuple-element.54), channel_id=1, source_target_pairs={{0,32},{1,33},{2,34},{3,35},{4,36},{5,37},{6,38},{7,39},{8,40},{9,... | collective-permute-start | bytes 786440 | tf_op jit(solution)/shard_map/ppermute | solution.py:634
  66.6 1.0 collective-permute-done.4.refs_1_
  67.5 1.0 collective-permute-start.3
  68.6 7.8 %all-to-all-start.1 = ((bf16[64,4,512]{2,1,0:T(4,128)(2,1)}), bf16[64,4,512]{2,1,0:T(4,128)(2,1)}, u32[]{:S(2)}, u32[]{:S(2)}) async-start(bf16[64,4,512]{2,1,0:T(4,128)(2,1)} %get-tuple-element.48), calls=%async_computation.1 | async-start | bytes 524288 | tf_op jit(solution)/shard_map/all_to_all | solution.py:711
  76.5 1.6 %collective-permute-start.7 = (bf16[128,256]{1,0:T(8,128)(2,1)S(1)}, bf16[128,256]{1,0:T(8,128)(2,1)S(1)}, u32[]{:S(2)}, u32[]{:S(2)}) collective-permute-start(bf16[128,256]{1,0:T(8,128)(2,1)S(1)} %get-tuple-element.61), channel_id=1, source_target_pairs={{0,16},{1,17},{2,18},{3,19},{4,20},{5,21},{6,22},{7,23},{8,24},{9,... | collective-permute-start | bytes 196616 | tf_op jit(solution)/shard_map/ppermute | solution.py:634
  78.1 1.2 %collective-permute-start.8 = (bf16[128,256]{1,0:T(8,128)(2,1)S(1)}, bf16[128,256]{1,0:T(8,128)(2,1)S(1)}, u32[]{:S(2)}, u32[]{:S(2)}) collective-permute-start(bf16[128,256]{1,0:T(8,128)(2,1)S(1)} %get-tuple-element.62), channel_id=1, source_target_pairs={{0,32},{1,33},{2,34},{3,35},{4,36},{5,37},{6,38},{7,39},{8,40},{9,... | collective-permute-start | bytes 196616 | tf_op jit(solution)/shard_map/ppermute | solution.py:634
  79.4 2.1 %collective-permute-start.9 = (bf16[128,256]{1,0:T(8,128)(2,1)S(1)}, bf16[128,256]{1,0:T(8,128)(2,1)S(1)}, u32[]{:S(2)}, u32[]{:S(2)}) collective-permute-start(bf16[128,256]{1,0:T(8,128)(2,1)S(1)} %get-tuple-element.63), channel_id=1, source_target_pairs={{0,48},{1,49},{2,50},{3,51},{4,52},{5,53},{6,54},{7,55},{8,56},{9,... | collective-permute-start | bytes 196616 | tf_op jit(solution)/shard_map/ppermute | solution.py:634
  81.5 4.4 %collective-permute-done.8.refs_6_ = bf16[128,256]{1,0:T(8,128)(2,1)S(1)} collective-permute-done((bf16[128,256]{1,0:T(8,128)(2,1)S(1)}, bf16[128,256]{1,0:T(8,128)(2,1)S(1)}, u32[]{:S(2)}, u32[]{:S(2)}) %collective-permute-start.8) | collective-permute-done | bytes 65568 | tf_op jit(solution)/shard_map/ppermute | solution.py:634
  86.1 0.9 shard_map.204
  87.0 0.8 all-to-all-done.1.refs_7_
  87.8 5.7 %all-to-all-start.2 = ((bf16[8,80,256]{2,1,0:T(8,128)(2,1)}), bf16[8,80,256]{2,1,0:T(8,128)(2,1)S(1)}, u32[]{:S(2)}, u32[]{:S(2)}) async-start(bf16[8,80,256]{2,1,0:T(8,128)(2,1)} %shard_map.204), calls=%async_computation.2 | async-start | bytes 655360 | tf_op jit(solution)/shard_map/all_to_all | solution.py:637
  93.4 7.9 %shard_map.201 = (bf16[1024,512]{1,0:T(8,128)(2,1)}, f32[8,128]{1,0:T(8,128)}) custom-call(s32[1,256]{1,0:T(1,128)} %refs_0_.6, bf16[1024,512]{1,0:T(8,128)(2,1)} %refs_1_.6, bf16[1024,512]{1,0:T(8,128)(2,1)} %get-tuple-element.45.refs_2_, bf16[1024,512]{1,0:T(8,128)(2,1)} %bitcast.21, bf16[1536,512]{1,0:T(8,128)(2,1)} %refs_4_.1, ...), custom_call_target="tpu_custom_call" | custom-call | flops 1610612736 | bytes 1053696 | tf_op jit(solution)/shard_map/pallas_call | solution.py:506
  101.3 5.3 %all-to-all-done.2.refs_0_ = bf16[8,80,256]{2,1,0:T(8,128)(2,1)S(1)} async-done(((bf16[8,80,256]{2,1,0:T(8,128)(2,1)}), bf16[8,80,256]{2,1,0:T(8,128)(2,1)S(1)}, u32[]{:S(2)}, u32[]{:S(2)}) %all-to-all-start.2) | async-done | bytes 327712 | tf_op jit(solution)/shard_map/all_to_all | solution.py:637
  107.4 2.4 %collective-permute-start.12 = (bf16[80,256]{1,0:T(8,128)(2,1)S(1)}, bf16[80,256]{1,0:T(8,128)(2,1)S(1)}, u32[]{:S(2)}, u32[]{:S(2)}) collective-permute-start(bf16[80,256]{1,0:T(8,128)(2,1)S(1)} %shard_map.205.refs_1_), channel_id=1, source_target_pairs={{0,192},{64,0},{128,64},{192,128},{1,193},{65,1},{129,65},{193,129... | collective-permute-start | bytes 122888 | tf_op jit(solution)/shard_map/ppermute | solution.py:631
  109.8 0.8 collective-permute-start.11
  110.6 0.9 collective-permute-start.10
  111.5 3.8 %collective-permute-done.11.refs_3_ = bf16[80,256]{1,0:T(8,128)(2,1)S(1)} collective-permute-done((bf16[80,256]{1,0:T(8,128)(2,1)S(1)}, bf16[80,256]{1,0:T(8,128)(2,1)S(1)}, u32[]{:S(2)}, u32[]{:S(2)}) %collective-permute-start.11) | collective-permute-done | bytes 40992 | tf_op jit(solution)/shard_map/ppermute | solution.py:631
  115.9 1.2 %shard_map.206 = (f32[24,512]{1,0:T(8,128)}, f32[8,512]{1,0:T(8,128)}, f32[16,512]{1,0:T(8,128)}, f32[8,512]{1,0:T(8,128)}, f32[8,512]{1,0:T(8,128)S(1)}) custom-call(s32[3]{0:T(128)S(1)} %copy-done.4, bf16[80,256]{1,0:T(8,128)(2,1)S(1)} %shard_map.205.refs_1_, bf16[80,256]{1,0:T(8,128)(2,1)S(1)} %collective-permute-done.10.refs_2_, ...), custom_call_target="tpu_custom_call" | custom-call | bytes 294924 | tf_op jit(solution)/shard_map/pallas_call | solution.py:506
  (25 shorter events, 3.9 us)
Async XLA Ops:
  0.6 1.2 %copy-start.1 = (bf16[1,1024,512]{2,1,0:T(8,128)(2,1)S(1)}, bf16[1,1024,512]{2,1,0:T(8,128)(2,1)}, u32[]{:S(2)}) copy-start(bf16[1,1024,512]{2,1,0:T(8,128)(2,1)} %param.14) | copy-start | bytes 3145732
  1.9 0.7 copy-start.3
  3.7 23.7 %all-to-all-start = ((bf16[64,4,512]{2,1,0:T(4,128)(2,1)}), bf16[64,4,512]{2,1,0:T(4,128)(2,1)S(1)}, u32[]{:S(2)}, u32[]{:S(2)}) async-start(bf16[64,4,512]{2,1,0:T(4,128)(2,1)} %shard_map.197), calls=%async_computation | async-start | bytes 524288 | tf_op jit(solution)/shard_map/all_to_all | solution.py:656
  27.4 0.7 copy-start.5
  50.8 4.5 %collective-permute-start = (bf16[8,512,256]{2,1,0:T(8,128)(2,1)}, bf16[8,512,256]{2,1,0:T(8,128)(2,1)S(1)}, u32[]{:S(2)}, u32[]{:S(2)}) collective-permute-start(bf16[8,512,256]{2,1,0:T(8,128)(2,1)} %get-tuple-element.51), channel_id=1, source_target_pairs={{0,1},{1,0},{2,3},{3,2},{4,5},{5,4},{6,7},{7,6},{8,9},{9,8},{10,11... | collective-permute-start | bytes 6291464 | tf_op jit(solution)/shard_map/ppermute | solution.py:691
  55.3 1.6 %copy-start = (bf16[8,512,256]{2,1,0:T(8,128)(2,1)S(1)}, bf16[8,512,256]{2,1,0:T(8,128)(2,1)}, u32[]{:S(2)}) copy-start(bf16[8,512,256]{2,1,0:T(8,128)(2,1)} %get-tuple-element.50.refs_0_) | copy-start | bytes 6291460
  58.0 9.6 %collective-permute-start.4 = (bf16[512,256]{1,0:T(8,128)(2,1)S(1)}, bf16[512,256]{1,0:T(8,128)(2,1)S(1)}, u32[]{:S(2)}, u32[]{:S(2)}) collective-permute-start(bf16[512,256]{1,0:T(8,128)(2,1)S(1)} %get-tuple-element.57), channel_id=1, source_target_pairs={{0,64},{64,128},{128,192},{192,0},{1,65},{65,129},{129,193},{193,1... | collective-permute-start | bytes 786440 | tf_op jit(solution)/shard_map/ppermute | solution.py:631
  59.5 16.8 %collective-permute-start.5 = (bf16[512,256]{1,0:T(8,128)(2,1)}, bf16[512,256]{1,0:T(8,128)(2,1)S(1)}, u32[]{:S(2)}, u32[]{:S(2)}) collective-permute-start(bf16[512,256]{1,0:T(8,128)(2,1)} %get-tuple-element.58), channel_id=1, source_target_pairs={{0,128},{64,192},{128,0},{192,64},{1,129},{65,193},{129,1},{193,65... | collective-permute-start | bytes 786440 | tf_op jit(solution)/shard_map/ppermute | solution.py:631
  62.2 14.1 %collective-permute-start.6 = (bf16[512,256]{1,0:T(8,128)(2,1)S(1)}, bf16[512,256]{1,0:T(8,128)(2,1)S(1)}, u32[]{:S(2)}, u32[]{:S(2)}) collective-permute-start(bf16[512,256]{1,0:T(8,128)(2,1)S(1)} %get-tuple-element.59), channel_id=1, source_target_pairs={{0,192},{64,0},{128,64},{192,128},{1,193},{65,1},{129,65},{193,129... | collective-permute-start | bytes 786440 | tf_op jit(solution)/shard_map/ppermute | solution.py:631
  63.6 15.7 %collective-permute-start.1 = (bf16[512,256]{1,0:T(8,128)(2,1)S(1)}, bf16[512,256]{1,0:T(8,128)(2,1)S(1)}, u32[]{:S(2)}, u32[]{:S(2)}) collective-permute-start(bf16[512,256]{1,0:T(8,128)(2,1)S(1)} %get-tuple-element.53), channel_id=1, source_target_pairs={{0,16},{1,17},{2,18},{3,19},{4,20},{5,21},{6,22},{7,23},{8,24},{9,... | collective-permute-start | bytes 786440 | tf_op jit(solution)/shard_map/ppermute | solution.py:634
  65.2 16.3 %collective-permute-start.2 = (bf16[512,256]{1,0:T(8,128)(2,1)S(1)}, bf16[512,256]{1,0:T(8,128)(2,1)S(1)}, u32[]{:S(2)}, u32[]{:S(2)}) collective-permute-start(bf16[512,256]{1,0:T(8,128)(2,1)S(1)} %get-tuple-element.54), channel_id=1, source_target_pairs={{0,32},{1,33},{2,34},{3,35},{4,36},{5,37},{6,38},{7,39},{8,40},{9,... | collective-permute-start | bytes 786440 | tf_op jit(solution)/shard_map/ppermute | solution.py:634
  67.5 13.9 %collective-permute-start.3 = (bf16[512,256]{1,0:T(8,128)(2,1)S(1)}, bf16[512,256]{1,0:T(8,128)(2,1)S(1)}, u32[]{:S(2)}, u32[]{:S(2)}) collective-permute-start(bf16[512,256]{1,0:T(8,128)(2,1)S(1)} %get-tuple-element.55), channel_id=1, source_target_pairs={{0,48},{1,49},{2,50},{3,51},{4,52},{5,53},{6,54},{7,55},{8,56},{9,... | collective-permute-start | bytes 786440 | tf_op jit(solution)/shard_map/ppermute | solution.py:634
  68.6 19.2 %all-to-all-start.1 = ((bf16[64,4,512]{2,1,0:T(4,128)(2,1)}), bf16[64,4,512]{2,1,0:T(4,128)(2,1)}, u32[]{:S(2)}, u32[]{:S(2)}) async-start(bf16[64,4,512]{2,1,0:T(4,128)(2,1)} %get-tuple-element.48), calls=%async_computation.1 | async-start | bytes 524288 | tf_op jit(solution)/shard_map/all_to_all | solution.py:711
  76.5 5.0 %collective-permute-start.7 = (bf16[128,256]{1,0:T(8,128)(2,1)S(1)}, bf16[128,256]{1,0:T(8,128)(2,1)S(1)}, u32[]{:S(2)}, u32[]{:S(2)}) collective-permute-start(bf16[128,256]{1,0:T(8,128)(2,1)S(1)} %get-tuple-element.61), channel_id=1, source_target_pairs={{0,16},{1,17},{2,18},{3,19},{4,20},{5,21},{6,22},{7,23},{8,24},{9,... | collective-permute-start | bytes 196616 | tf_op jit(solution)/shard_map/ppermute | solution.py:634
  78.1 7.8 %collective-permute-start.8 = (bf16[128,256]{1,0:T(8,128)(2,1)S(1)}, bf16[128,256]{1,0:T(8,128)(2,1)S(1)}, u32[]{:S(2)}, u32[]{:S(2)}) collective-permute-start(bf16[128,256]{1,0:T(8,128)(2,1)S(1)} %get-tuple-element.62), channel_id=1, source_target_pairs={{0,32},{1,33},{2,34},{3,35},{4,36},{5,37},{6,38},{7,39},{8,40},{9,... | collective-permute-start | bytes 196616 | tf_op jit(solution)/shard_map/ppermute | solution.py:634
  79.4 6.7 %collective-permute-start.9 = (bf16[128,256]{1,0:T(8,128)(2,1)S(1)}, bf16[128,256]{1,0:T(8,128)(2,1)S(1)}, u32[]{:S(2)}, u32[]{:S(2)}) collective-permute-start(bf16[128,256]{1,0:T(8,128)(2,1)S(1)} %get-tuple-element.63), channel_id=1, source_target_pairs={{0,48},{1,49},{2,50},{3,51},{4,52},{5,53},{6,54},{7,55},{8,56},{9,... | collective-permute-start | bytes 196616 | tf_op jit(solution)/shard_map/ppermute | solution.py:634
  87.8 18.9 %all-to-all-start.2 = ((bf16[8,80,256]{2,1,0:T(8,128)(2,1)}), bf16[8,80,256]{2,1,0:T(8,128)(2,1)S(1)}, u32[]{:S(2)}, u32[]{:S(2)}) async-start(bf16[8,80,256]{2,1,0:T(8,128)(2,1)} %shard_map.204), calls=%async_computation.2 | async-start | bytes 655360 | tf_op jit(solution)/shard_map/all_to_all | solution.py:637
  93.4 22.4 %copy-start.4 = (s32[3]{0:T(128)S(1)}, s32[3]{0:T(128)}, u32[]{:S(2)}) copy-start(s32[3]{0:T(128)} %pad_add_fusion.refs_0_) | copy-start | bytes 40
  106.7 0.7 copy-start.2
  107.4 4.1 %collective-permute-start.12 = (bf16[80,256]{1,0:T(8,128)(2,1)S(1)}, bf16[80,256]{1,0:T(8,128)(2,1)S(1)}, u32[]{:S(2)}, u32[]{:S(2)}) collective-permute-start(bf16[80,256]{1,0:T(8,128)(2,1)S(1)} %shard_map.205.refs_1_), channel_id=1, source_target_pairs={{0,192},{64,0},{128,64},{192,128},{1,193},{65,1},{129,65},{193,129... | collective-permute-start | bytes 122888 | tf_op jit(solution)/shard_map/ppermute | solution.py:631
  109.8 5.5 %collective-permute-start.11 = (bf16[80,256]{1,0:T(8,128)(2,1)S(1)}, bf16[80,256]{1,0:T(8,128)(2,1)S(1)}, u32[]{:S(2)}, u32[]{:S(2)}) collective-permute-start(bf16[80,256]{1,0:T(8,128)(2,1)S(1)} %shard_map.205.refs_1_), channel_id=1, source_target_pairs={{0,128},{64,192},{128,0},{192,64},{1,129},{65,193},{129,1},{193,65... | collective-permute-start | bytes 122888 | tf_op jit(solution)/shard_map/ppermute | solution.py:631
  110.6 5.2 %collective-permute-start.10 = (bf16[80,256]{1,0:T(8,128)(2,1)S(1)}, bf16[80,256]{1,0:T(8,128)(2,1)S(1)}, u32[]{:S(2)}, u32[]{:S(2)}) collective-permute-start(bf16[80,256]{1,0:T(8,128)(2,1)S(1)} %shard_map.205.refs_1_), channel_id=1, source_target_pairs={{0,64},{64,128},{128,192},{192,0},{1,65},{65,129},{129,193},{193,1... | collective-permute-start | bytes 122888 | tf_op jit(solution)/shard_map/ppermute | solution.py:631
